TPU v7x, 128 devices: a whole 4x4x4 slice. The times are simulated.
128 devices in a mesh: seq: 4 (over z), fsdp: 32 (over x, y, core).
Axes of the slice: x: 4, y: 4, z: 4, core: 2. Of those that a mesh axis runs over, the one named last changes fastest.
Arguments:
- activations: bfloat16 [32, 512, 1536], P('fsdp', 'seq'), may hold values from -6 to 6
- cotangent: bfloat16 [32, 512, 1536], P('fsdp', 'seq'), may hold values from -6 to 6
- seq_lengths: int32 [32, 3], P('fsdp'), may hold values from 1 to 448, 512 in all within a row
- deal_order: int32 [32, 512], P('fsdp'), may hold values from 0 to 511, each once within a row
- routes: int32 [32, 512, 8], P('fsdp', 'seq'), may hold values from 0 to 39, all different within a row; in each aligned block of 128 rows (0 to 127, 128 to 255, ..., all dimensions but the last counted through in order) at most 29 rows name the same one
- entry_weight: float32 [1536, 2560], P(('seq', 'fsdp')), may hold values from -0.15625 to 0.15625
- entry_mean: float32 [1536, 2560], P(('seq', 'fsdp'))
- entry_square: float32 [1536, 2560], P(('seq', 'fsdp')), as said below
- exit_weight: float32 [1536, 1536], P(('seq', 'fsdp')), may hold values from -2.5 to 2.5
- exit_mean: float32 [1536, 1536], P(('seq', 'fsdp'))
- exit_square: float32 [1536, 1536], P(('seq', 'fsdp')), as said below
- router_weight: float32 [1536, 40], P(('seq', 'fsdp')), may hold values from -0.078125 to 0.078125
- router_mean: float32 [1536, 40], P(('seq', 'fsdp'))
- router_square: float32 [1536, 40], P(('seq', 'fsdp')), as said below
- expand_weight: float32 [40, 1536, 1024], P('seq', 'fsdp'), may hold values from -0.15625 to 0.15625
- expand_mean: float32 [40, 1536, 1024], P('seq', 'fsdp')
- expand_square: float32 [40, 1536, 1024], P('seq', 'fsdp'), as said below
- shrink_weight: float32 [40, 512, 1536], P('seq', 'fsdp'), may hold values from -1 to 1
- shrink_mean: float32 [40, 512, 1536], P('seq', 'fsdp')
- shrink_square: float32 [40, 512, 1536], P('seq', 'fsdp'), as said below
- norm_gains: float32 [2, 1536], P(None, ('seq', 'fsdp')), may hold values from 0.5 to 1.5
- gains_mean: float32 [2, 1536], P(None, ('seq', 'fsdp'))
- gains_square: float32 [2, 1536], P(None, ('seq', 'fsdp')), as said below
Outputs:
- block_output: bfloat16 [32, 512, 1536], P('fsdp', 'seq')
- input_grad: bfloat16 [32, 512, 1536], P('fsdp', 'seq')
- entry_drift: float32 [1536, 2560], P(('seq', 'fsdp'))
- entry_spread: float32 [1536, 2560], P(('seq', 'fsdp'))
- entry_master: float32 [1536, 2560], P(('seq', 'fsdp'))
- exit_drift: float32 [1536, 1536], P(('seq', 'fsdp'))
- exit_spread: float32 [1536, 1536], P(('seq', 'fsdp'))
- exit_master: float32 [1536, 1536], P(('seq', 'fsdp'))
- router_drift: float32 [1536, 40], P(('seq', 'fsdp'))
- router_spread: float32 [1536, 40], P(('seq', 'fsdp'))
- router_master: float32 [1536, 40], P(('seq', 'fsdp'))
- expand_drift: float32 [40, 1536, 1024], P('seq', 'fsdp')
- expand_spread: float32 [40, 1536, 1024], P('seq', 'fsdp')
- expand_master: float32 [40, 1536, 1024], P('seq', 'fsdp')
- shrink_drift: float32 [40, 512, 1536], P('seq', 'fsdp')
- shrink_spread: float32 [40, 512, 1536], P('seq', 'fsdp')
- shrink_master: float32 [40, 512, 1536], P('seq', 'fsdp')
- gains_drift: float32 [2, 1536], P(None, ('seq', 'fsdp'))
- gains_spread: float32 [2, 1536], P(None, ('seq', 'fsdp'))
- gains_master: float32 [2, 1536], P(None, ('seq', 'fsdp'))
Inputs may be any that keep to these rules, and one draw needn't show every extreme that they name: `seq_lengths`: each row sums to 512 and its longest entry is 448. `deal_order`: each row names every slot's token once. `routes`: each slot names 8 different experts; among the 128 slots of one device no expert is named more than 29 times. `entry_square`: positive. `exit_square`: positive. `router_square`: positive. `expand_square`: positive. `shrink_square`: positive. `gains_square`: positive.
All inputs are finite; a program needn't handle non-finite values.
Results may differ from a plain program's by a relative error of at most 0.025.
Values may be sent and summed in bfloat16 or wider, within the bound.
A program may use at most 320 MiB of HBM per device.

v0:
```python
import jax
import jax.numpy as jnp
from jax import lax
from jax.sharding import PartitionSpec as P

D = 1536
QH = 24
KVH = 8
HD = 64
FF = 512
EXPERTS = 40
TOP = 8
STEP = 10
CAP = 29


norm_eps = 1e-06
rope_base = 10000.0
beta_first = 0.9
beta_second = 0.95
adam_eps = 1e-08
weight_decay = 0.1


def norm_apply(vector, gain_vec):
    return (
        vector * lax.rsqrt(jnp.mean(vector * vector, axis=-1, keepdims=True) + norm_eps) * gain_vec
    )


def seq_layout(lengths_row, order_row):
    seq_ends = jnp.cumsum(lengths_row)
    starts = seq_ends - lengths_row
    seq_ids = jnp.sum((order_row[:, None] >= seq_ends[None, :]).astype(jnp.int32), axis=1)
    seq_match = seq_ids[:, None] == jnp.arange(lengths_row.shape[0], dtype=jnp.int32)[None, :]
    positions = order_row - jnp.sum(jnp.where(seq_match, starts[None, :], 0), axis=1)
    return (seq_ids, positions)


def angles(positions, width):
    half_width = width // 2
    frequency = rope_base ** (-jnp.arange(half_width, dtype=jnp.float32) * 2.0 / width)
    phase_angle = positions.astype(jnp.float32)[:, None] * frequency[None, :]
    return (jnp.cos(phase_angle)[:, None, :], jnp.sin(phase_angle)[:, None, :])


def rotate(vector, positions):
    half_width = vector.shape[-1] // 2
    cosine, sine_part = angles(positions, vector.shape[-1])
    first_half = vector[..., :half_width]
    second_half = vector[..., half_width:]
    return jnp.concatenate(
        [
            first_half * cosine - second_half * sine_part,
            second_half * cosine + first_half * sine_part,
        ],
        axis=-1,
    )


def rotate_back(gradient, positions):
    half_width = gradient.shape[-1] // 2
    cosine, sine_part = angles(positions, gradient.shape[-1])
    first_half = gradient[..., :half_width]
    second_half = gradient[..., half_width:]
    return jnp.concatenate(
        [
            first_half * cosine + second_half * sine_part,
            second_half * cosine - first_half * sine_part,
        ],
        axis=-1,
    )


def block_scores(query_rows, key_heads, row_seq, row_pos, seq_ids, positions):
    scores = jnp.einsum(
        "qhgd,khd->hgqk", query_rows, key_heads, preferred_element_type=jnp.float32
    ) * HD ** (-0.5)
    allowed = (row_seq[:, None] == seq_ids[None, :]) & (positions[None, :] <= row_pos[:, None])
    return jnp.where(allowed[None, None], scores, -1e30)


def attend_forward(query_heads, pair_heads, seq_ids, positions):
    group_tok, local_kv = (query_heads.shape[0], query_heads.shape[1])
    per_kv = QH // KVH
    block_rows = min(512, group_tok)
    key_heads = pair_heads[:, :, :HD]
    values = pair_heads[:, :, HD:]

    def one_block(block_start):
        query_rows = query_heads.reshape(block_rows, local_kv, per_kv, HD)
        scores = block_scores(query_rows, key_heads, seq_ids, positions, seq_ids, positions)
        row_peak = jnp.max(scores, axis=-1, keepdims=True)
        row_expo = jnp.exp(scores - row_peak)
        row_total = jnp.sum(row_expo, axis=-1, keepdims=True)
        prob_rows = (row_expo / row_total).astype(jnp.bfloat16)
        mixed_heads = jnp.einsum(
            "hgqk,khd->qhgd", prob_rows, values, preferred_element_type=jnp.float32
        )
        return (
            mixed_heads.reshape(block_rows, local_kv, per_kv * HD).astype(jnp.bfloat16),
            (row_peak + jnp.log(row_total))[..., 0],
        )

    starts = jnp.arange(group_tok // block_rows, dtype=jnp.int32) * block_rows
    mixed_heads, log_totals = lax.map(one_block, starts)
    return (mixed_heads.reshape(group_tok, local_kv, per_kv * HD), log_totals)


def attend_backward(query_heads, pair_heads, grad_heads, log_totals, seq_ids, positions):
    group_tok, local_kv = (query_heads.shape[0], query_heads.shape[1])
    per_kv = QH // KVH
    block_rows = min(512, group_tok)
    key_heads = pair_heads[:, :, :HD]
    values = pair_heads[:, :, HD:]

    def one_block(running, inputs):
        key_grad, value_grad = running
        block_start, row_lse = inputs
        query_rows = query_heads.reshape(block_rows, local_kv, per_kv, HD)
        grad_rows = grad_heads.reshape(block_rows, local_kv, per_kv, HD)
        scores = block_scores(query_rows, key_heads, seq_ids, positions, seq_ids, positions)
        prob_rows = jnp.exp(scores - row_lse[..., None])
        prob_grad = jnp.einsum(
            "qhgd,khd->hgqk", grad_rows, values, preferred_element_type=jnp.float32
        )
        row_delta = jnp.sum(prob_rows * prob_grad, axis=-1, keepdims=True)
        score_grad = (prob_rows * (prob_grad - row_delta) * HD ** (-0.5)).astype(jnp.bfloat16)
        query_grad = jnp.einsum(
            "hgqk,khd->qhgd", score_grad, key_heads, preferred_element_type=jnp.float32
        )
        key_grad = key_grad + jnp.einsum(
            "hgqk,qhgd->khd", score_grad, query_rows, preferred_element_type=jnp.float32
        )
        value_grad = value_grad + jnp.einsum(
            "hgqk,qhgd->khd",
            prob_rows.astype(jnp.bfloat16),
            grad_rows,
            preferred_element_type=jnp.float32,
        )
        return ((key_grad, value_grad), query_grad)

    starts = jnp.arange(group_tok // block_rows, dtype=jnp.int32) * block_rows
    zero_heads = jnp.zeros((group_tok, local_kv, HD), jnp.float32)
    (key_grad, value_grad), query_grad = lax.scan(
        one_block, (zero_heads, zero_heads), (starts, log_totals)
    )
    return (query_grad.reshape(group_tok, local_kv * per_kv, HD), key_grad, value_grad)


def gather_experts(expand_weight, shrink_weight):
    return (
        lax.all_gather(expand_weight.astype(jnp.bfloat16), "fsdp", axis=1, tiled=True),
        lax.all_gather(shrink_weight.astype(jnp.bfloat16), "fsdp", axis=1, tiled=True),
    )


def adamw_step(weight, gradient, mean_old, square_old, rate, decay):
    drift = beta_first * mean_old + (1.0 - beta_first) * gradient
    spread = beta_second * square_old + (1.0 - beta_second) * gradient * gradient
    mean_hat = drift / (1.0 - beta_first**STEP)
    square_hat = spread / (1.0 - beta_second**STEP)
    master = weight - rate * (mean_hat / (jnp.sqrt(square_hat) + adam_eps) + decay * weight)
    return (drift, spread, master)


def on_device(
    activations,
    cotangent,
    seq_lengths,
    deal_order,
    routes,
    entry_weight,
    entry_mean,
    entry_square,
    exit_weight,
    exit_mean,
    exit_square,
    router_weight,
    router_mean,
    router_square,
    expand_weight,
    expand_mean,
    expand_square,
    shrink_weight,
    shrink_mean,
    shrink_square,
    norm_gains,
    gains_mean,
    gains_square,
):
    tok_dev = activations.shape[1]
    seq_count = lax.axis_size("seq")
    seq_index = lax.axis_index("seq")
    group_tok = tok_dev * seq_count
    local_experts = EXPERTS // seq_count
    query_width = QH * HD
    whole_in, whole_cot = (
        lax.all_gather(activations, "seq", axis=1, tiled=True),
        lax.all_gather(cotangent, "seq", axis=1, tiled=True),
    )
    order_row = deal_order[0]
    my_slots = lax.dynamic_slice_in_dim(order_row, seq_index * tok_dev, tok_dev, 0)
    dealt = jnp.take(whole_in[0], my_slots, axis=0).astype(jnp.float32)
    dealt_cot = jnp.take(whole_cot[0], my_slots, axis=0).astype(jnp.float32)
    seq_ids, positions = seq_layout(seq_lengths[0], order_row)
    my_pos = lax.dynamic_slice_in_dim(positions, seq_index * tok_dev, tok_dev, 0)
    entry_full, exit_full, router_full, gains_full = (
        lax.all_gather(entry_weight.astype(jnp.bfloat16), ("seq", "fsdp"), axis=0, tiled=True),
        lax.all_gather(exit_weight.astype(jnp.bfloat16), ("seq", "fsdp"), axis=0, tiled=True),
        lax.all_gather(router_weight.astype(jnp.bfloat16), ("seq", "fsdp"), axis=0, tiled=True),
        lax.all_gather(norm_gains.astype(jnp.bfloat16), ("seq", "fsdp"), axis=1, tiled=True),
    )
    expand_full, shrink_full = gather_experts(expand_weight, shrink_weight)
    gain_one = gains_full[0].astype(jnp.float32)
    gain_two = gains_full[1].astype(jnp.float32)
    normed = norm_apply(dealt, gain_one).astype(jnp.bfloat16)
    mixed_proj = jnp.dot(normed, entry_full, preferred_element_type=jnp.float32)
    query_rot = rotate(mixed_proj[:, :query_width].reshape(tok_dev, QH, HD), my_pos)
    pair_proj = mixed_proj[:, query_width:].reshape(tok_dev, KVH, 2, HD)
    key_rot = rotate(pair_proj[:, :, 0], my_pos)
    query_send = query_rot.astype(jnp.bfloat16).reshape(tok_dev, KVH, query_width // KVH)
    pair_send = jnp.concatenate([key_rot, pair_proj[:, :, 1]], axis=-1).astype(jnp.bfloat16)
    query_heads, pair_heads = (
        lax.all_to_all(query_send, "seq", split_axis=1, concat_axis=0, tiled=True),
        lax.all_to_all(pair_send, "seq", split_axis=1, concat_axis=0, tiled=True),
    )
    attended_heads, log_totals = attend_forward(query_heads, pair_heads, seq_ids, positions)
    attended = lax.all_to_all(
        attended_heads, "seq", split_axis=0, concat_axis=1, tiled=True
    ).reshape(tok_dev, query_width)
    middle = dealt + jnp.dot(attended, exit_full, preferred_element_type=jnp.float32)
    normed_two = norm_apply(middle, gain_two).astype(jnp.bfloat16)
    logits = jnp.dot(normed_two, router_full, preferred_element_type=jnp.float32)
    route_rows = routes[0]
    picked = jnp.take_along_axis(logits, route_rows, axis=1)
    gate_peak = jnp.max(picked, axis=1, keepdims=True)
    gate_expo = jnp.exp(picked - gate_peak)
    gate_probs = gate_expo / jnp.sum(gate_expo, axis=1, keepdims=True)
    expert_ids = jnp.arange(EXPERTS, dtype=jnp.int32)
    token_ids = jnp.arange(tok_dev, dtype=jnp.int32)
    route_hit = (route_rows[:, :, None] == expert_ids[None, None, :]).astype(jnp.int32)
    chosen = jnp.sum(route_hit, axis=1)
    route_pick = jnp.sum(route_hit * jnp.arange(TOP, dtype=jnp.int32)[None, :, None], axis=1)
    slot_rank = jnp.cumsum(chosen, axis=0) - chosen
    slot_of = jnp.sum(route_hit * slot_rank[:, None, :], axis=2)
    slot_match = (chosen[:, :, None] > 0) & (
        slot_rank[:, :, None] == jnp.arange(CAP, dtype=jnp.int32)[None, None, :]
    )
    filled = jnp.any(slot_match, axis=0)
    source_token = jnp.sum(jnp.where(slot_match, token_ids[:, None, None], 0), axis=0)
    source_pair = jnp.sum(
        jnp.where(slot_match, (token_ids[:, None] * TOP + route_pick)[:, :, None], 0), axis=0
    )
    back_index = (route_rows * CAP + slot_of).reshape(-1)
    send_rows = jnp.where(
        filled[:, :, None],
        jnp.take(normed_two, source_token.reshape(-1), axis=0).reshape(EXPERTS, CAP, D),
        0,
    )
    expert_rows = lax.all_to_all(
        send_rows.reshape(seq_count, local_experts, CAP, D),
        "seq",
        split_axis=0,
        concat_axis=2,
        tiled=True,
    )[0]
    gate_up = jnp.einsum(
        "erd,edf->erf", expert_rows, expand_full, preferred_element_type=jnp.float32
    )
    gate_pre = gate_up[..., :FF]
    up_part = gate_up[..., FF:]
    hidden = (jax.nn.silu(gate_pre) * up_part).astype(jnp.bfloat16)
    expert_out = jnp.einsum(
        "erf,efd->erd", hidden, shrink_full, preferred_element_type=jnp.float32
    ).astype(jnp.bfloat16)
    returned = lax.all_to_all(
        expert_out[None], "seq", split_axis=2, concat_axis=0, tiled=True
    ).reshape(EXPERTS * CAP, D)
    routed_out = jnp.take(returned, back_index, axis=0).reshape(tok_dev, TOP, D).astype(jnp.float32)
    output_rows = middle + jnp.sum(gate_probs[:, :, None] * routed_out, axis=1)
    gate_grad = jnp.sum(routed_out * dealt_cot[:, None, :], axis=2)
    expert_grad = (
        (gate_probs[:, :, None] * dealt_cot[:, None, :])
        .astype(jnp.bfloat16)
        .reshape(tok_dev * TOP, D)
    )
    grad_send = jnp.where(
        filled[:, :, None],
        jnp.take(expert_grad, source_pair.reshape(-1), axis=0).reshape(EXPERTS, CAP, D),
        0,
    )
    grad_rows = lax.all_to_all(
        grad_send.reshape(seq_count, local_experts, CAP, D),
        "seq",
        split_axis=0,
        concat_axis=2,
        tiled=True,
    )[0]
    held = lax.optimization_barrier((expand_weight, shrink_weight, grad_rows))
    expand_back, shrink_back = gather_experts(held[0], held[1])
    hidden_grad = jnp.einsum(
        "erd,efd->erf", grad_rows, shrink_back, preferred_element_type=jnp.float32
    )
    gate_sig = jax.nn.sigmoid(gate_pre)
    up_grad = jnp.concatenate(
        [
            hidden_grad * up_part * gate_sig * (1.0 + gate_pre * (1.0 - gate_sig)),
            hidden_grad * gate_pre * gate_sig,
        ],
        axis=-1,
    ).astype(jnp.bfloat16)
    shrink_grad = jnp.einsum("erf,erd->efd", hidden, grad_rows, preferred_element_type=jnp.float32)
    expand_grad = jnp.einsum(
        "erd,erf->edf", expert_rows, up_grad, preferred_element_type=jnp.float32
    )
    expand_sum, shrink_sum = (
        lax.psum_scatter(
            expand_grad.astype(jnp.bfloat16), "fsdp", scatter_dimension=1, tiled=True
        ).astype(jnp.float32),
        lax.psum_scatter(
            shrink_grad.astype(jnp.bfloat16), "fsdp", scatter_dimension=1, tiled=True
        ).astype(jnp.float32),
    )
    row_grad = jnp.einsum(
        "erf,edf->erd", up_grad, expand_back, preferred_element_type=jnp.float32
    ).astype(jnp.bfloat16)
    row_back = lax.all_to_all(
        row_grad[None], "seq", split_axis=2, concat_axis=0, tiled=True
    ).reshape(EXPERTS * CAP, D)
    normed_two_grad = jnp.sum(
        jnp.take(row_back, back_index, axis=0).reshape(tok_dev, TOP, D).astype(jnp.float32), axis=1
    )
    mean_term = jnp.sum(gate_probs * gate_grad, axis=1, keepdims=True)
    picked_grad = gate_probs * (gate_grad - mean_term)
    logit_grad = jnp.sum(route_hit.astype(jnp.float32) * picked_grad[:, :, None], axis=1).astype(
        jnp.bfloat16
    )
    router_grad = jnp.dot(normed_two.T, logit_grad, preferred_element_type=jnp.float32)
    normed_two_grad = normed_two_grad + jnp.dot(
        logit_grad, router_full.T, preferred_element_type=jnp.float32
    )
    middle_value, norm_two_pull = jax.vjp(norm_apply, middle, gain_two)
    middle_back, gain_two_grad = norm_two_pull(normed_two_grad)
    middle_grad = dealt_cot + middle_back
    branch_grad = middle_grad.astype(jnp.bfloat16)
    exit_grad = jnp.dot(attended.T, branch_grad, preferred_element_type=jnp.float32)
    attended_grad = (
        jnp.dot(branch_grad, exit_full.T, preferred_element_type=jnp.float32)
        .astype(jnp.bfloat16)
        .reshape(tok_dev, KVH, query_width // KVH)
    )
    grad_heads = lax.all_to_all(attended_grad, "seq", split_axis=1, concat_axis=0, tiled=True)
    query_grad, key_grad, value_grad = attend_backward(
        query_heads, pair_heads, grad_heads, log_totals, seq_ids, positions
    )
    local_kv = key_grad.shape[1]
    query_back = (
        rotate_back(query_grad, positions)
        .astype(jnp.bfloat16)
        .reshape(group_tok, local_kv, query_width // KVH)
    )
    pair_back = jnp.concatenate([rotate_back(key_grad, positions), value_grad], axis=-1).astype(
        jnp.bfloat16
    )
    query_home, pair_home = (
        lax.all_to_all(query_back, "seq", split_axis=0, concat_axis=1, tiled=True),
        lax.all_to_all(pair_back, "seq", split_axis=0, concat_axis=1, tiled=True),
    )
    mixed_grad = jnp.concatenate(
        [query_home.reshape(tok_dev, query_width), pair_home.reshape(tok_dev, 2 * KVH * HD)], axis=1
    )
    entry_grad = jnp.dot(normed.T, mixed_grad, preferred_element_type=jnp.float32)
    normed_grad = jnp.dot(mixed_grad, entry_full.T, preferred_element_type=jnp.float32)
    dealt_value, norm_one_pull = jax.vjp(norm_apply, dealt, gain_one)
    dealt_back, gain_one_grad = norm_one_pull(normed_grad)
    input_rows = middle_grad + dealt_back
    entry_sum, exit_sum, router_sum, gains_sum = (
        lax.psum_scatter(entry_grad, ("seq", "fsdp"), scatter_dimension=0, tiled=True),
        lax.psum_scatter(exit_grad, ("seq", "fsdp"), scatter_dimension=0, tiled=True),
        lax.psum_scatter(router_grad, ("seq", "fsdp"), scatter_dimension=0, tiled=True),
        lax.psum_scatter(
            jnp.stack([gain_one_grad, gain_two_grad]),
            ("seq", "fsdp"),
            scatter_dimension=1,
            tiled=True,
        ),
    )
    output_all, input_all = (
        lax.all_gather(output_rows.astype(jnp.bfloat16), "seq", axis=0, tiled=True),
        lax.all_gather(input_rows.astype(jnp.bfloat16), "seq", axis=0, tiled=True),
    )
    natural_ids = seq_index * tok_dev + token_ids
    slot_of_token = jnp.sum(
        jnp.where(
            order_row[None, :] == natural_ids[:, None],
            jnp.arange(group_tok, dtype=jnp.int32)[None, :],
            0,
        ),
        axis=1,
    )
    block_output = jnp.take(output_all, slot_of_token, axis=0)[None]
    input_grad = jnp.take(input_all, slot_of_token, axis=0)[None]
    entry_drift, entry_spread, entry_master = adamw_step(
        entry_weight, entry_sum, entry_mean, entry_square, 0.02, weight_decay
    )
    exit_drift, exit_spread, exit_master = adamw_step(
        exit_weight, exit_sum, exit_mean, exit_square, 0.15, weight_decay
    )
    router_drift, router_spread, router_master = adamw_step(
        router_weight, router_sum, router_mean, router_square, 0.01, weight_decay
    )
    expand_drift, expand_spread, expand_master = adamw_step(
        expand_weight, expand_sum, expand_mean, expand_square, 0.02, weight_decay
    )
    shrink_drift, shrink_spread, shrink_master = adamw_step(
        shrink_weight, shrink_sum, shrink_mean, shrink_square, 0.12, weight_decay
    )
    gains_drift, gains_spread, gains_master = adamw_step(
        norm_gains, gains_sum, gains_mean, gains_square, 0.5, 0.0
    )
    return (
        block_output,
        input_grad,
        entry_drift,
        entry_spread,
        entry_master,
        exit_drift,
        exit_spread,
        exit_master,
        router_drift,
        router_spread,
        router_master,
        expand_drift,
        expand_spread,
        expand_master,
        shrink_drift,
        shrink_spread,
        shrink_master,
        gains_drift,
        gains_spread,
        gains_master,
    )


def solution(mesh):
    return jax.shard_map(
        on_device,
        mesh=mesh,
        in_specs=(
            P("fsdp", "seq", None),
            P("fsdp", "seq", None),
            P("fsdp", None),
            P("fsdp", None),
            P("fsdp", "seq", None),
            P(("seq", "fsdp"), None),
            P(("seq", "fsdp"), None),
            P(("seq", "fsdp"), None),
            P(("seq", "fsdp"), None),
            P(("seq", "fsdp"), None),
            P(("seq", "fsdp"), None),
            P(("seq", "fsdp"), None),
            P(("seq", "fsdp"), None),
            P(("seq", "fsdp"), None),
            P("seq", "fsdp", None),
            P("seq", "fsdp", None),
            P("seq", "fsdp", None),
            P("seq", "fsdp", None),
            P("seq", "fsdp", None),
            P("seq", "fsdp", None),
            P(None, ("seq", "fsdp")),
            P(None, ("seq", "fsdp")),
            P(None, ("seq", "fsdp")),
        ),
        out_specs=(
            P("fsdp", "seq", None),
            P("fsdp", "seq", None),
            P(("seq", "fsdp"), None),
            P(("seq", "fsdp"), None),
            P(("seq", "fsdp"), None),
            P(("seq", "fsdp"), None),
            P(("seq", "fsdp"), None),
            P(("seq", "fsdp"), None),
            P(("seq", "fsdp"), None),
            P(("seq", "fsdp"), None),
            P(("seq", "fsdp"), None),
            P("seq", "fsdp", None),
            P("seq", "fsdp", None),
            P("seq", "fsdp", None),
            P("seq", "fsdp", None),
            P("seq", "fsdp", None),
            P("seq", "fsdp", None),
            P(None, ("seq", "fsdp")),
            P(None, ("seq", "fsdp")),
            P(None, ("seq", "fsdp")),
        ),
        check_vma=False,
    )
```

profile of v0, /device:TPU:1, one launch (start us, length us, event | category | flops | bytes accessed | tf_op | source)
XLA Modules:
  0.0 1835.9 jit_solution(11031941977464848905)
XLA Ops:
  17.9 34.4 %all-gather = bf16[128,12,2]{1,2,0:T(2,128)(2,1)S(1)} all-gather(bf16[1,12,2]{1,2,0:T(2,128)(2,1)S(1)} %convert_bitcast_fusion.4), channel_id=1, replica_groups=mesh['seq'=4,'fsdp'=32] {'seq','fsdp'}, dimensions={0}, use_global_device_ids=true | all-gather | bytes 6192 | tf_op jit(solution)/shard_map/all_gather | solution.py:212
  53.9 33.8 %all-gather.3 = bf16[128,12,40]{2,1,0:T(8,128)(2,1)S(1)} all-gather(bf16[1,12,40]{2,1,0:T(8,128)(2,1)S(1)} %convert_bitcast_fusion.3), channel_id=1, replica_groups=mesh['seq'=4,'fsdp'=32] {'seq','fsdp'}, dimensions={0}, use_global_device_ids=true | all-gather | bytes 123840 | tf_op jit(solution)/shard_map/all_gather | solution.py:211
  93.4 22.1 %all-gather.31.cloned.1.call-done = bf16[128,12,2560]{2,1,0:T(8,128)(2,1)} async-done(((bf16[1,12,2560]{2,1,0:T(8,128)(2,1)}), bf16[128,12,2560]{2,1,0:T(8,128)(2,1)}) %all-gather.31.cloned.1.call-update) | async-done | bytes 7864336 | tf_op jit(solution)/shard_map/all_gather | solution.py:209
  115.5 12.8 reshape.754
  165.0 51.7 %all-gather.33.cloned.1.call-done = bf16[128,12,1536]{2,1,0:T(8,128)(2,1)} async-done(((bf16[1,12,1536]{2,1,0:T(8,128)(2,1)}), bf16[128,12,1536]{2,1,0:T(8,128)(2,1)}) %all-gather.33.cloned.1.call-update) | async-done | bytes 4718608 | tf_op jit(solution)/shard_map/all_gather | solution.py:210
  216.7 8.2 reshape.756
  269.7 48.2 %all_to_all.153 = bf16[4,10,29,1536]{3,2,1,0:T(8,128)(2,1)S(1)} all-to-all(bf16[4,10,29,1536]{3,2,1,0:T(8,128)(2,1)S(1)} %get-tuple-element.140), channel_id=1, replica_groups=mesh['seq'=4,'fsdp'=32] {'seq'}, dimensions={0} | all-to-all | bytes 7127040 | tf_op jit(solution)/shard_map/all_to_all | solution.py:293
  327.0 48.4 %all_to_all.154 = bf16[4,10,29,1536]{3,2,1,0:T(8,128)(2,1)S(1)} all-to-all(bf16[4,10,29,1536]{3,2,1,0:T(8,128)(2,1)} %get-tuple-element.139), channel_id=1, replica_groups=mesh['seq'=4,'fsdp'=32] {'seq'}, dimensions={0} | all-to-all | bytes 7127040 | tf_op jit(solution)/shard_map/all_to_all | solution.py:261
  383.9 18.4 %fusion.101 = f32[10,116,1024]{2,1,0:T(8,128)} fusion(bf16[10,116,1536]{2,1,0:T(8,128)(2,1)} %squeeze.43, bf16[10,1536,1024]{2,1,0:T(8,128)(2,1)} %all-gather.17.cloned.1.call-done), kind=kOutput, calls=%fused_computation.228 | convolution fusion | flops 3649044480 | bytes 39772160 | tf_op jit(solution)/shard_map/erd,edf->erf/dot_general | solution.py:268
  402.3 11.7 multiply_convert_fusion.1
  414.0 9.7 convolution_convert_fusion.1
  426.5 108.1 %reduce-scatter.12.cloned.1.call-done = bf16[10,16,1536]{2,1,0:T(8,128)(2,1)} async-done(((bf16[10,512,1536]{2,1,0:T(8,128)(2,1)}), bf16[10,16,1536]{2,1,0:T(8,128)(2,1)}) %reduce-scatter.12.cloned.1.call-update) | async-done | bytes 491536 | tf_op jit(solution)/shard_map/reduce_scatter | solution.py:321
  539.4 16.3 convolution_convert_fusion
  555.7 91.3 %all-gather.27.cloned.1.call-done = bf16[10,1536,1024]{2,1,0:T(8,128)(2,1)} async-done(((bf16[10,48,1024]{2,1,0:T(8,128)(2,1)}), bf16[10,1536,1024]{2,1,0:T(8,128)(2,1)}) %all-gather.27.cloned.1.call-update) | async-done | bytes 31457296 | tf_op jit(solution)/shard_map/all_gather | solution.py:153
  647.0 17.6 fusion.14
  675.8 43.3 %all-gather.19.cloned.1.call-done = bf16[10,512,1536]{2,1,0:T(8,128)(2,1)} async-done(((bf16[10,16,1536]{2,1,0:T(8,128)(2,1)}), bf16[10,512,1536]{2,1,0:T(8,128)(2,1)}) %all-gather.19.cloned.1.call-update) | async-done | bytes 15728656 | tf_op jit(solution)/shard_map/all_gather | solution.py:154
  719.1 7.7 fusion.13
  730.8 10.1 all-to-all-done.6
  761.2 10.4 gather_fusion.7
  771.7 39.2 %all-to-all-done.4 = bf16[1,10,116,1536]{3,1,0,2:T(8,128)(2,1)} async-done(((bf16[1,10,116,1536]{3,1,0,2:T(8,128)(2,1)}), bf16[1,10,116,1536]{3,1,0,2:T(8,128)(2,1)}, u32[]{:S(2)}, u32[]{:S(2)}) %all-to-all-start.4) | async-done | bytes 3563552 | tf_op jit(solution)/shard_map/all_to_all | solution.py:277
  823.9 9.2 gather_fusion.4
  862.5 11.3 fusion.28
  882.1 12.0 fusion.21
  909.0 7.8 fusion.48
  916.8 410.9 %fusion.88 = (f32[16,2560]{1,0:T(8,128)}, f32[16,1536]{1,0:T(8,128)S(1)}, f32[16,40]{1,0:T(8,128)S(1)}) fusion(f32[1536,2560]{1,0:T(8,128)} %fusion.48, f32[1536,1536]{1,0:T(8,128)} %fusion.50, f32[1536,40]{1,0:T(8,128)S(1)} %fusion.102), kind=kCustom, calls=%all-reduce-scatter.3 | all-reduce-scatter fusion | flops 8470529 | bytes 25676288
  1339.5 10.6 collective-permute-start.86
  1468.9 9.6 collective-permute-start.42
  1524.2 10.4 collective-permute-done.31
  1575.9 68.1 %all-reduce.3 = f32[2,1536]{1,0:T(2,128)S(1)} all-reduce(f32[2,1536]{1,0:T(2,128)S(1)} %pad_maximum_fusion.10), channel_id=7, replica_groups=mesh['seq'=4,'fsdp'=32] {'seq','fsdp'}, use_global_device_ids=true, to_apply=%region_32.35.clone | all-reduce | flops 3072 | bytes 24576
  1667.2 24.6 %concatenate.34 = f32[524,40]{1,0:T(8,128)S(1)} concatenate(f32[12,40]{1,0:T(8,128)} %copy-done.107, f32[16,40]{1,0:T(8,128)} %copy-done.108, f32[16,40]{1,0:T(8,128)} %copy-done.109, f32[16,40]{1,0:T(8,128)} %copy-done.110, f32[16,40]{1,0:T(8,128)} %copy-done.111, f32[16,40]{1,0:T(8,128)} %copy-done.112, f32[16,40]{1,0:T(8,128)} %copy-done.113, f32[16,40]{1,0:T(8,128)} %copy-done.114, ...), dimensions={0} | concatenate | bytes 167680
  1710.2 31.7 %concatenate.33 = f32[524,1536]{1,0:T(8,128)S(1)} concatenate(f32[12,1536]{1,0:T(8,128)} %copy-done.61, f32[16,1536]{1,0:T(8,128)} %copy-done.58, f32[16,1536]{1,0:T(8,128)} %copy-done.59, f32[16,1536]{1,0:T(8,128)} %copy-done.60, f32[16,1536]{1,0:T(8,128)} %copy-done.62, f32[16,1536]{1,0:T(8,128)} %copy-done.63, f32[16,1536]{1,0:T(8,128)} %copy-done.64, f32[16,1536]{1,0:T(8,128)} %copy-done.65, ...), dimensions={0} | concatenate | bytes 6438912
  1762.2 57.5 %concatenate.32 = f32[524,2560]{1,0:T(8,128)} concatenate(f32[12,2560]{1,0:T(8,128)} %copy-done.33, f32[16,2560]{1,0:T(8,128)} %collective-permute-done.30, f32[16,2560]{1,0:T(8,128)} %collective-permute-done.29, f32[16,2560]{1,0:T(8,128)} %collective-permute-done.28, f32[16,2560]{1,0:T(8,128)} %collective-permute-done.27, f32[16,2560]{1,0:T(8,128)} %copy-done.34, ...), dimensions={0} | concatenate | bytes 10731520
  (709 shorter events, 510.1 us)
Async XLA Ops:
  7.2 83.0 %all-gather.15.cloned.1.call-start = ((), (), s32[]{:S(2)}) async-start(), calls=%async_computation.12 | async-start | bytes 1966080 | tf_op jit(solution)/shard_map/all_gather | solution.py:199
  8.0 107.5 %all-gather.31.cloned.1.call-start = ((), (), s32[]{:S(2)}) async-start(), calls=%async_computation.22 | async-start | bytes 10567680 | tf_op jit(solution)/shard_map/all_gather | solution.py:209
  9.6 139.5 %all-gather.23.cloned.1.call-start = ((), (), s32[]{:S(2)}) async-start(), calls=%async_computation.16 | async-start | bytes 1966080 | tf_op jit(solution)/shard_map/all_gather | solution.py:200
  10.4 206.3 %all-gather.33.cloned.1.call-start = ((), (), s32[]{:S(2)}) async-start(), calls=%async_computation.23 | async-start | bytes 6340608 | tf_op jit(solution)/shard_map/all_gather | solution.py:210
  11.9 371.9 %all-gather.17.cloned.1.call-start = ((), (), s32[]{:S(2)}) async-start(), calls=%async_computation.13 | async-start | bytes 32440320 | tf_op jit(solution)/shard_map/all_gather | solution.py:153
  160.4 64.5 %all-to-all-start.2 = ((bf16[512,2,192]{2,1,0:T(2,128)(2,1)}), bf16[512,2,192]{2,1,0:T(2,128)(2,1)S(1)}, u32[]{:S(2)}, u32[]{:S(2)}) async-start(bf16[512,2,192]{2,1,0:T(2,128)(2,1)} %copy.163), calls=%async_computation.2 | async-start | bytes 1048576 | tf_op jit(solution)/shard_map/all_to_all | solution.py:229
  163.9 238.4 %all-gather.25.cloned.1.call-start = ((), (), s32[]{:S(2)}) async-start(), calls=%async_computation.17 | async-start | bytes 16220160 | tf_op jit(solution)/shard_map/all_gather | solution.py:154
  327.0 207.6 %reduce-scatter.12.cloned.1.call-start = ((), (), s32[]{:S(2)}) async-start(), calls=%async_computation.21 | async-start | bytes 16220160 | tf_op jit(solution)/shard_map/reduce_scatter | solution.py:321
  423.8 223.2 %all-gather.27.cloned.1.call-start = ((), (), s32[]{:S(2)}) async-start(), calls=%async_computation.18 | async-start | bytes 32440320 | tf_op jit(solution)/shard_map/all_gather | solution.py:153
  426.4 292.6 %all-gather.19.cloned.1.call-start = ((), (), s32[]{:S(2)}) async-start(), calls=%async_computation.14 | async-start | bytes 16220160 | tf_op jit(solution)/shard_map/all_gather | solution.py:154
  539.1 1017.0 %reduce-scatter.10.cloned.1.call-start = ((), (), s32[]{:S(2)}) async-start(), calls=%async_computation.20 | async-start | bytes 32440320 | tf_op jit(solution)/shard_map/reduce_scatter | solution.py:318
  670.6 70.3 %all-to-all-start.6 = ((bf16[1,10,116,1536]{3,1,0,2:T(8,128)(2,1)}), bf16[1,10,116,1536]{3,1,0,2:T(8,128)(2,1)}, u32[]{:S(2)}, u32[]{:S(2)}) async-start(bf16[1,10,116,1536]{3,1,0,2:T(8,128)(2,1)} %copy.185), calls=%async_computation.6 | async-start | bytes 11403264 | tf_op jit(solution)/shard_map/all_to_all | solution.py:328
  740.9 70.0 %all-to-all-start.4 = ((bf16[1,10,116,1536]{3,1,0,2:T(8,128)(2,1)}), bf16[1,10,116,1536]{3,1,0,2:T(8,128)(2,1)}, u32[]{:S(2)}, u32[]{:S(2)}) async-start(bf16[1,10,116,1536]{3,1,0,2:T(8,128)(2,1)} %copy.179), calls=%async_computation.4 | async-start | bytes 11403264 | tf_op jit(solution)/shard_map/all_to_all | solution.py:277
  900.8 920.8 %all-gather.21.cloned.1.call-start = ((), (), s32[]{:S(2)}) async-start(), calls=%async_computation.15 | async-start | bytes 1966080 | tf_op jit(solution)/shard_map/all_gather | solution.py:390
  905.8 918.7 %all-gather.29.cloned.1.call-start = ((), (), s32[]{:S(2)}) async-start(), calls=%async_computation.19 | async-start | bytes 1966080 | tf_op jit(solution)/shard_map/all_gather | solution.py:391
  1483.1 27.2 %collective-permute-start.38 = (f32[16,1536]{1,0:T(8,128)S(1)}, f32[16,1536]{1,0:T(8,128)S(1)}, u32[]{:S(2)}, u32[]{:S(2)}) collective-permute-start(f32[16,1536]{1,0:T(8,128)S(1)} %get-tuple-element.99), channel_id=1, source_target_pairs={{0,7},{1,8},{2,9},{3,10},{4,11},{5,12},{6,13},{7,14},{8,15},{9,16}... | collective-permute-start | bytes 294920
  1484.4 27.5 %collective-permute-start.37 = (f32[16,1536]{1,0:T(8,128)S(1)}, f32[16,1536]{1,0:T(8,128)S(1)}, u32[]{:S(2)}, u32[]{:S(2)}) collective-permute-start(f32[16,1536]{1,0:T(8,128)S(1)} %get-tuple-element.99), channel_id=1, source_target_pairs={{0,6},{1,7},{2,8},{3,9},{4,10},{5,11},{6,12},{7,13},{8,14},{9,15},... | collective-permute-start | bytes 294920
  1562.4 81.5 %collective-permute-start.19 = (f32[16,2560]{1,0:T(8,128)}, f32[16,2560]{1,0:T(8,128)S(1)}, u32[]{:S(2)}, u32[]{:S(2)}) collective-permute-start(f32[16,2560]{1,0:T(8,128)} %get-tuple-element.98), channel_id=1, source_target_pairs={{0,20},{1,21},{2,22},{3,23},{4,24},{5,25},{6,26},{7,27},{8,28},{9,... | collective-permute-start | bytes 491528
  1567.9 80.0 %collective-permute-start.18 = (f32[16,2560]{1,0:T(8,128)}, f32[16,2560]{1,0:T(8,128)S(1)}, u32[]{:S(2)}, u32[]{:S(2)}) collective-permute-start(f32[16,2560]{1,0:T(8,128)} %get-tuple-element.98), channel_id=1, source_target_pairs={{0,19},{1,20},{2,21},{3,22},{4,23},{5,24},{6,25},{7,26},{8,27},{9,... | collective-permute-start | bytes 491528
  1569.4 81.9 %collective-permute-start.17 = (f32[16,2560]{1,0:T(8,128)}, f32[16,2560]{1,0:T(8,128)S(1)}, u32[]{:S(2)}, u32[]{:S(2)}) collective-permute-start(f32[16,2560]{1,0:T(8,128)} %get-tuple-element.98), channel_id=1, source_target_pairs={{0,18},{1,19},{2,20},{3,21},{4,22},{5,23},{6,24},{7,25},{8,26},{9,... | collective-permute-start | bytes 491528
  1572.8 81.8 %collective-permute-start.16 = (f32[16,2560]{1,0:T(8,128)}, f32[16,2560]{1,0:T(8,128)S(1)}, u32[]{:S(2)}, u32[]{:S(2)}) collective-permute-start(f32[16,2560]{1,0:T(8,128)} %get-tuple-element.98), channel_id=1, source_target_pairs={{0,17},{1,18},{2,19},{3,20},{4,21},{5,22},{6,23},{7,24},{8,25},{9,... | collective-permute-start | bytes 491528
  1574.2 85.1 %collective-permute-start.15 = (f32[16,2560]{1,0:T(8,128)}, f32[16,2560]{1,0:T(8,128)S(1)}, u32[]{:S(2)}, u32[]{:S(2)}) collective-permute-start(f32[16,2560]{1,0:T(8,128)} %get-tuple-element.98), channel_id=1, source_target_pairs={{0,16},{1,17},{2,18},{3,19},{4,20},{5,21},{6,22},{7,23},{8,24},{9,... | collective-permute-start | bytes 491528
  1644.0 47.9 %collective-permute-start.14 = (f32[16,2560]{1,0:T(8,128)}, f32[16,2560]{1,0:T(8,128)S(1)}, u32[]{:S(2)}, u32[]{:S(2)}) collective-permute-start(f32[16,2560]{1,0:T(8,128)} %get-tuple-element.98), channel_id=1, source_target_pairs={{0,15},{1,16},{2,17},{3,18},{4,19},{5,20},{6,21},{7,22},{8,23},{9,... | collective-permute-start | bytes 491528
  1647.8 46.0 %collective-permute-start.13 = (f32[16,2560]{1,0:T(8,128)}, f32[16,2560]{1,0:T(8,128)S(1)}, u32[]{:S(2)}, u32[]{:S(2)}) collective-permute-start(f32[16,2560]{1,0:T(8,128)} %get-tuple-element.98), channel_id=1, source_target_pairs={{0,14},{1,15},{2,16},{3,17},{4,18},{5,19},{6,20},{7,21},{8,22},{9,... | collective-permute-start | bytes 491528
  1651.3 45.9 %collective-permute-start.12 = (f32[16,2560]{1,0:T(8,128)}, f32[16,2560]{1,0:T(8,128)S(1)}, u32[]{:S(2)}, u32[]{:S(2)}) collective-permute-start(f32[16,2560]{1,0:T(8,128)} %get-tuple-element.98), channel_id=1, source_target_pairs={{0,13},{1,14},{2,15},{3,16},{4,17},{5,18},{6,19},{7,20},{8,21},{9,... | collective-permute-start | bytes 491528
  1654.6 45.7 %collective-permute-start.11 = (f32[16,2560]{1,0:T(8,128)}, f32[16,2560]{1,0:T(8,128)S(1)}, u32[]{:S(2)}, u32[]{:S(2)}) collective-permute-start(f32[16,2560]{1,0:T(8,128)} %get-tuple-element.98), channel_id=1, source_target_pairs={{0,12},{1,13},{2,14},{3,15},{4,16},{5,17},{6,18},{7,19},{8,20},{9,... | collective-permute-start | bytes 491528
  1659.3 45.5 %collective-permute-start.10 = (f32[16,2560]{1,0:T(8,128)}, f32[16,2560]{1,0:T(8,128)S(1)}, u32[]{:S(2)}, u32[]{:S(2)}) collective-permute-start(f32[16,2560]{1,0:T(8,128)} %get-tuple-element.98), channel_id=1, source_target_pairs={{0,11},{1,12},{2,13},{3,14},{4,15},{5,16},{6,17},{7,18},{8,19},{9,... | collective-permute-start | bytes 491528
  1691.8 50.1 %collective-permute-start.9 = (f32[16,2560]{1,0:T(8,128)}, f32[16,2560]{1,0:T(8,128)}, u32[]{:S(2)}, u32[]{:S(2)}) collective-permute-start(f32[16,2560]{1,0:T(8,128)} %get-tuple-element.98), channel_id=1, source_target_pairs={{0,10},{1,11},{2,12},{3,13},{4,14},{5,15},{6,16},{7,17},{8,18},{9,... | collective-permute-start | bytes 491528
  1693.8 52.4 %collective-permute-start.8 = (f32[16,2560]{1,0:T(8,128)}, f32[16,2560]{1,0:T(8,128)}, u32[]{:S(2)}, u32[]{:S(2)}) collective-permute-start(f32[16,2560]{1,0:T(8,128)} %get-tuple-element.98), channel_id=1, source_target_pairs={{0,9},{1,10},{2,11},{3,12},{4,13},{5,14},{6,15},{7,16},{8,17},{9,1... | collective-permute-start | bytes 491528
  1697.2 51.7 %collective-permute-start.7 = (f32[16,2560]{1,0:T(8,128)}, f32[16,2560]{1,0:T(8,128)}, u32[]{:S(2)}, u32[]{:S(2)}) collective-permute-start(f32[16,2560]{1,0:T(8,128)} %get-tuple-element.98), channel_id=1, source_target_pairs={{0,8},{1,9},{2,10},{3,11},{4,12},{5,13},{6,14},{7,15},{8,16},{9,17... | collective-permute-start | bytes 491528
  1700.3 53.0 %collective-permute-start.6 = (f32[16,2560]{1,0:T(8,128)}, f32[16,2560]{1,0:T(8,128)}, u32[]{:S(2)}, u32[]{:S(2)}) collective-permute-start(f32[16,2560]{1,0:T(8,128)} %get-tuple-element.98), channel_id=1, source_target_pairs={{0,7},{1,8},{2,9},{3,10},{4,11},{5,12},{6,13},{7,14},{8,15},{9,16}... | collective-permute-start | bytes 491528
  1704.8 50.7 %collective-permute-start.5 = (f32[16,2560]{1,0:T(8,128)}, f32[16,2560]{1,0:T(8,128)}, u32[]{:S(2)}, u32[]{:S(2)}) collective-permute-start(f32[16,2560]{1,0:T(8,128)} %get-tuple-element.98), channel_id=1, source_target_pairs={{0,6},{1,7},{2,8},{3,9},{4,10},{5,11},{6,12},{7,13},{8,14},{9,15},... | collective-permute-start | bytes 491528
  (238 other events, 8736.2 us)
Sparse Core Ops, SparseCore 0:
  9.7 29.9 all-gather.14
  43.4 71.9 all-gather.30
  117.1 24.4 all-gather.22
  145.2 71.4 all-gather.32
  219.4 105.8 all-gather.16
  328.0 69.5 all-gather.24
  423.9 110.6 reduce-scatter.11
  537.7 109.2 all-gather.26
  649.5 69.5 all-gather.18
  723.4 158.2 reduce-scatter.9
  906.0 34.1 all-gather.20
  1541.9 55.2 all-gather.28
where the time goes:
time: 1850 us; the launch traced here: 1840 us
  blocking collectives  644 us (35%)
  waiting for transfers between devices  401 us (22%)
  starting transfers between devices  301 us (16%)
  local copies, waits for them, and re-layouts  267 us (14%)
  matrix products  146 us (8%)
  other arithmetic  58.6 us (3%)
    unnamed x2, blocking collectives  479 us
    unnamed x96, starting transfers between devices  267 us
    unnamed x319, local copies, waits for them, and re-layouts  142 us
    reduce_scatter x1, waiting for transfers between devices, on_device(): lax.psum_scatter(shrink_grad.astype(jnp.bfloat16), 'fsdp', scatter_dimens...  108 us
    all_gather x2, waiting for transfers between devices, gather_experts(): lax.all_gather(expand_weight.astype(jnp.bfloat16), 'fsdp', axis=1, tiled=...  91.3 us
    all_gather x1, waiting for transfers between devices, on_device(): lax.all_gather(exit_weight.astype(jnp.bfloat16), ('seq', 'fsdp'), axis=0,...  51.7 us
    all_to_all x1, blocking collectives, on_device(): lax.all_to_all(send_rows.reshape(seq_count, local_experts, CAP, D), 'seq'...  48.4 us
    all_to_all x1, blocking collectives, on_device(): lax.all_to_all(grad_send.reshape(seq_count, local_experts, CAP, D), 'seq'...  48.2 us
  transfers between devices with their start and end apart: 116, of which 15 were waited for; matrix products, arithmetic and copies ran while one was open for 46% of the time, Pallas kernels for 0%

commit v1 on v0

v1 whole, which is shorter than its diff:
```python
import jax
import jax.numpy as jnp
from jax import lax
from jax.experimental import pallas as pl
from jax.experimental.pallas import tpu as pltpu
from jax.sharding import Mesh, PartitionSpec as P

D = 1536
QH = 24
KVH = 8
HD = 64
FF = 512
EXPERTS = 40
TOP = 8
STEP = 10
CAP = 29

N_SEQ = 4
TOK_DEV = 128
GROUP = 512
PAIR_TOK = 2 * GROUP
LOCAL_E = EXPERTS // (2 * N_SEQ)
SLOTS = 240
Q_OWN = QH * HD // N_SEQ
KV_OWN = 2 * KVH * HD // N_SEQ
MIX_OWN = Q_OWN + KV_OWN
HEADS_OWN = QH // N_SEQ
KV_HEADS_OWN = KVH // N_SEQ
PER_KV = QH // KVH
ROWS = 12

norm_eps = 1e-06
rope_base = 10000.0
beta_first = 0.9
beta_second = 0.95
adam_eps = 1e-08
weight_decay = 0.1

FSDP = ("x", "y", "core")
PLANE = ("x", "y")
f32 = jnp.float32
bf16 = jnp.bfloat16


def dot(a, b, dims):
    return lax.dot_general(a, b, (dims, ((), ())), preferred_element_type=f32)


def z_exchange(call_id, gathered=(), scattered=()):
    arrays = list(gathered) + list(scattered)
    n_gather = len(gathered)
    count = len(arrays)

    def kernel(*refs):
        ins, outs = refs[:count], refs[count : 2 * count]
        send_sem, recv_sem, copy_sem = refs[2 * count :]
        me = lax.axis_index("seq")
        peers = [lax.rem(me + k, N_SEQ) for k in range(1, N_SEQ)]
        barrier = pltpu.get_barrier_semaphore()
        for peer in peers:
            pl.semaphore_signal(
                barrier, inc=1, device_id={"seq": peer}, device_id_type=pl.DeviceIdType.MESH
            )
        pl.semaphore_wait(barrier, N_SEQ - 1)
        copies = []
        for i in range(count):
            for k in (0, 2, 1):
                peer = peers[k]
                source = ins[i] if i < n_gather else ins[i].at[peer]
                copy = pltpu.make_async_remote_copy(
                    src_ref=source,
                    dst_ref=outs[i].at[me],
                    send_sem=send_sem.at[i, k],
                    recv_sem=recv_sem.at[i, k],
                    device_id={"seq": peer},
                    device_id_type=pl.DeviceIdType.MESH,
                )
                copy.start()
                copies.append(copy)
        for i in range(count):
            source = ins[i] if i < n_gather else ins[i].at[me]
            copy = pltpu.make_async_copy(source, outs[i].at[me], copy_sem.at[i])
            copy.start()
            copies.append(copy)
        for copy in copies:
            copy.wait()

    shapes = [
        jax.ShapeDtypeStruct((N_SEQ,) + a.shape if i < n_gather else a.shape, a.dtype)
        for i, a in enumerate(arrays)
    ]
    return pl.pallas_call(
        kernel,
        out_shape=shapes,
        in_specs=[pl.BlockSpec(memory_space=pl.ANY)] * count,
        out_specs=[pl.BlockSpec(memory_space=pl.ANY)] * count,
        scratch_shapes=[
            pltpu.SemaphoreType.DMA((count, N_SEQ - 1)),
            pltpu.SemaphoreType.DMA((count, N_SEQ - 1)),
            pltpu.SemaphoreType.DMA((count,)),
        ],
        compiler_params=pltpu.CompilerParams(collective_id=call_id, has_side_effects=True),
    )(*arrays)


def core_swap(value):
    return lax.ppermute(value, "core", [(0, 1), (1, 0)])


def core_order(core, mine, other, axis):
    return jnp.concatenate(
        [jnp.where(core == 0, mine, other), jnp.where(core == 0, other, mine)], axis=axis
    )


def flat_rows(parts, rows):
    flat = jnp.concatenate([p.reshape(-1) for p in parts])
    return jnp.pad(flat, (0, rows * 128 - flat.shape[0])).reshape(rows, 128)


def norm_back(vector, gain, grad):
    scale = lax.rsqrt(jnp.mean(vector * vector, axis=-1, keepdims=True) + norm_eps)
    unit = vector * scale
    pulled = grad * gain
    back = scale * (pulled - unit * jnp.mean(pulled * unit, axis=-1, keepdims=True))
    return back, jnp.sum(unit * grad, axis=0)


def norm_apply(vector, gain):
    scale = lax.rsqrt(jnp.mean(vector * vector, axis=-1, keepdims=True) + norm_eps)
    return vector * scale * gain


def adamw_step(weight, gradient, mean_old, square_old, rate, decay):
    drift = beta_first * mean_old + (1.0 - beta_first) * gradient
    spread = beta_second * square_old + (1.0 - beta_second) * gradient * gradient
    mean_hat = drift / (1.0 - beta_first**STEP)
    square_hat = spread / (1.0 - beta_second**STEP)
    master = weight - rate * (mean_hat / (jnp.sqrt(square_hat) + adam_eps) + decay * weight)
    return (drift, spread, master)


def rotate(vector, cosine, sine):
    first, second = vector[..., : HD // 2], vector[..., HD // 2 :]
    return jnp.concatenate(
        [first * cosine - second * sine, second * cosine + first * sine], axis=-1
    )


def on_device(
    activations,
    cotangent,
    seq_lengths,
    deal_order,
    routes,
    entry_weight,
    entry_mean,
    entry_square,
    exit_weight,
    exit_mean,
    exit_square,
    router_weight,
    router_mean,
    router_square,
    expand_weight,
    expand_mean,
    expand_square,
    shrink_weight,
    shrink_mean,
    shrink_square,
    norm_gains,
    gains_mean,
    gains_square,
):
    seq = lax.axis_index("seq")
    core = lax.axis_index("core")

    def to_core(weight):
        weight = weight.astype(bf16)
        mine = lax.dynamic_slice_in_dim(weight, core * LOCAL_E, LOCAL_E, 0)
        other = lax.dynamic_slice_in_dim(weight, (1 - core) * LOCAL_E, LOCAL_E, 0)
        return core_order(core, mine, core_swap(other), 1)

    expand_part, shrink_part = to_core(expand_weight), to_core(shrink_weight)

    entry_b = entry_weight.astype(bf16)
    entry_cols = jnp.concatenate(
        [
            entry_b[:, : QH * HD].reshape(ROWS, N_SEQ, Q_OWN),
            entry_b[:, QH * HD :].reshape(ROWS, N_SEQ, KV_OWN),
        ],
        axis=2,
    ).transpose(1, 0, 2)
    expert_ids = jnp.arange(EXPERTS, dtype=jnp.int32)
    hit_slots = jnp.any(routes[0][:, :, None] == expert_ids[None, None, :], axis=1).astype(bf16)
    shared = jnp.concatenate(
        [
            router_weight.astype(bf16).reshape(-1),
            norm_gains.astype(bf16).reshape(-1),
            hit_slots.reshape(-1),
        ]
    )
    payload = jnp.concatenate(
        [
            entry_cols.reshape(N_SEQ, -1),
            jnp.broadcast_to(shared[None], (N_SEQ,) + shared.shape),
        ],
        axis=1,
    )
    payload = jnp.pad(payload, ((0, 0), (0, 112 * 128 - payload.shape[1])))
    in_all, cot_all, small = z_exchange(
        1, gathered=(activations[0], cotangent[0]), scattered=(payload.reshape(N_SEQ, 112, 128),)
    )
    in_all = in_all.reshape(GROUP, D)
    cot_all = cot_all.reshape(GROUP, D)
    small = small.reshape(N_SEQ, 112 * 128)
    n_entry, n_router, n_gain = ROWS * MIX_OWN, ROWS * EXPERTS, 2 * ROWS
    hit_base = n_entry + n_router + n_gain
    hit_slot_all = small[:, hit_base : hit_base + TOK_DEV * EXPERTS].reshape(GROUP, EXPERTS)
    packed = flat_rows([small[:, :hit_base], exit_weight.astype(bf16)], 400)
    full = lax.all_gather(packed, FSDP, axis=0, tiled=False).reshape(32, 400 * 128)
    n_small = N_SEQ * hit_base
    from_z = full[:, :n_small].reshape(32, N_SEQ, hit_base).transpose(1, 0, 2)
    entry_own = from_z[:, :, :n_entry].reshape(D, MIX_OWN)
    router_full = from_z[:, :, n_entry : n_entry + n_router].reshape(D, EXPERTS)
    gains_full = (
        from_z[:, :, n_entry + n_router :]
        .reshape(N_SEQ, 32, 2, ROWS)
        .transpose(2, 0, 1, 3)
        .reshape(2, D)
        .astype(f32)
    )
    exit_own = full[:, n_small : n_small + ROWS * D].reshape(Q_OWN, D)

    expand_full = lax.all_gather(expand_part, PLANE, axis=1, tiled=True)
    shrink_full = lax.all_gather(shrink_part, PLANE, axis=1, tiled=True)

    order_row = deal_order[0]
    token = jnp.arange(GROUP, dtype=jnp.int32)
    back_hot = (order_row[None, :] == token[:, None]).astype(bf16)
    hit = dot(back_hot, hit_slot_all, ((1,), (0,)))
    seq_ends = jnp.cumsum(seq_lengths[0])
    starts = seq_ends - seq_lengths[0]
    seq_ids = jnp.sum((token[:, None] >= seq_ends[None, :]).astype(jnp.int32), axis=1)
    seq_match = seq_ids[:, None] == jnp.arange(seq_ends.shape[0], dtype=jnp.int32)[None, :]
    positions = token - jnp.sum(jnp.where(seq_match, starts[None, :], 0), axis=1)
    frequency = rope_base ** (-jnp.arange(HD // 2, dtype=f32) * 2.0 / HD)
    phase = positions.astype(f32)[:, None] * frequency[None, :]
    cosine, sine = jnp.cos(phase)[:, None, :], jnp.sin(phase)[:, None, :]
    allowed = (seq_ids[:, None] == seq_ids[None, :]) & (token[None, :] <= token[:, None])

    normed = norm_apply(in_all.astype(f32), gains_full[0]).astype(bf16)
    mixed = dot(normed, entry_own, ((1,), (0,)))
    queries = rotate(mixed[:, :Q_OWN].reshape(GROUP, HEADS_OWN, HD), cosine, sine)
    pairs = mixed[:, Q_OWN:].reshape(GROUP, KV_HEADS_OWN, 2, HD)
    keys = rotate(pairs[:, :, 0], cosine, sine)
    queries = queries.astype(bf16).reshape(GROUP, KV_HEADS_OWN, PER_KV, HD)
    keys, values = keys.astype(bf16), pairs[:, :, 1].astype(bf16)
    scores = jnp.einsum("qhgd,khd->hgqk", queries, keys, preferred_element_type=f32) * HD**-0.5
    scores = jnp.where(allowed[None, None], scores, -1e30)
    peak = jnp.max(scores, axis=-1, keepdims=True)
    expo = jnp.exp(scores - peak)
    probs = expo / jnp.sum(expo, axis=-1, keepdims=True)
    probs_b = probs.astype(bf16)
    attended = (
        jnp.einsum("hgqk,khd->qhgd", probs_b, values, preferred_element_type=f32)
        .reshape(GROUP, Q_OWN)
        .astype(bf16)
    )
    branch_part = dot(attended, exit_own, ((1,), (0,))).astype(bf16)
    (branch,) = z_exchange(2, scattered=(branch_part.reshape(N_SEQ, TOK_DEV, D),))
    middle = activations[0].astype(f32) + jnp.sum(branch.astype(f32), axis=0)
    normed_two = norm_apply(middle, gains_full[1]).astype(bf16)
    (two_all,) = z_exchange(3, gathered=(normed_two,))
    two_all = two_all.reshape(GROUP, D)

    tokens = core_order(core, two_all, core_swap(two_all), 0)
    cots = core_order(core, cot_all, core_swap(cot_all), 0)
    hits = core_order(core, hit, core_swap(hit), 0)

    logits = dot(tokens, router_full, ((1,), (0,)))
    masked = jnp.where(hits > 0, logits, -jnp.inf)
    gate_expo = jnp.exp(masked - jnp.max(masked, axis=1, keepdims=True))
    gates = gate_expo / jnp.sum(gate_expo, axis=1, keepdims=True)
    first = (seq * 2 + core) * LOCAL_E
    own_hits = lax.dynamic_slice_in_dim(hits, first, LOCAL_E, 1)
    own_gates = lax.dynamic_slice_in_dim(gates, first, LOCAL_E, 1).T
    rank = jnp.cumsum(own_hits.astype(jnp.int32), axis=0) - 1
    rank = jnp.where(own_hits > 0, rank, -1).T
    pick = rank[:, None, :] == jnp.arange(SLOTS, dtype=jnp.int32)[None, :, None]
    row_gates = jnp.sum(jnp.where(pick, own_gates[:, None, :], 0.0), axis=2, keepdims=True)
    pick = pick.astype(bf16)

    rows = jnp.einsum("est,td->esd", pick, tokens, preferred_element_type=bf16)
    cot_rows = jnp.einsum("est,td->esd", pick, cots, preferred_element_type=f32)
    grad_rows = (row_gates * cot_rows).astype(bf16)
    gate_up = jnp.einsum("esd,edf->esf", rows, expand_full, preferred_element_type=f32)
    gate_pre, up_part = gate_up[..., :FF], gate_up[..., FF:]
    gate_sig = jax.nn.sigmoid(gate_pre)
    hidden = (gate_pre * gate_sig * up_part).astype(bf16)
    shrink_grad = jnp.einsum("esf,esd->efd", hidden, grad_rows, preferred_element_type=f32)
    shrink_sum = lax.psum_scatter(shrink_grad.astype(bf16), PLANE, scatter_dimension=1, tiled=True)
    hidden_grad = jnp.einsum("esd,efd->esf", grad_rows, shrink_full, preferred_element_type=f32)
    up_grad = jnp.concatenate(
        [
            hidden_grad * up_part * gate_sig * (1.0 + gate_pre * (1.0 - gate_sig)),
            hidden_grad * gate_pre * gate_sig,
        ],
        axis=-1,
    ).astype(bf16)
    expand_grad = jnp.einsum("esd,esf->edf", rows, up_grad, preferred_element_type=f32)
    expand_sum = lax.psum_scatter(expand_grad.astype(bf16), PLANE, scatter_dimension=1, tiled=True)
    row_grad = jnp.einsum("esf,edf->esd", up_grad, expand_full, preferred_element_type=f32)
    back_part = jnp.einsum(
        "est,esd->td", pick, row_grad.astype(bf16), preferred_element_type=f32
    )
    expert_out = jnp.einsum(
        "esf,efd->esd", hidden, shrink_full, preferred_element_type=f32
    ).astype(bf16).astype(f32)
    row_gate_grad = jnp.sum(expert_out * cot_rows, axis=2)
    gate_grad_part = jnp.einsum("est,es->te", pick.astype(f32), row_gate_grad, precision="highest")
    out_part = jnp.einsum(
        "est,esd->td", pick, (row_gates * expert_out).astype(bf16), preferred_element_type=f32
    )

    def core_sum(part):
        mine = lax.dynamic_slice_in_dim(part, core * GROUP, GROUP, 0)
        other = lax.dynamic_slice_in_dim(part, (1 - core) * GROUP, GROUP, 0)
        return mine + core_swap(other.astype(bf16)).astype(f32)

    back_send = core_sum(back_part).astype(bf16).reshape(N_SEQ, TOK_DEV, D)
    out_send = core_sum(out_part).astype(bf16).reshape(N_SEQ, TOK_DEV, D)
    gg_mine = lax.dynamic_slice_in_dim(gate_grad_part, core * GROUP, GROUP, 0)
    gg_other = core_swap(lax.dynamic_slice_in_dim(gate_grad_part, (1 - core) * GROUP, GROUP, 0))
    gg_send = core_order(core, gg_mine, gg_other, 1)
    gg_send = jnp.pad(gg_send, ((0, 0), (0, 128 - 2 * LOCAL_E))).reshape(N_SEQ, TOK_DEV, 128)
    back_got, gg_got = z_exchange(4, scattered=(back_send, gg_send))
    normed_two_grad = jnp.sum(back_got.astype(f32), axis=0)
    gate_grad = gg_got[:, :, : 2 * LOCAL_E].transpose(1, 0, 2).reshape(TOK_DEV, EXPERTS)
    my_gates = lax.dynamic_slice_in_dim(gates, core * GROUP + seq * TOK_DEV, TOK_DEV, 0)
    mean_term = jnp.sum(my_gates * gate_grad, axis=1, keepdims=True)
    logit_grad = (my_gates * (gate_grad - mean_term)).astype(bf16)
    router_grad = dot(normed_two, logit_grad, ((0,), (0,)))
    normed_two_grad = normed_two_grad + dot(logit_grad, router_full, ((1,), (1,)))
    middle_back, gain_two_grad = norm_back(middle, gains_full[1], normed_two_grad)
    middle_grad = cotangent[0].astype(f32) + middle_back
    (branch_grad,) = z_exchange(5, gathered=(middle_grad.astype(bf16),))
    branch_grad = branch_grad.reshape(GROUP, D)
    exit_grad = dot(attended, branch_grad, ((0,), (0,)))
    attended_grad = dot(branch_grad, exit_own, ((1,), (1,))).astype(bf16)
    attended_grad = attended_grad.reshape(GROUP, KV_HEADS_OWN, PER_KV, HD)
    prob_grad = jnp.einsum("qhgd,khd->hgqk", attended_grad, values, preferred_element_type=f32)
    delta = jnp.sum(probs * prob_grad, axis=-1, keepdims=True)
    score_grad = (probs * (prob_grad - delta) * HD**-0.5).astype(bf16)
    query_grad = jnp.einsum("hgqk,khd->qhgd", score_grad, keys, preferred_element_type=f32)
    key_grad = jnp.einsum("hgqk,qhgd->khd", score_grad, queries, preferred_element_type=f32)
    value_grad = jnp.einsum("hgqk,qhgd->khd", probs_b, attended_grad, preferred_element_type=f32)
    query_grad = rotate(query_grad.reshape(GROUP, HEADS_OWN, HD), cosine, -sine)
    key_grad = rotate(key_grad, cosine, -sine)
    mixed_grad = jnp.concatenate(
        [
            query_grad.reshape(GROUP, Q_OWN),
            jnp.stack([key_grad, value_grad], axis=2).reshape(GROUP, KV_OWN),
        ],
        axis=1,
    ).astype(bf16)
    entry_grad = dot(normed, mixed_grad, ((0,), (0,))).astype(bf16)
    normed_part = dot(mixed_grad, entry_own, ((1,), (1,))).astype(bf16)
    (normed_got,) = z_exchange(6, scattered=(normed_part.reshape(N_SEQ, TOK_DEV, D),))
    (out_got,) = z_exchange(7, scattered=(out_send,))
    block_output = (middle + jnp.sum(out_got.astype(f32), axis=0)).astype(bf16)
    normed_grad = jnp.sum(normed_got.astype(f32), axis=0)
    dealt_back, gain_one_grad = norm_back(activations[0].astype(f32), gains_full[0], normed_grad)
    input_grad = (middle_grad + dealt_back).astype(bf16)

    gains_grad = jnp.stack([gain_one_grad, gain_two_grad])
    z_small = jnp.concatenate(
        [
            router_grad.reshape(N_SEQ, -1),
            gains_grad.reshape(2, N_SEQ, -1).transpose(1, 0, 2).reshape(N_SEQ, -1),
        ],
        axis=1,
    )
    z_small = jnp.pad(z_small, ((0, 0), (0, 128 * 128 - z_small.shape[1])))
    (z_small,) = z_exchange(8, scattered=(z_small.reshape(N_SEQ, 128, 128),))
    z_small = jnp.sum(z_small, axis=0).reshape(-1)
    router_part = z_small[: Q_OWN * EXPERTS].reshape(32, -1)
    gains_part = (
        z_small[Q_OWN * EXPERTS : Q_OWN * (EXPERTS + 2)]
        .reshape(2, 32, ROWS)
        .transpose(1, 0, 2)
        .reshape(32, -1)
    )
    owed = jnp.concatenate(
        [
            entry_grad.reshape(N_SEQ, 32, ROWS * MIX_OWN).transpose(1, 0, 2).reshape(32, -1),
            exit_grad.astype(bf16).reshape(32, -1),
            router_part.astype(bf16),
            gains_part.astype(bf16),
        ],
        axis=1,
    )
    owed = jnp.pad(owed, ((0, 0), (0, 400 * 128 - owed.shape[1])))
    summed = lax.psum_scatter(
        owed.reshape(32 * 400, 128), FSDP, scatter_dimension=0, tiled=True
    ).reshape(-1)
    entry_cols = summed[: N_SEQ * n_entry].reshape(N_SEQ, ROWS * MIX_OWN // 128, 128)
    entry_cols = jnp.pad(entry_cols, ((0, 0), (0, 4), (0, 0)))
    (entry_cols,) = z_exchange(9, scattered=(entry_cols,))
    entry_cols = entry_cols[:, :60].reshape(N_SEQ, ROWS, MIX_OWN).transpose(1, 0, 2).astype(f32)
    entry_sum = jnp.concatenate(
        [
            entry_cols[:, :, :Q_OWN].reshape(ROWS, QH * HD),
            entry_cols[:, :, Q_OWN:].reshape(ROWS, 2 * KVH * HD),
        ],
        axis=1,
    )
    base = N_SEQ * n_entry
    exit_sum = summed[base : base + ROWS * D].reshape(ROWS, D).astype(f32)
    base += ROWS * D
    router_sum = summed[base : base + n_router].reshape(ROWS, EXPERTS).astype(f32)
    base += n_router
    gains_sum = summed[base : base + n_gain].reshape(2, ROWS).astype(f32)

    def to_owner(summed, rows):
        mine = lax.dynamic_slice_in_dim(summed, core * rows, rows, 1)
        other = lax.dynamic_slice_in_dim(summed, (1 - core) * rows, rows, 1)
        return core_order(core, mine, core_swap(other), 0).astype(f32)

    expand_sum = to_owner(expand_sum, 48)
    shrink_sum = to_owner(shrink_sum, 16)
    entry_new = adamw_step(entry_weight, entry_sum, entry_mean, entry_square, 0.02, weight_decay)
    exit_new = adamw_step(exit_weight, exit_sum, exit_mean, exit_square, 0.15, weight_decay)
    router_new = adamw_step(
        router_weight, router_sum, router_mean, router_square, 0.01, weight_decay
    )
    expand_new = adamw_step(
        expand_weight, expand_sum, expand_mean, expand_square, 0.02, weight_decay
    )
    shrink_new = adamw_step(
        shrink_weight, shrink_sum, shrink_mean, shrink_square, 0.12, weight_decay
    )
    gains_new = adamw_step(norm_gains, gains_sum, gains_mean, gains_square, 0.5, 0.0)
    return (
        block_output[None],
        input_grad[None],
        *entry_new,
        *exit_new,
        *router_new,
        *expand_new,
        *shrink_new,
        *gains_new,
    )


def solution(mesh):
    fine = Mesh(mesh.devices.reshape(4, 4, 4, 2), ("seq", "x", "y", "core"))
    rows = P(FSDP, "seq", None)
    lists = P(FSDP, None)
    owned = P(("seq",) + FSDP, None)
    experts = P("seq", FSDP, None)
    gains = P(None, ("seq",) + FSDP)
    return jax.shard_map(
        on_device,
        mesh=fine,
        in_specs=(rows, rows, lists, lists, rows)
        + (owned,) * 9
        + (experts,) * 6
        + (gains,) * 3,
        out_specs=(rows, rows) + (owned,) * 9 + (experts,) * 6 + (gains,) * 3,
        check_vma=False,
    )
```

time: 1850 us -> 792 us (0.43)
  blocking collectives: 644 us -> 0 us
  starting transfers between devices: 301 us -> 13.9 us
  Pallas kernels: 0 us -> 177 us
  local copies, waits for them, and re-layouts: 267 us -> 101 us
  waiting for transfers between devices: 401 us -> 267 us
    unnamed x2 -> x0, blocking collectives: 479 us -> none
    unnamed x96 -> x0, starting transfers between devices: 267 us -> none
    pallas_call x0 -> x9, Pallas kernels: none -> 177 us  [z_exchange(): pl.pallas_call(kernel, out_shape=shapes, in_specs=[pl.BlockSpec(memory_sp...]
    all_gather x10 -> x3, waiting for transfers between devices: 208 us -> 71.8 us  [the longest x1 36.9 us: on_device(): shrink_full = lax.all_gather(shrink_part, PLANE, axis=1, tiled=True)]
    unnamed x319 -> x149, local copies, waits for them, and re-layouts: 142 us -> 19.9 us
    all_to_all x2 -> x0, blocking collectives: 96.5 us -> none  [the longest x1 48.4 us: on_device(): lax.all_to_all(send_rows.reshape(seq_count, local_experts, CAP, D), 'seq'...]
    reduce_scatter x2 -> x3, waiting for transfers between devices: 108 us -> 188 us  [the longest x1 103 us: on_device(): lax.psum_scatter(expand_grad.astype(bf16), PLANE, scatter_dimension=1, ti...]
    all_gather x2 -> x0, blocking collectives: 68.3 us -> none  [the longest x1 34.4 us: on_device(): lax.all_gather(norm_gains.astype(jnp.bfloat16), ('seq', 'fsdp'), axis=1,...]
  transfers between devices with their start and end apart: 116 -> 16, of which waited for: 15 -> 9; matrix products, arithmetic and copies ran while one was open for 46% -> 21% of each run, Pallas kernels for 0% -> 9%
where the time goes in v1:
time: 792 us; the launch traced here: 786 us
  waiting for transfers between devices  267 us (34%)
  Pallas kernels  177 us (22%)
  matrix products  145 us (18%)
  local copies, waits for them, and re-layouts  101 us (13%)
  other arithmetic  65.9 us (8%)
  between operations  15.6 us (2%)
  starting transfers between devices  13.9 us (2%)
    pallas_call x9, Pallas kernels, z_exchange(): pl.pallas_call(kernel, out_shape=shapes, in_specs=[pl.BlockSpec(memory_sp...  177 us
    reduce_scatter x1, waiting for transfers between devices, on_device(): lax.psum_scatter(expand_grad.astype(bf16), PLANE, scatter_dimension=1, ti...  103 us
    reduce_scatter x1, waiting for transfers between devices, on_device(): lax.psum_scatter(shrink_grad.astype(bf16), PLANE, scatter_dimension=1, ti...  69.8 us
    all_gather x1, waiting for transfers between devices, on_device(): shrink_full = lax.all_gather(shrink_part, PLANE, axis=1, tiled=True)  36.9 us
    all_gather x1, waiting for transfers between devices, on_device(): lax.all_gather(packed, FSDP, axis=0, tiled=False).reshape(32, 400 * 128)  34.9 us
    unnamed x149, local copies, waits for them, and re-layouts  19.9 us
    dot_general x10, matrix products, dot(): return lax.dot_general(a, b, (dims, ((), ())), preferred_element_type=f32)  17.9 us
  transfers between devices with their start and end apart: 16, of which 9 were waited for; matrix products, arithmetic and copies ran while one was open for 21% of the time, Pallas kernels for 9%

profile of v1, /device:TPU:1, one launch (start us, length us, event | category | flops | bytes accessed | tf_op | source)
XLA Modules:
  0.0 785.7 jit_solution(15752407008280351655)
XLA Ops:
  12.8 41.3 %shard_map.374 = (bf16[4,128,1536]{2,1,0:T(8,128)(2,1)}, bf16[4,128,1536]{2,1,0:T(8,128)(2,1)}, bf16[4,112,128]{2,1,0:T(8,128)(2,1)}) custom-call(bf16[128,1536]{1,0:T(8,128)(2,1)} %bitcast.283, bf16[128,1536]{1,0:T(8,128)(2,1)} %bitcast.292, bf16[4,112,128]{2,1,0:T(8,128)(2,1)} %bitcast.308), custom_call_target="tpu_custom_call" | custom-call | tf_op jit(solution)/shard_map/pallas_call | solution.py:92
  68.2 34.9 %all-gather.4.cloned.1.call-done = bf16[32,400,128]{2,1,0:T(8,128)(2,1)} async-done(((bf16[1,400,128]{2,1,0:T(8,128)(2,1)}), bf16[32,400,128]{2,1,0:T(8,128)(2,1)}) %all-gather.4.cloned.1.call-update) | async-done | bytes 3276816 | tf_op jit(solution)/shard_map/all_gather | solution.py:221
  108.8 8.1 %copy.180 = bf16[32,32736]{0,1:T(8,128)(2,1)} copy(bf16[32,32736]{1,0:T(8,128)(2,1)} %slice.162) | data formatting | bytes 4190208 | tf_op jit(solution)/shard_map/reshape | solution.py:223
  116.9 6.9 slice.165
  124.8 7.7 copy.149
  132.5 4.9 reshape.444
  147.8 6.0 fusion.129
  160.5 21.6 %shard_map.375 = bf16[4,128,1536]{2,1,0:T(8,128)(2,1)} custom-call(bf16[4,128,1536]{2,1,0:T(8,128)(2,1)} %bitcast.289), custom_call_target="tpu_custom_call" | custom-call | tf_op jit(solution)/shard_map/pallas_call | solution.py:92
  185.0 19.8 %shard_map.376 = bf16[4,128,1536]{2,1,0:T(8,128)(2,1)} custom-call(bf16[128,1536]{1,0:T(8,128)(2,1)} %multiply_convert_fusion.7.refs_0_), custom_call_target="tpu_custom_call" | custom-call | tf_op jit(solution)/shard_map/pallas_call | solution.py:92
  219.7 5.5 fusion.11
  225.2 6.0 fusion.9
  231.2 13.0 %fusion.132 = f32[5,240,1024]{2,1,0:T(8,128)} fusion(bf16[5,240,1536]{2,1,0:T(8,128)(2,1)} %fusion.11, bf16[5,1536,1024]{2,1,0:T(8,128)(2,1)} %all-gather.6.cloned.1.call-done), kind=kOutput, calls=%fused_computation.268 | convolution fusion | flops 3774873600 | bytes 24330240 | tf_op jit(solution)/shard_map/esd,edf->esf/dot_general | solution.py:297
  244.2 36.9 %all-gather.8.cloned.1.call-done = bf16[5,512,1536]{2,1,0:T(8,128)(2,1)} async-done(((bf16[5,32,1536]{2,1,0:T(8,128)(2,1)}), bf16[5,512,1536]{2,1,0:T(8,128)(2,1)}) %all-gather.8.cloned.1.call-update) | async-done | bytes 7864336 | tf_op jit(solution)/shard_map/all_gather | solution.py:236
  281.1 11.9 %multiply_convert_fusion.3 = (bf16[5,240,512]{2,1,0:T(8,128)(2,1)}, bf16[5,240,512]{2,1,0:T(8,128)(2,1)}, bf16[5,240,512]{2,1,0:T(8,128)(2,1)}) fusion(f32[5,240,1024]{2,1,0:T(8,128)} %fusion.132, bf16[5,512,1536]{2,1,0:T(8,128)(2,1)} %all-gather.8.cloned.1.call-done, f32[5,240,1536]{2,1,0:T(8,128)} %fusion.9, f32[5,240]{1,0:T(8,128)S(1)} %select_reduce_fusion), kind=kOutput, calls=%fused_computation.64 | convolution fusion | flops 1900953600 | bytes 23843520 | tf_op jit(solution)/shard_map/esd,efd->esf/dot_general | solution.py:303
  293.0 14.4 %fusion.14 = f32[1024,1536]{1,0:T(8,128)} fusion(bf16[5,1536,1024]{2,1,0:T(8,128)(2,1)} %all-gather.6.cloned.1.call-done, s32[5,1024]{1,0:T(8,128)S(1)} %copy-done.41, bf16[5,240,512]{2,1,0:T(8,128)(2,1)} %get-tuple-element.54, bf16[5,240,512]{2,1,0:T(8,128)(2,1)} %get-tuple-element.53), kind=kOutput, calls=%fused_computation.25 | convolution fusion | flops 7557734400 | bytes 24498176 | tf_op jit(solution)/shard_map/est,esd->td/dot_general | solution.py:314
  311.5 9.2 %fusion.3 = (f32[5,240]{1,0:T(8,128)S(1)}, bf16[5,240,1536]{2,1,0:T(8,128)(2,1)}) fusion(f32[5,240,1536]{2,1,0:T(8,128)} %fusion.9, bf16[5,240,512]{2,1,0:T(8,128)(2,1)S(1)} %copy-done.8, bf16[5,512,1536]{2,1,0:T(8,128)(2,1)} %all-gather.8.cloned.1.call-done), kind=kOutput, calls=%fused_computation.6 | convolution fusion | flops 1894808448 | bytes 20157120 | tf_op jit(solution)/shard_map/esf,efd->esd/dot_general | solution.py:317
  328.9 24.0 %shard_map.378 = (bf16[4,128,1536]{2,1,0:T(8,128)(2,1)}, f32[4,128,128]{2,1,0:T(8,128)}) custom-call(bf16[4,128,1536]{2,1,0:T(8,128)(2,1)} %bitcast.290, f32[4,128,128]{2,1,0:T(8,128)} %bitcast.303), custom_call_target="tpu_custom_call" | custom-call | tf_op jit(solution)/shard_map/pallas_call | solution.py:92
  360.9 19.3 %shard_map.379 = bf16[4,128,1536]{2,1,0:T(8,128)(2,1)} custom-call(bf16[128,1536]{1,0:T(8,128)(2,1)} %fusion.119.refs_0_), custom_call_target="tpu_custom_call" | custom-call | tf_op jit(solution)/shard_map/pallas_call | solution.py:92
  392.7 10.5 %fusion.47 = f32[512,2,64]{0,2,1:T(8,128)} fusion(f32[2,512,512,3]{2,1,3,0:T(8,128)} %fusion.87, bf16[512,2,3,32]{0,3,2,1:T(8,128)(2,1)S(1)} %bitcast.327, bf16[512,2,3,32]{0,3,2,1:T(8,128)(2,1)S(1)} %bitcast.325, f32[2,3,512,512]{2,3,1,0:T(8,128)} %get-tuple-element.88, f32[2,3,512]{2,1,0:T(4,128)S(1)} %copy-done.65), kind=kOutput, calls=%fused_computation.93 | convolution fusion | flops 213126656 | bytes 13250560 | tf_op jit(solution)/shard_map/hgqk,qhgd->khd/dot_general | solution.py:356
  403.2 11.7 %fusion.27 = f32[2,64,3,512]{3,1,2,0:T(8,128)} fusion(f32[2,512,512,3]{2,1,3,0:T(8,128)} %fusion.87, bf16[512,2,32]{0,2,1:T(8,128)(2,1)S(1)} %copy-done.45, bf16[512,2,32]{0,2,1:T(8,128)(2,1)S(1)} %copy-done.44, f32[2,3,512,512]{2,3,1,0:T(8,128)} %get-tuple-element.88, f32[2,3,512]{2,1,0:T(4,128)S(1)} %copy-done.65), kind=kOutput, calls=%fused_computation.59 | convolution fusion | flops 212602368 | bytes 13512704 | tf_op jit(solution)/shard_map/hgqk,khd->qhgd/dot_general | solution.py:355
  423.5 18.5 %shard_map.380 = bf16[4,128,1536]{2,1,0:T(8,128)(2,1)} custom-call(bf16[4,128,1536]{2,1,0:T(8,128)(2,1)} %bitcast.299), custom_call_target="tpu_custom_call" | custom-call | tf_op jit(solution)/shard_map/pallas_call | solution.py:92
  447.3 5.7 shard_map.381
  483.7 5.0 reshape.473
  489.9 8.5 %convolution_convert_fusion.1 = bf16[5,512,1536]{2,1,0:T(8,128)(2,1)} fusion(bf16[5,240,512]{2,1,0:T(8,128)(2,1)S(1)} %copy-done.9, f32[5,240,1536]{2,1,0:T(8,128)} %fusion.9, f32[5,240]{1,0:T(8,128)S(1)} %copy-done.47), kind=kOutput, calls=%fused_computation.15 | convolution fusion | flops 1895055360 | bytes 16470720 | tf_op jit(solution)/shard_map/esf,esd->efd/dot_general | solution.py:301
  499.7 10.2 %convolution_convert_fusion = bf16[5,1536,1024]{2,1,0:T(8,128)(2,1)} fusion(bf16[5,240,1536]{2,1,0:T(8,128)(2,1)} %fusion.11, bf16[5,240,512]{2,1,0:T(8,128)(2,1)} %get-tuple-element.54, bf16[5,240,512]{2,1,0:T(8,128)(2,1)S(1)} %copy-done.27), kind=kOutput, calls=%fused_computation.2 | convolution fusion | flops 3787653120 | bytes 21872640 | tf_op jit(solution)/shard_map/esd,esf->edf/dot_general | solution.py:311
  510.7 6.6 fusion.13
  521.2 4.7 collective-permute-start.4
  532.7 20.7 %shard_map.377 = bf16[4,128,1536]{2,1,0:T(8,128)(2,1)} custom-call(bf16[4,128,1536]{2,1,0:T(8,128)(2,1)} %bitcast.291), custom_call_target="tpu_custom_call" | custom-call | tf_op jit(solution)/shard_map/pallas_call | solution.py:92
  557.5 14.6 %reduce-scatter.4.cloned.1.call-done = bf16[400,128]{1,0:T(8,128)(2,1)} async-done(((bf16[12800,128]{1,0:T(8,128)(2,1)}), bf16[400,128]{1,0:T(8,128)(2,1)}) %reduce-scatter.4.cloned.1.call-update) | async-done | bytes 102416 | tf_op jit(solution)/shard_map/reduce_scatter | solution.py:404
  573.5 5.5 shard_map.382
  589.1 69.8 %reduce-scatter.8.cloned.1.call-done = bf16[5,32,1536]{2,1,0:T(8,128)(2,1)} async-done(((bf16[5,512,1536]{2,1,0:T(8,128)(2,1)}), bf16[5,32,1536]{2,1,0:T(8,128)(2,1)}) %reduce-scatter.8.cloned.1.call-update) | async-done | bytes 491536 | tf_op jit(solution)/shard_map/reduce_scatter | solution.py:302
  665.3 103.5 %reduce-scatter.6.cloned.1.call-done = bf16[5,96,1024]{2,1,0:T(8,128)(2,1)} async-done(((bf16[5,1536,1024]{2,1,0:T(8,128)(2,1)}), bf16[5,96,1024]{2,1,0:T(8,128)(2,1)}) %reduce-scatter.6.cloned.1.call-update) | async-done | bytes 983056 | tf_op jit(solution)/shard_map/reduce_scatter | solution.py:312
  (348 shorter events, 183.1 us)
Async XLA Ops:
  7.2 48.9 %copy-start.2 = (f32[10,48,1024]{2,1,0:T(8,128)S(1)}, f32[10,48,1024]{2,1,0:T(8,128)}, u32[]{:S(2)}) copy-start(f32[10,48,1024]{2,1,0:T(8,128)} %param.37) | copy-start | bytes 5898244
  7.2 96.0 %all-gather.4.cloned.1.call-start = ((), (), s32[]{:S(2)}) async-start(), calls=%async_computation.3 | async-start | bytes 3379200 | tf_op jit(solution)/shard_map/all_gather | solution.py:221
  56.1 175.2 %all-gather.6.cloned.1.call-start = ((), (), s32[]{:S(2)}) async-start(), calls=%async_computation.4 | async-start | bytes 16711680 | tf_op jit(solution)/shard_map/all_gather | solution.py:235
  56.3 3.1 collective-permute-start.2
  60.6 220.5 %all-gather.8.cloned.1.call-start = ((), (), s32[]{:S(2)}) async-start(), calls=%async_computation.5 | async-start | bytes 8355840 | tf_op jit(solution)/shard_map/all_gather | solution.py:236
  62.0 1.6 collective-permute-start.3
  64.5 507.5 %reduce-scatter.4.cloned.1.call-start = ((), (), s32[]{:S(2)}) async-start(), calls=%async_computation.6 | async-start | bytes 3379200 | tf_op jit(solution)/shard_map/reduce_scatter | solution.py:404
  64.6 149.9 %collective-permute-start.5 = (bf16[512,1536]{1,0:T(8,128)(2,1)}, bf16[512,1536]{1,0:T(8,128)(2,1)}, u32[]{:S(2)}, u32[]{:S(2)}) collective-permute-start(bf16[512,1536]{1,0:T(8,128)(2,1)} %bitcast.298), channel_id=1, source_target_pairs={{0,1},{1,0},{2,3},{3,2},{4,5},{5,4},{6,7},{7,6},{8,9},{9,8},{10,11... | collective-permute-start | bytes 4718600 | tf_op jit(solution)/shard_map/ppermute | solution.py:107
  67.3 80.3 %copy-start.23 = (f32[512,32]{0,1:T(8,128)}, f32[512,32]{0,1:T(8,128)S(1)}, u32[]{:S(2)}) copy-start(f32[512,32]{0,1:T(8,128)S(1)} %get-tuple-element.84) | copy-start | bytes 196612
  160.5 23.4 %copy-start = (bf16[1,128,1536]{2,1,0:T(8,128)(2,1)S(1)}, bf16[1,128,1536]{2,1,0:T(8,128)(2,1)}, u32[]{:S(2)}) copy-start(bf16[1,128,1536]{2,1,0:T(8,128)(2,1)} %param.23) | copy-start | bytes 1179652
  182.1 25.9 %copy-start.62 = (s32[1,512]{1,0:T(1,128)S(1)}, s32[1,512]{1,0:T(1,128)}, u32[]{:S(2)}) copy-start(s32[1,512]{1,0:T(1,128)} %param.26) | copy-start | bytes 6148
  204.8 9.7 %collective-permute-start.1 = (bf16[512,1536]{1,0:T(8,128)(2,1)}, bf16[512,1536]{1,0:T(8,128)(2,1)}, u32[]{:S(2)}, u32[]{:S(2)}) collective-permute-start(bf16[512,1536]{1,0:T(8,128)(2,1)} %bitcast.288), channel_id=1, source_target_pairs={{0,1},{1,0},{2,3},{3,2},{4,5},{5,4},{6,7},{7,6},{8,9},{9,8},{10,11... | collective-permute-start | bytes 4718600 | tf_op jit(solution)/shard_map/ppermute | solution.py:107
  208.4 1.7 collective-permute-start
  219.7 61.4 %copy-start.46 = (f32[5,240]{1,0:T(8,128)}, f32[5,240]{1,0:T(8,128)S(1)}, u32[]{:S(2)}) copy-start(f32[5,240]{1,0:T(8,128)S(1)} %select_reduce_fusion) | copy-start | bytes 14404
  310.8 14.1 %collective-permute-start.6 = (bf16[512,1536]{1,0:T(8,128)(2,1)}, bf16[512,1536]{1,0:T(8,128)(2,1)}, u32[]{:S(2)}, u32[]{:S(2)}) collective-permute-start(bf16[512,1536]{1,0:T(8,128)(2,1)} %dynamic-slice_convert_fusion), channel_id=1, source_target_pairs={{0,1},{1,0},{2,3},{3,2},{4,5},{5,4},{6,7},{7,6},{8,9},{9,8},{10,11... | collective-permute-start | bytes 4718600 | tf_op jit(solution)/shard_map/ppermute | solution.py:107
  322.3 1.7 collective-permute-start.7
  328.9 26.9 %copy-start.16 = (bf16[128,1536]{1,0:T(8,128)(2,1)S(1)}, bf16[128,1536]{1,0:T(8,128)(2,1)}, u32[]{:S(2)}) copy-start(bf16[128,1536]{1,0:T(8,128)(2,1)} %multiply_convert_fusion.7.refs_0_) | copy-start | bytes 1179652
  358.2 22.0 %copy-start.11 = (bf16[384,1536]{1,0:T(8,128)(2,1)S(1)}, bf16[384,1536]{1,0:T(8,128)(2,1)}, u32[]{:S(2)}) copy-start(bf16[384,1536]{1,0:T(8,128)(2,1)} %reshape.449) | copy-start | bytes 3538948
  423.5 22.0 %copy-start.50 = (f32[1,4,384]{2,0,1:T(1,128)S(1)}, f32[1,4,384]{2,0,1:T(1,128)}, u32[]{:S(2)}) copy-start(f32[1,4,384]{2,0,1:T(1,128)} %stack.25) | copy-start | bytes 18436
  488.7 170.2 %reduce-scatter.8.cloned.1.call-start = ((), (), s32[]{:S(2)}) async-start(), calls=%async_computation.8 | async-start | bytes 8355840 | tf_op jit(solution)/shard_map/reduce_scatter | solution.py:302
  498.5 270.3 %reduce-scatter.6.cloned.1.call-start = ((), (), s32[]{:S(2)}) async-start(), calls=%async_computation.7 | async-start | bytes 16711680 | tf_op jit(solution)/shard_map/reduce_scatter | solution.py:312
  521.2 8.0 %collective-permute-start.4 = (bf16[512,1536]{1,0:T(8,128)(2,1)}, bf16[512,1536]{1,0:T(8,128)(2,1)S(1)}, u32[]{:S(2)}, u32[]{:S(2)}) collective-permute-start(bf16[512,1536]{1,0:T(8,128)(2,1)} %dynamic-slice_convert_fusion.1), channel_id=1, source_target_pairs={{0,1},{1,0},{2,3},{3,2},{4,5},{5,4},{6,7},{7,6},{8,9},{9,8},{10,11... | collective-permute-start | bytes 4718600 | tf_op jit(solution)/shard_map/ppermute | solution.py:107
  532.7 22.6 %copy-start.60 = (f32[128]{0:T(128)S(1)}, f32[128]{0:T(128)}, u32[]{:S(2)}) copy-start(f32[128]{0:T(128)} %get-tuple-element.33) | copy-start | bytes 1540
  557.5 29.8 %copy-start.31 = (f32[12,2560]{1,0:T(8,128)S(1)}, f32[12,2560]{1,0:T(8,128)}, u32[]{:S(2)}) copy-start(f32[12,2560]{1,0:T(8,128)} %param.28) | copy-start | bytes 368644
  557.5 105.3 %copy-start.49 = (f32[12,40]{1,0:T(8,128)S(1)}, f32[12,40]{1,0:T(8,128)}, u32[]{:S(2)}) copy-start(f32[12,40]{1,0:T(8,128)} %param.34) | copy-start | bytes 5764
  557.5 105.4 %copy-start.51 = (f32[12,40]{1,0:T(8,128)S(1)}, f32[12,40]{1,0:T(8,128)}, u32[]{:S(2)}) copy-start(f32[12,40]{1,0:T(8,128)} %param.36) | copy-start | bytes 5764
  557.5 105.4 %copy-start.52 = (f32[12,40]{1,0:T(8,128)S(1)}, f32[12,40]{1,0:T(8,128)}, u32[]{:S(2)}) copy-start(f32[12,40]{1,0:T(8,128)} %param.35) | copy-start | bytes 5764
  580.0 191.2 %copy-start.13 = (f32[10,16,1536]{2,1,0:T(8,128)S(1)}, f32[10,16,1536]{2,1,0:T(8,128)}, u32[]{:S(2)}) copy-start(f32[10,16,1536]{2,1,0:T(8,128)} %param.40) | copy-start | bytes 2949124
  580.0 191.1 %copy-start.28 = (f32[10,16,1536]{2,1,0:T(8,128)S(1)}, f32[10,16,1536]{2,1,0:T(8,128)}, u32[]{:S(2)}) copy-start(f32[10,16,1536]{2,1,0:T(8,128)} %param.42) | copy-start | bytes 2949124
  580.0 191.1 %copy-start.29 = (f32[10,16,1536]{2,1,0:T(8,128)S(1)}, f32[10,16,1536]{2,1,0:T(8,128)}, u32[]{:S(2)}) copy-start(f32[10,16,1536]{2,1,0:T(8,128)} %param.41) | copy-start | bytes 2949124
  659.8 3.6 collective-permute-start.9
  769.9 4.4 collective-permute-start.8
  (50 other events, 245.7 us)
Sparse Core Ops, SparseCore 0:
  56.2 46.9 all-gather.3
  105.9 104.8 all-gather.5
  212.9 68.1 all-gather.7
  488.8 83.2 reduce-scatter.3
  575.4 83.4 reduce-scatter.7
  662.6 106.1 reduce-scatter.5

commit v2 on v1

v2 whole, which is shorter than its diff:
```python
import jax
import jax.numpy as jnp
from jax import lax
from jax.experimental import pallas as pl
from jax.experimental.pallas import tpu as pltpu
from jax.sharding import Mesh, PartitionSpec as P

D = 1536
QH = 24
KVH = 8
HD = 64
FF = 512
EXPERTS = 40
TOP = 8
STEP = 10
CAP = 29

N_SEQ = 4
TOK_DEV = 128
GROUP = 512
PAIR_TOK = 2 * GROUP
LOCAL_E = EXPERTS // (2 * N_SEQ)
SLOTS = 256
Q_OWN = QH * HD // N_SEQ
KV_OWN = 2 * KVH * HD // N_SEQ
MIX_OWN = Q_OWN + KV_OWN
HEADS_OWN = QH // N_SEQ
KV_HEADS_OWN = KVH // N_SEQ
PER_KV = QH // KVH
ROWS = 12

norm_eps = 1e-06
rope_base = 10000.0
beta_first = 0.9
beta_second = 0.95
adam_eps = 1e-08
weight_decay = 0.1

FSDP = ("x", "y", "core")
PLANE = ("x", "y")
f32 = jnp.float32
bf16 = jnp.bfloat16


BIG = 56 * 1024 * 1024
HALF = TOK_DEV // 2
QOWN = Q_OWN
MESH = pl.DeviceIdType.MESH
ANY = pl.BlockSpec(memory_space=pl.ANY)
VMEM = pl.BlockSpec(memory_space=pltpu.VMEM)


def dot(a, b, dims):
    return lax.dot_general(a, b, (dims, ((), ())), preferred_element_type=f32)


def greet(peers):
    barrier = pltpu.get_barrier_semaphore()
    for axis, peer in peers:
        pl.semaphore_signal(barrier, inc=1, device_id={axis: peer}, device_id_type=MESH)
    pl.semaphore_wait(barrier, len(peers))


def sender(send_sem, recv_sem):
    def send(src, dst, index, axis, peer):
        copy = pltpu.make_async_remote_copy(
            src_ref=src,
            dst_ref=dst,
            send_sem=send_sem.at[index],
            recv_sem=recv_sem.at[index],
            device_id={axis: peer},
            device_id_type=MESH,
        )
        copy.start()
        return copy

    return send


def ring(me):
    right, left = lax.rem(me + 1, N_SEQ), lax.rem(me + 3, N_SEQ)
    return right, left, lax.rem(me + 2, N_SEQ)


TOP_ROWS, LOW_ROWS = pl.ds(0, HALF), pl.ds(HALF, HALF)
GATHER_SEMS = 10


class Gather:
    def __init__(self, send, base, mine, out, me, core=None):
        self.send, self.base, self.out, self.core, self.me = send, base, out, core, me
        right, left, self.far = ring(me)
        self.right, self.left = right, left
        here = out.at[me]
        self.first = [
            send(mine.at[TOP_ROWS], here.at[TOP_ROWS], base, "seq", right),
            send(mine.at[LOW_ROWS], here.at[LOW_ROWS], base + 1, "seq", left),
            send(mine.at[LOW_ROWS], here.at[LOW_ROWS], base + 2, "seq", right),
            send(mine.at[TOP_ROWS], here.at[TOP_ROWS], base + 3, "seq", left),
        ]
        self.later = []
        self.pairs = []

    def relay(self):
        send, base, out = self.send, self.base, self.out
        self.first[0].wait_recv()
        part = out.at[self.left, TOP_ROWS]
        self.later.append(send(part, part, base + 4, "seq", self.right))
        self.first[1].wait_recv()
        part = out.at[self.right, LOW_ROWS]
        self.later.append(send(part, part, base + 5, "seq", self.left))

    def finish(self):
        self.first[2].wait_recv()
        self.first[3].wait_recv()
        for copy in self.later:
            copy.wait_recv()

    def drain(self):
        for copy in self.first + self.later:
            copy.wait_send()


def pair_blocks(send, base, mine, out, other, gather, me, core):
    copies = [send(mine, out.at[core, me], base, "core", other)]
    gather.relay()
    gather.first[2].wait_recv()
    block = out.at[core, gather.left]
    copies.append(send(block, block, base + 1, "core", other))
    gather.first[3].wait_recv()
    block = out.at[core, gather.right]
    copies.append(send(block, block, base + 2, "core", other))
    for copy in gather.later:
        copy.wait_recv()
    block = out.at[core, gather.far]
    copies.append(send(block, block, base + 3, "core", other))
    return copies


def reduce_scratch(width):
    half = pltpu.VMEM((HALF, width), bf16)
    block = pltpu.VMEM((TOK_DEV, width), bf16)
    return [half, half, half, half, block, block]


class Reduce:
    def __init__(self, send, base, part, bufs, me):
        self.send, self.base, self.part, self.bufs, self.me = send, base, part, bufs, me
        self.right, self.left, self.far = ring(me)

    def start_far(self):
        from_left, from_right = self.bufs[0], self.bufs[1]
        part = self.part
        self.copies = [
            self.send(part.at[self.far, TOP_ROWS], from_left, self.base, "seq", self.right),
            self.send(part.at[self.far, LOW_ROWS], from_right, self.base + 1, "seq", self.left),
        ]

    def start_near(self):
        got_left, got_right = self.bufs[4], self.bufs[5]
        part = self.part
        self.copies += [
            self.send(
                part.at[self.right, LOW_ROWS],
                got_left.at[LOW_ROWS],
                self.base + 2,
                "seq",
                self.right,
            ),
            self.send(
                part.at[self.left, TOP_ROWS],
                got_right.at[TOP_ROWS],
                self.base + 3,
                "seq",
                self.left,
            ),
        ]

    def relay(self):
        from_left, from_right, to_right, to_left, got_left, got_right = self.bufs
        part = self.part
        self.copies[0].wait_recv()
        to_right[...] = (
            part[self.right, :HALF].astype(f32) + from_left[...].astype(f32)
        ).astype(bf16)
        self.copies.append(
            self.send(to_right, got_left.at[TOP_ROWS], self.base + 4, "seq", self.right)
        )
        self.copies[1].wait_recv()
        to_left[...] = (
            part[self.left, HALF:].astype(f32) + from_right[...].astype(f32)
        ).astype(bf16)
        self.copies.append(
            self.send(to_left, got_right.at[LOW_ROWS], self.base + 5, "seq", self.left)
        )

    def total(self):
        for copy in self.copies[2:]:
            copy.wait_recv()
        got_left, got_right = self.bufs[4], self.bufs[5]
        return (
            self.part[self.me].astype(f32) + got_left[...].astype(f32) + got_right[...].astype(f32)
        )

    def drain(self):
        for copy in self.copies:
            copy.wait_send()


def sems(count):
    return [pltpu.SemaphoreType.DMA((count,)), pltpu.SemaphoreType.DMA((count,))]


def unit_scale(vector):
    return lax.rsqrt(jnp.mean(vector * vector, axis=-1, keepdims=True) + norm_eps)


def norm_back(vector, gain, grad):
    scale = unit_scale(vector)
    unit = vector * scale
    pulled = grad * gain
    back = scale * (pulled - unit * jnp.mean(pulled * unit, axis=-1, keepdims=True))
    return back, jnp.sum(unit * grad, axis=0, keepdims=True)


def inputs_kernel(in_ref, cot_ref, hit_ref, in_all, cot_all, hit_all, send_sem, recv_sem, copy_sem):
    me, core = lax.axis_index("seq"), lax.axis_index("core")
    right, left, _ = ring(me)
    greet([("seq", right), ("seq", left), ("core", 1 - core)])
    send = sender(send_sem, recv_sem)
    hits = Gather(send, 0, hit_ref, hit_all, me)
    rows = Gather(send, 6, in_ref, in_all, me)
    cots = Gather(send, 12, cot_ref, cot_all.at[core], me)
    local = [
        pltpu.make_async_copy(hit_ref, hit_all.at[me], copy_sem.at[0]),
        pltpu.make_async_copy(in_ref, in_all.at[me], copy_sem.at[1]),
        pltpu.make_async_copy(cot_ref, cot_all.at[core, me], copy_sem.at[2]),
    ]
    for copy in local:
        copy.start()
    hits.relay()
    rows.relay()
    pairs = pair_blocks(send, 18, cot_ref, cot_all, 1 - core, cots, me, core)
    hits.finish()
    rows.finish()
    for copy in pairs:
        copy.wait()
    for gather in (hits, rows, cots):
        gather.drain()
    for copy in local:
        copy.wait()


def gather_inputs(rows, cots, hits):
    return pl.pallas_call(
        inputs_kernel,
        out_shape=[
            jax.ShapeDtypeStruct((N_SEQ, TOK_DEV, D), bf16),
            jax.ShapeDtypeStruct((2, N_SEQ, TOK_DEV, D), bf16),
            jax.ShapeDtypeStruct((N_SEQ, TOK_DEV, 128), bf16),
        ],
        in_specs=[ANY] * 3,
        out_specs=[ANY] * 3,
        scratch_shapes=sems(22) + [pltpu.SemaphoreType.DMA((3,))],
        compiler_params=pltpu.CompilerParams(collective_id=1, has_side_effects=True),
    )(rows, cots, hits)


def middle_kernel(
    part_ref, in_ref, gain_ref, middle_ref, tokens_ref, mine, *rest
):
    bufs, (send_sem, recv_sem, copy_sem) = rest[:6], rest[6:]
    me, core = lax.axis_index("seq"), lax.axis_index("core")
    right, left, _ = ring(me)
    greet([("seq", right), ("seq", left), ("core", 1 - core)])
    send = sender(send_sem, recv_sem)
    reduce = Reduce(send, 0, part_ref, bufs, me)
    reduce.start_far()
    reduce.start_near()
    reduce.relay()
    middle = in_ref[...].astype(f32) + reduce.total()
    middle_ref[...] = middle
    mine[...] = (middle * unit_scale(middle) * gain_ref[...]).astype(bf16)
    gather = Gather(send, 6, mine, tokens_ref.at[core], me)
    local = pltpu.make_async_copy(mine, tokens_ref.at[core, me], copy_sem)
    local.start()
    pairs = pair_blocks(send, 12, mine, tokens_ref, 1 - core, gather, me, core)
    for copy in pairs:
        copy.wait()
    gather.drain()
    reduce.drain()
    local.wait()


def middle_tokens(part, rows, gain):
    return pl.pallas_call(
        middle_kernel,
        out_shape=[
            jax.ShapeDtypeStruct((TOK_DEV, D), f32),
            jax.ShapeDtypeStruct((2, N_SEQ, TOK_DEV, D), bf16),
        ],
        in_specs=[VMEM] * 3,
        out_specs=[VMEM, ANY],
        scratch_shapes=[pltpu.VMEM((TOK_DEV, D), bf16)]
        + reduce_scratch(D)
        + sems(16)
        + [pltpu.SemaphoreType.DMA],
        compiler_params=pltpu.CompilerParams(
            collective_id=2, has_side_effects=True, vmem_limit_bytes=BIG
        ),
    )(part, rows, gain)


BACK_WIDTH = D + 128


def turn_kernel(
    back_ref, middle_ref, cot_ref, gate_ref, router_ref, gain_ref,
    grad_ref, branch_ref, logit_ref, gain_grad_ref, part, from_core, mine, *rest
):
    bufs, (send_sem, recv_sem, copy_sem) = rest[:6], rest[6:]
    me, core = lax.axis_index("seq"), lax.axis_index("core")
    right, left, far = ring(me)
    greet([("seq", right), ("seq", left), ("core", 1 - core)])
    send = sender(send_sem, recv_sem)
    order = (far, right, left, me)
    swaps = [
        send(back_ref.at[1 - core, block], from_core.at[i], 12 + i, "core", 1 - core)
        for i, block in enumerate(order)
    ]
    reduce = Reduce(send, 0, part, bufs, me)
    for i, block in enumerate(order):
        swaps[i].wait_recv()
        part[block] = (back_ref[core, block].astype(f32) + from_core[i].astype(f32)).astype(bf16)
        if i == 0:
            reduce.start_far()
        if i == 2:
            reduce.start_near()
    reduce.relay()
    total = reduce.total()
    gates, gate_grad = gate_ref[...], total[:, D:]
    mean_term = jnp.sum(gates * gate_grad, axis=1, keepdims=True)
    logit_grad = (gates * (gate_grad - mean_term)).astype(bf16)
    logit_ref[...] = logit_grad
    normed_grad = total[:, :D] + dot(logit_grad, router_ref[...], ((1,), (1,)))
    back, gain_grad = norm_back(middle_ref[...], gain_ref[...], normed_grad)
    gain_grad_ref[...] = gain_grad
    middle_grad = cot_ref[...].astype(f32) + back
    grad_ref[...] = middle_grad
    mine[...] = middle_grad.astype(bf16)
    gather = Gather(send, 6, mine, branch_ref, me)
    local = pltpu.make_async_copy(mine, branch_ref.at[me], copy_sem)
    local.start()
    gather.relay()
    gather.finish()
    gather.drain()
    reduce.drain()
    for copy in swaps:
        copy.wait_send()
    local.wait()


def turn(back, middle, cot, gates, router, gain):
    return pl.pallas_call(
        turn_kernel,
        out_shape=[
            jax.ShapeDtypeStruct((TOK_DEV, D), f32),
            jax.ShapeDtypeStruct((N_SEQ, TOK_DEV, D), bf16),
            jax.ShapeDtypeStruct((TOK_DEV, 128), bf16),
            jax.ShapeDtypeStruct((1, D), f32),
        ],
        in_specs=[VMEM] * 6,
        out_specs=[VMEM, ANY, VMEM, VMEM],
        scratch_shapes=[
            pltpu.VMEM((N_SEQ, TOK_DEV, BACK_WIDTH), bf16),
            pltpu.VMEM((N_SEQ, TOK_DEV, BACK_WIDTH), bf16),
            pltpu.VMEM((TOK_DEV, D), bf16),
        ]
        + reduce_scratch(BACK_WIDTH)
        + sems(16)
        + [pltpu.SemaphoreType.DMA],
        compiler_params=pltpu.CompilerParams(
            collective_id=3, has_side_effects=True, vmem_limit_bytes=BIG
        ),
    )(back, middle, cot, gates, router, gain)


def input_kernel(part_ref, in_ref, grad_ref, gain_ref, out_ref, gain_grad_ref, *rest):
    bufs, (send_sem, recv_sem) = rest[:6], rest[6:]
    me = lax.axis_index("seq")
    right, left, _ = ring(me)
    greet([("seq", right), ("seq", left)])
    reduce = Reduce(sender(send_sem, recv_sem), 0, part_ref, bufs, me)
    reduce.start_far()
    reduce.start_near()
    reduce.relay()
    back, gain_grad = norm_back(in_ref[...].astype(f32), gain_ref[...], reduce.total())
    gain_grad_ref[...] = gain_grad
    out_ref[...] = (grad_ref[...] + back).astype(bf16)
    reduce.drain()


def input_back(part, rows, middle_grad, gain):
    return pl.pallas_call(
        input_kernel,
        out_shape=[
            jax.ShapeDtypeStruct((TOK_DEV, D), bf16),
            jax.ShapeDtypeStruct((1, D), f32),
        ],
        in_specs=[VMEM] * 4,
        out_specs=[VMEM, VMEM],
        scratch_shapes=reduce_scratch(D) + sems(6),
        compiler_params=pltpu.CompilerParams(
            collective_id=4, has_side_effects=True, vmem_limit_bytes=BIG
        ),
    )(part, rows, middle_grad, gain)


PAD_ROWS = 16
WIDE = 768


def peers_of(axis):
    me = lax.axis_index(axis)
    return [lax.rem(me + k, 4) for k in (1, 2, 3)]


def plane_greet():
    greet(
        [(axis, peer) for axis in ("seq", "x", "y") for peer in peers_of(axis)]
        + [("core", 1 - lax.axis_index("core"))]
    )


def row_pick(shape, padded_axis):
    padded = lax.broadcasted_iota(jnp.int32, shape, padded_axis)
    plain = lax.broadcasted_iota(jnp.int32, shape, 1 - padded_axis)
    row = lax.rem(padded, 16)
    return ((plain == lax.div(padded, 16) * 12 + row) & (row < 12)).astype(bf16)


def weights_kernel(
    entry_ref, exit_ref, entry_out, shared_out, exit_out, hold, full, send_sem, recv_sem, copy_sem
):
    z, x, y, c = (lax.axis_index(a) for a in ("seq", "x", "y", "core"))
    plane_greet()
    send = sender(send_sem, recv_sem)
    copies = [
        send(entry_ref.at[peer], hold.at[z], k, "seq", peer)
        for k, peer in enumerate(peers_of("seq"))
    ]
    local = [
        pltpu.make_async_copy(entry_ref.at[z], hold.at[z], copy_sem.at[0]),
        pltpu.make_async_copy(exit_ref, hold.at[pl.ds(4, 2)], copy_sem.at[1]),
    ]
    for copy in local:
        copy.start()
    for copy in local:
        copy.wait()
    for copy in copies:
        copy.wait_recv()
    own = pltpu.make_async_copy(hold, full.at[:, x, y, c], copy_sem.at[2])
    own.start()
    low, high = pl.ds(0, 3), pl.ds(3, 3)
    first_x = [
        send(hold.at[low], full.at[low, x, y, c], 3 + k, "x", peer)
        for k, peer in enumerate(peers_of("x"))
    ]
    first_y = [
        send(hold.at[high], full.at[high, x, y, c], 6 + k, "y", peer)
        for k, peer in enumerate(peers_of("y"))
    ]
    own.wait()
    for copy in first_x:
        copy.wait_recv()
    line = full.at[low, :, y, c]
    second_y = [send(line, line, 9 + k, "y", peer) for k, peer in enumerate(peers_of("y"))]
    for copy in first_y:
        copy.wait_recv()
    line = full.at[high, x, :, c]
    second_x = [send(line, line, 12 + k, "x", peer) for k, peer in enumerate(peers_of("x"))]
    for copy in second_y + second_x:
        copy.wait_recv()
    half = full.at[:, :, :, c]
    last = send(half, half, 15, "core", 1 - c)
    last.wait_recv()
    pick = row_pick((QOWN, 512), 1)
    for block in range(4):
        got = dot(pick, full[block].reshape(512, WIDE), ((1,), (0,))).astype(bf16)
        entry_out[QOWN * block : QOWN * (block + 1), :] = got[:, :640]
        shared_out[QOWN * block : QOWN * (block + 1), :] = got[:, 640:]
    for block in range(2):
        got = dot(pick, full[4 + block].reshape(512, WIDE), ((1,), (0,))).astype(bf16)
        exit_out[:, WIDE * block : WIDE * (block + 1)] = got
    for copy in copies + first_x + first_y + second_x + second_y + [last]:
        copy.wait_send()


def gather_weights(entry_cols, exit_cols):
    return pl.pallas_call(
        weights_kernel,
        out_shape=[
            jax.ShapeDtypeStruct((D, 640), bf16),
            jax.ShapeDtypeStruct((D, 128), bf16),
            jax.ShapeDtypeStruct((QOWN, D), bf16),
        ],
        in_specs=[VMEM] * 2,
        out_specs=[VMEM] * 3,
        scratch_shapes=[
            pltpu.VMEM((6, PAD_ROWS, WIDE), bf16),
            pltpu.VMEM((6, 4, 4, 2, PAD_ROWS, WIDE), bf16),
        ]
        + sems(16)
        + [pltpu.SemaphoreType.DMA((3,))],
        compiler_params=pltpu.CompilerParams(
            collective_id=5, has_side_effects=True, vmem_limit_bytes=BIG
        ),
    )(entry_cols, exit_cols)


def owners_kernel(
    normed_ref, mixed_ref, attended_ref, branch_ref, shared_ref, entry_out, exit_out,
    full, core_buf, chip, got_x, got_y, line_x, line_y, last_x, last_y, final, got_z,
    send_sem, recv_sem,
):
    z, x, y, c = (lax.axis_index(a) for a in ("seq", "x", "y", "core"))
    plane_greet()
    send = sender(send_sem, recv_sem)
    pick = row_pick((512, QOWN), 0)
    shape = (4, 4, 2, PAD_ROWS, WIDE)
    swaps = []
    for block in range(6):
        if block < 4:
            rows = slice(QOWN * block, QOWN * (block + 1))
            grad = dot(normed_ref[:, rows], mixed_ref[...], ((0,), (0,))).astype(bf16)
            grad = jnp.concatenate([grad, shared_ref[rows, :]], axis=1)
        else:
            cols = slice(WIDE * (block - 4), WIDE * (block - 3))
            grad = dot(attended_ref[...], branch_ref[:, cols], ((0,), (0,))).astype(bf16)
        full[block] = dot(pick, grad, ((1,), (0,))).astype(bf16).reshape(shape)
        swaps.append(send(full.at[block, :, :, 1 - c], core_buf.at[block], block, "core", 1 - c))
    for block in range(6):
        swaps[block].wait_recv()
        chip[block] = (full[block, :, :, c].astype(f32) + core_buf[block].astype(f32)).astype(bf16)
    low, high = pl.ds(0, 3), pl.ds(3, 3)
    first_x = [
        send(chip.at[low, peer], got_x.at[k], 6 + k, "x", peer)
        for k, peer in enumerate(peers_of("x"))
    ]
    first_y = [
        send(chip.at[high, :, peer], got_y.at[k], 9 + k, "y", peer)
        for k, peer in enumerate(peers_of("y"))
    ]
    for copy in first_x:
        copy.wait_recv()
    total = chip[low, x].astype(f32)
    for k in range(3):
        total += got_x[k].astype(f32)
    line_x[...] = total.astype(bf16)
    second_y = [
        send(line_x.at[:, peer], last_y.at[k], 12 + k, "y", peer)
        for k, peer in enumerate(peers_of("y"))
    ]
    for copy in first_y:
        copy.wait_recv()
    total = chip[high, :, y].astype(f32)
    for k in range(3):
        total += got_y[k].astype(f32)
    line_y[...] = total.astype(bf16)
    second_x = [
        send(line_y.at[:, peer], last_x.at[k], 15 + k, "x", peer)
        for k, peer in enumerate(peers_of("x"))
    ]
    for copy in second_y:
        copy.wait_recv()
    total = line_x[:, y].astype(f32)
    for k in range(3):
        total += last_y[k].astype(f32)
    final[low] = total
    for copy in second_x:
        copy.wait_recv()
    total = line_y[:, x].astype(f32)
    for k in range(3):
        total += last_x[k].astype(f32)
    final[high] = total
    third = [
        send(final.at[peer], got_z.at[k], 18 + k, "seq", peer)
        for k, peer in enumerate(peers_of("seq"))
    ]
    exit_out[...] = final[pl.ds(4, 2)]
    entry_out[z] = final[z]
    for k, copy in enumerate(third):
        copy.wait_recv()
        entry_out[lax.rem(z + 3 - k, 4)] = got_z[k]
    for copy in swaps + first_x + first_y + second_x + second_y + third:
        copy.wait_send()


def sum_to_owners(normed, mixed_grad, attended, branch_grad, shared):
    block = (PAD_ROWS, WIDE)
    return pl.pallas_call(
        owners_kernel,
        out_shape=[
            jax.ShapeDtypeStruct((4,) + block, f32),
            jax.ShapeDtypeStruct((2,) + block, f32),
        ],
        in_specs=[VMEM] * 5,
        out_specs=[VMEM] * 2,
        scratch_shapes=[
            pltpu.VMEM((6, 4, 4, 2) + block, bf16),
            pltpu.VMEM((6, 4, 4) + block, bf16),
            pltpu.VMEM((6, 4, 4) + block, bf16),
            pltpu.VMEM((3, 3, 4) + block, bf16),
            pltpu.VMEM((3, 3, 4) + block, bf16),
            pltpu.VMEM((3, 4) + block, bf16),
            pltpu.VMEM((3, 4) + block, bf16),
            pltpu.VMEM((3, 3) + block, bf16),
            pltpu.VMEM((3, 3) + block, bf16),
            pltpu.VMEM((6,) + block, f32),
            pltpu.VMEM((3,) + block, f32),
        ]
        + sems(21),
        compiler_params=pltpu.CompilerParams(
            collective_id=6, has_side_effects=True, vmem_limit_bytes=BIG
        ),
    )(normed, mixed_grad, attended, branch_grad, shared)


def dispatch_kernel(rank_ref, gate_ref, tokens_ref, cots_ref, rows_ref, cot_rows_ref, row_gate_ref):
    slot = lax.broadcasted_iota(jnp.int32, (SLOTS, PAIR_TOK), 0)
    match = rank_ref[0] == slot
    row_gate_ref[0] = jnp.sum(jnp.where(match, gate_ref[0], 0.0), axis=1, keepdims=True)
    pick = match.astype(bf16)
    for j in range(3):
        cols = slice(512 * j, 512 * (j + 1))
        rows_ref[0, :, cols] = dot(pick, tokens_ref[:, cols], ((1,), (0,))).astype(bf16)
        cot_rows_ref[0, :, cols] = dot(pick, cots_ref[:, cols], ((1,), (0,))).astype(bf16)

def dispatch(rank, gates, tokens, cots):
    one = lambda e: (e, 0, 0)
    whole = lambda e: (0, 0)
    return pl.pallas_call(
        dispatch_kernel,
        grid=(LOCAL_E,),
        in_specs=[
            pl.BlockSpec((1, 1, PAIR_TOK), one),
            pl.BlockSpec((1, 1, PAIR_TOK), one),
            pl.BlockSpec((PAIR_TOK, D), whole),
            pl.BlockSpec((PAIR_TOK, D), whole),
        ],
        out_specs=[
            pl.BlockSpec((1, SLOTS, D), one),
            pl.BlockSpec((1, SLOTS, D), one),
            pl.BlockSpec((1, SLOTS, 1), one),
        ],
        out_shape=[
            jax.ShapeDtypeStruct((LOCAL_E, SLOTS, D), bf16),
            jax.ShapeDtypeStruct((LOCAL_E, SLOTS, D), bf16),
            jax.ShapeDtypeStruct((LOCAL_E, SLOTS, 1), f32),
        ],
        compiler_params=pltpu.CompilerParams(vmem_limit_bytes=BIG),
        cost_estimate=pl.CostEstimate(
            flops=4 * LOCAL_E * SLOTS * PAIR_TOK * D, bytes_accessed=16 << 20, transcendentals=0
        ),
    )(rank[:, None], gates[:, None], tokens, cots)

def weights_of(w_ref):
    expand = w_ref[:, 0, :96, :].reshape(D, 2 * FF)
    left = w_ref[:, 0, 96:128, :].reshape(FF, 1024)
    right = jnp.concatenate([w_ref[:, 0, 128:144, :512], w_ref[:, 0, 128:144, 512:]], axis=1)
    return expand, left, right.reshape(FF, 512)

def grads_kernel(rows_ref, cot_ref, gate_ref, w_ref, hidden_ref, up_ref, out_ref):
    expand, left, right = weights_of(w_ref)
    grad_rows = (gate_ref[0] * cot_ref[0].astype(f32)).astype(bf16)
    rows = rows_ref[0]
    gate_pre = dot(rows, expand[:, :FF], ((1,), (0,)))
    up_part = dot(rows, expand[:, FF:], ((1,), (0,)))
    sig = jax.nn.sigmoid(gate_pre)
    hidden = (gate_pre * sig * up_part).astype(bf16)
    hidden_ref[0] = hidden
    hidden_grad = dot(grad_rows[:, :1024], left, ((1,), (1,))) + dot(
        grad_rows[:, 1024:], right, ((1,), (1,))
    )
    up_ref[0, :, :FF] = (hidden_grad * up_part * sig * (1.0 + gate_pre * (1.0 - sig))).astype(bf16)
    up_ref[0, :, FF:] = (hidden_grad * gate_pre * sig).astype(bf16)
    grad_left = dot(hidden, grad_rows[:, :1024], ((0,), (0,))).astype(bf16)
    out_ref[:, 0, 96:128, :] = grad_left.reshape(16, 32, 1024)
    grad_right = dot(hidden, grad_rows[:, 1024:], ((0,), (0,))).astype(bf16).reshape(16, 32, 512)
    out_ref[:, 0, 128:144, :512] = grad_right[:, :16]
    out_ref[:, 0, 128:144, 512:] = grad_right[:, 16:]
    up_grad = up_ref[0]
    for j in range(4):
        part = dot(rows[:, 384 * j : 384 * (j + 1)], up_grad, ((0,), (0,))).astype(bf16)
        out_ref[4 * j : 4 * (j + 1), 0, :96, :] = part.reshape(4, 96, 1024)

def expert_grads(rows, cot_rows, row_gates, weights):
    one = lambda e: (e, 0, 0)
    wide = lambda e: (0, e, 0, 0)
    return pl.pallas_call(
        grads_kernel,
        grid=(LOCAL_E,),
        in_specs=[
            pl.BlockSpec((1, SLOTS, D), one),
            pl.BlockSpec((1, SLOTS, D), one),
            pl.BlockSpec((1, SLOTS, 1), one),
            pl.BlockSpec((16, 1, 144, 1024), wide),
        ],
        out_specs=[
            pl.BlockSpec((1, SLOTS, FF), one),
            pl.BlockSpec((1, SLOTS, 2 * FF), one),
            pl.BlockSpec((16, 1, 144, 1024), wide),
        ],
        out_shape=[
            jax.ShapeDtypeStruct((LOCAL_E, SLOTS, FF), bf16),
            jax.ShapeDtypeStruct((LOCAL_E, SLOTS, 2 * FF), bf16),
            jax.ShapeDtypeStruct((16, LOCAL_E, 144, 1024), bf16),
        ],
        compiler_params=pltpu.CompilerParams(vmem_limit_bytes=BIG),
        cost_estimate=pl.CostEstimate(
            flops=12 * LOCAL_E * SLOTS * D * FF, bytes_accessed=60 << 20, transcendentals=0
        ),
    )(rows, cot_rows, row_gates, weights)

def combine_kernel(
    first_ref, rank_ref, up_ref, hidden_ref, gate_ref, cot_ref, w_ref, back_ref, out_ref, back_s, out_s
):
    e = pl.program_id(0)

    @pl.when(e < LOCAL_E)
    def _():
        expand, left, right = weights_of(w_ref)
        at = pl.ds(pl.multiple_of(e * SLOTS, SLOTS), SLOTS)
        back_s[at, :D] = dot(up_ref[0], expand, ((1,), (1,))).astype(bf16)
        hidden = hidden_ref[0]
        expert_out = jnp.concatenate(
            [dot(hidden, left, ((1,), (0,))), dot(hidden, right, ((1,), (0,)))], axis=1
        )
        expert_out = expert_out.astype(bf16).astype(f32)
        gate_grad = jnp.sum(expert_out * cot_ref[0].astype(f32), axis=1, keepdims=True)
        lane = lax.broadcasted_iota(jnp.int32, (SLOTS, 128), 1)
        back_s[at, D:] = jnp.where(lane == first_ref[0] + e, gate_grad, 0.0).astype(bf16)
        out_s[at, :] = (gate_ref[0] * expert_out).astype(bf16)

    @pl.when(e == LOCAL_E)
    def _():
        slot = lax.broadcasted_iota(jnp.int32, (256, SLOTS), 1)
        for i in range(4):
            toks = slice(256 * i, 256 * (i + 1))
            picks = jnp.concatenate(
                [(rank_ref[toks, k : k + 1] == slot).astype(bf16) for k in range(LOCAL_E)], axis=1
            )
            back_ref[toks, :] = dot(picks, back_s[...], ((1,), (0,))).astype(bf16)
            out_ref[toks, :] = dot(picks, out_s[...], ((1,), (0,))).astype(bf16)

def combine(first, rank_cols, up_grad, hidden, row_gates, cot_rows, weights):
    last = LOCAL_E - 1
    one = lambda e: (jnp.minimum(e, last), 0, 0)
    wide = lambda e: (0, jnp.minimum(e, last), 0, 0)
    whole = lambda e: (0, 0)
    return pl.pallas_call(
        combine_kernel,
        grid=(LOCAL_E + 1,),
        in_specs=[
            pl.BlockSpec(memory_space=pltpu.SMEM),
            pl.BlockSpec((PAIR_TOK, LOCAL_E), whole),
            pl.BlockSpec((1, SLOTS, 2 * FF), one),
            pl.BlockSpec((1, SLOTS, FF), one),
            pl.BlockSpec((1, SLOTS, 1), one),
            pl.BlockSpec((1, SLOTS, D), one),
            pl.BlockSpec((16, 1, 144, 1024), wide),
        ],
        out_specs=[
            pl.BlockSpec((PAIR_TOK, BACK_WIDTH), whole),
            pl.BlockSpec((PAIR_TOK, D), whole),
        ],
        out_shape=[
            jax.ShapeDtypeStruct((PAIR_TOK, BACK_WIDTH), bf16),
            jax.ShapeDtypeStruct((PAIR_TOK, D), bf16),
        ],
        scratch_shapes=[
            pltpu.VMEM((LOCAL_E * SLOTS, BACK_WIDTH), bf16),
            pltpu.VMEM((LOCAL_E * SLOTS, D), bf16),
        ],
        compiler_params=pltpu.CompilerParams(vmem_limit_bytes=BIG),
        cost_estimate=pl.CostEstimate(
            flops=6 * LOCAL_E * SLOTS * D * FF + 4 * LOCAL_E * SLOTS * PAIR_TOK * D,
            bytes_accessed=40 << 20,
            transcendentals=0,
        ),
    )(first, rank_cols, up_grad, hidden, row_gates, cot_rows, weights)


def core_swap(value):
    return lax.ppermute(value, "core", [(0, 1), (1, 0)])


def core_order(core, mine, other, axis):
    return jnp.concatenate(
        [jnp.where(core == 0, mine, other), jnp.where(core == 0, other, mine)], axis=axis
    )


def norm_apply(vector, gain):
    scale = lax.rsqrt(jnp.mean(vector * vector, axis=-1, keepdims=True) + norm_eps)
    return vector * scale * gain


def adamw_step(weight, gradient, mean_old, square_old, rate, decay):
    drift = beta_first * mean_old + (1.0 - beta_first) * gradient
    spread = beta_second * square_old + (1.0 - beta_second) * gradient * gradient
    mean_hat = drift / (1.0 - beta_first**STEP)
    square_hat = spread / (1.0 - beta_second**STEP)
    master = weight - rate * (mean_hat / (jnp.sqrt(square_hat) + adam_eps) + decay * weight)
    return (drift, spread, master)


def rotate(vector, cosine, sine):
    first, second = vector[..., : HD // 2], vector[..., HD // 2 :]
    return jnp.concatenate(
        [first * cosine - second * sine, second * cosine + first * sine], axis=-1
    )


def on_device(
    activations,
    cotangent,
    seq_lengths,
    deal_order,
    routes,
    entry_weight,
    entry_mean,
    entry_square,
    exit_weight,
    exit_mean,
    exit_square,
    router_weight,
    router_mean,
    router_square,
    expand_weight,
    expand_mean,
    expand_square,
    shrink_weight,
    shrink_mean,
    shrink_square,
    norm_gains,
    gains_mean,
    gains_square,
):
    seq = lax.axis_index("seq")
    core = lax.axis_index("core")
    first = (seq * 2 + core) * LOCAL_E

    expand_b = expand_weight.astype(bf16)
    shrink_b = shrink_weight.astype(bf16)
    piece = jnp.concatenate([expand_b, shrink_b[:, :, :1024]], axis=1)

    def exchange(value):
        mine = lax.dynamic_slice_in_dim(value, core * LOCAL_E, LOCAL_E, 0)
        other = core_swap(lax.dynamic_slice_in_dim(value, (1 - core) * LOCAL_E, LOCAL_E, 0))
        return jnp.where(core == 0, mine, other), jnp.where(core == 0, other, mine)

    low, high = exchange(piece)
    low_end, high_end = exchange(shrink_b[:, :, 1024:])
    packed = jnp.concatenate(
        [
            low[:, :48],
            high[:, :48],
            low[:, 48:],
            high[:, 48:],
            jnp.concatenate([low_end, high_end], axis=2),
        ],
        axis=1,
    )
    packed, rows_in, cots_in = lax.optimization_barrier((packed, activations[0], cotangent[0]))
    weights = lax.all_gather(packed, PLANE, axis=0, tiled=False)

    entry_b = entry_weight.astype(bf16)
    shared_b = jnp.concatenate([router_weight, norm_gains.T], axis=1).astype(bf16)
    shared_b = jnp.pad(shared_b, ((0, 0), (0, 128 - EXPERTS - 2)))
    entry_cols = jnp.concatenate(
        [
            entry_b[:, : QH * HD].reshape(ROWS, N_SEQ, Q_OWN).transpose(1, 0, 2),
            entry_b[:, QH * HD :].reshape(ROWS, N_SEQ, KV_OWN).transpose(1, 0, 2),
            jnp.broadcast_to(shared_b[None], (N_SEQ, ROWS, 128)),
        ],
        axis=2,
    )
    exit_cols = exit_weight.astype(bf16).reshape(ROWS, 2, WIDE).transpose(1, 0, 2)
    pad = ((0, 0), (0, PAD_ROWS - ROWS), (0, 0))
    expert_ids = jnp.arange(128, dtype=jnp.int32)
    hit_slots = jnp.any(routes[0][:, :, None] == expert_ids[None, None, :], axis=1).astype(bf16)
    in_all, cots, hit_slots = gather_inputs(rows_in, cots_in, hit_slots)
    in_all = in_all.reshape(GROUP, D)
    entry_own, shared, exit_own = gather_weights(jnp.pad(entry_cols, pad), jnp.pad(exit_cols, pad))
    gains_full = shared[:, EXPERTS : EXPERTS + 2].astype(f32).T

    order_row = deal_order[0]
    token = jnp.arange(GROUP, dtype=jnp.int32)
    back_hot = (order_row[None, :] == token[:, None]).astype(bf16)
    hit = dot(back_hot, hit_slots.reshape(GROUP, 128), ((1,), (0,))).astype(bf16)
    hits = core_order(core, hit, core_swap(hit), 0)[:, :EXPERTS]
    own_hits = lax.dynamic_slice_in_dim(hits, first, LOCAL_E, 1)
    rank = jnp.cumsum(own_hits.astype(jnp.int32), axis=0) - 1
    rank = jnp.where(own_hits > 0, rank, -1)
    seq_ends = jnp.cumsum(seq_lengths[0])
    starts = seq_ends - seq_lengths[0]
    seq_ids = jnp.sum((token[:, None] >= seq_ends[None, :]).astype(jnp.int32), axis=1)
    seq_match = seq_ids[:, None] == jnp.arange(seq_ends.shape[0], dtype=jnp.int32)[None, :]
    positions = token - jnp.sum(jnp.where(seq_match, starts[None, :], 0), axis=1)
    frequency = rope_base ** (-jnp.arange(HD // 2, dtype=f32) * 2.0 / HD)
    phase = positions.astype(f32)[:, None] * frequency[None, :]
    cosine, sine = jnp.cos(phase)[:, None, :], jnp.sin(phase)[:, None, :]
    allowed = (seq_ids[:, None] == seq_ids[None, :]) & (token[None, :] <= token[:, None])

    normed = norm_apply(in_all.astype(f32), gains_full[0]).astype(bf16)
    mixed = dot(normed, entry_own, ((1,), (0,)))
    queries = rotate(mixed[:, :Q_OWN].reshape(GROUP, HEADS_OWN, HD), cosine, sine)
    pairs = mixed[:, Q_OWN:].reshape(GROUP, KV_HEADS_OWN, 2, HD)
    keys = rotate(pairs[:, :, 0], cosine, sine)
    queries = queries.astype(bf16).reshape(GROUP, KV_HEADS_OWN, PER_KV, HD)
    keys, values = keys.astype(bf16), pairs[:, :, 1].astype(bf16)
    scores = jnp.einsum("qhgd,khd->hgqk", queries, keys, preferred_element_type=f32) * HD**-0.5
    scores = jnp.where(allowed[None, None], scores, -1e30)
    peak = jnp.max(scores, axis=-1, keepdims=True)
    expo = jnp.exp(scores - peak)
    probs = expo / jnp.sum(expo, axis=-1, keepdims=True)
    probs_b = probs.astype(bf16)
    attended = (
        jnp.einsum("hgqk,khd->qhgd", probs_b, values, preferred_element_type=f32)
        .reshape(GROUP, Q_OWN)
        .astype(bf16)
    )
    branch_part = dot(attended, exit_own, ((1,), (0,))).astype(bf16)
    middle, tokens = middle_tokens(
        branch_part.reshape(N_SEQ, TOK_DEV, D), activations[0], gains_full[1:2]
    )
    normed_two = lax.dynamic_slice(tokens, (core, seq, 0, 0), (1, 1, TOK_DEV, D))[0, 0]
    tokens = tokens.reshape(PAIR_TOK, D)

    logits = dot(tokens, shared[:, :EXPERTS], ((1,), (0,)))
    masked = jnp.where(hits > 0, logits, -jnp.inf)
    gate_expo = jnp.exp(masked - jnp.max(masked, axis=1, keepdims=True))
    gates = gate_expo / jnp.sum(gate_expo, axis=1, keepdims=True)
    own_gates = lax.dynamic_slice_in_dim(gates, first, LOCAL_E, 1)
    rows, cot_rows, row_gates = dispatch(rank.T, own_gates.T, tokens, cots.reshape(PAIR_TOK, D))
    hidden, up_grad, expert_grad = expert_grads(rows, cot_rows, row_gates, weights)
    expert_sum = lax.psum_scatter(expert_grad, PLANE, scatter_dimension=0, tiled=False)
    back_part, out_part = combine(
        first[None], rank, up_grad, hidden, row_gates, cot_rows, weights
    )
    my_gates = lax.dynamic_slice_in_dim(gates, core * GROUP + seq * TOK_DEV, TOK_DEV, 0)
    my_gates = jnp.pad(my_gates, ((0, 0), (0, 128 - EXPERTS)))
    middle_grad, branch_grad, logit_grad, gain_two_grad = turn(
        back_part.reshape(2, N_SEQ, TOK_DEV, BACK_WIDTH),
        middle,
        cotangent[0],
        my_gates,
        shared,
        gains_full[1:2],
    )
    branch_grad = branch_grad.reshape(GROUP, D)
    router_grad = dot(normed_two, logit_grad, ((0,), (0,)))

    out_part = out_part.reshape(2, GROUP, D)
    out_mine = lax.dynamic_index_in_dim(out_part, core, 0, keepdims=False)
    out_other = core_swap(lax.dynamic_index_in_dim(out_part, 1 - core, 0, keepdims=False))
    out_sum = (out_mine.astype(f32) + out_other.astype(f32)).astype(bf16)
    out_sum = out_sum.reshape(N_SEQ, TOK_DEV, D)
    out_rows = lax.dynamic_index_in_dim(out_sum, seq, 0, keepdims=False).astype(f32)
    for step in range(1, N_SEQ):
        block = lax.dynamic_index_in_dim(out_sum, (seq + step) % N_SEQ, 0, keepdims=False)
        got = lax.ppermute(block, "seq", [(i, (i + step) % N_SEQ) for i in range(N_SEQ)])
        out_rows = out_rows + got.astype(f32)
    block_output = (middle + out_rows).astype(bf16)

    attended_grad = dot(branch_grad, exit_own, ((1,), (1,))).astype(bf16)
    attended_grad = attended_grad.reshape(GROUP, KV_HEADS_OWN, PER_KV, HD)
    prob_grad = jnp.einsum("qhgd,khd->hgqk", attended_grad, values, preferred_element_type=f32)
    delta = jnp.sum(probs * prob_grad, axis=-1, keepdims=True)
    score_grad = (probs * (prob_grad - delta) * HD**-0.5).astype(bf16)
    query_grad = jnp.einsum("hgqk,khd->qhgd", score_grad, keys, preferred_element_type=f32)
    key_grad = jnp.einsum("hgqk,qhgd->khd", score_grad, queries, preferred_element_type=f32)
    value_grad = jnp.einsum("hgqk,qhgd->khd", probs_b, attended_grad, preferred_element_type=f32)
    query_grad = rotate(query_grad.reshape(GROUP, HEADS_OWN, HD), cosine, -sine)
    key_grad = rotate(key_grad, cosine, -sine)
    mixed_grad = jnp.concatenate(
        [
            query_grad.reshape(GROUP, Q_OWN),
            jnp.stack([key_grad, value_grad], axis=2).reshape(GROUP, KV_OWN),
        ],
        axis=1,
    ).astype(bf16)
    normed_part = dot(mixed_grad, entry_own, ((1,), (1,))).astype(bf16)
    input_grad, gain_one_grad = input_back(
        normed_part.reshape(N_SEQ, TOK_DEV, D), activations[0], middle_grad, gains_full[0:1]
    )

    lane = jnp.arange(128)[None, :]
    shared_grad = jnp.where(lane == EXPERTS, gain_one_grad.T, router_grad)
    shared_grad = jnp.where(lane == EXPERTS + 1, gain_two_grad.T, shared_grad).astype(bf16)
    entry_got, exit_got = sum_to_owners(normed, mixed_grad, attended, branch_grad, shared_grad)
    entry_got = entry_got[:, :ROWS]
    entry_sum = jnp.concatenate(
        [
            entry_got[:, :, :Q_OWN].transpose(1, 0, 2).reshape(ROWS, QH * HD),
            entry_got[:, :, Q_OWN:MIX_OWN].transpose(1, 0, 2).reshape(ROWS, 2 * KVH * HD),
        ],
        axis=1,
    )
    shared_sum = jnp.sum(entry_got[:, :, MIX_OWN:], axis=0)
    router_sum = shared_sum[:, :EXPERTS]
    gains_sum = shared_sum[:, EXPERTS : EXPERTS + 2].T
    exit_sum = exit_got[:, :ROWS].transpose(1, 0, 2).reshape(ROWS, D)

    ends = expert_sum[:, 128:].reshape(LOCAL_E, 16, 2, 512).transpose(2, 0, 1, 3)
    rows_of = jnp.stack(
        [
            jnp.concatenate([expert_sum[:, :48], expert_sum[:, 96:112]], axis=1),
            jnp.concatenate([expert_sum[:, 48:96], expert_sum[:, 112:128]], axis=1),
        ]
    )

    def to_owner(value):
        mine = lax.dynamic_index_in_dim(value, core, 0, keepdims=False)
        other = core_swap(lax.dynamic_index_in_dim(value, 1 - core, 0, keepdims=False))
        return core_order(core, mine, other, 0).astype(f32)

    rows_of, ends = to_owner(rows_of), to_owner(ends)
    expand_sum = rows_of[:, :48]
    shrink_sum = jnp.concatenate([rows_of[:, 48:], ends], axis=2)
    entry_new = adamw_step(entry_weight, entry_sum, entry_mean, entry_square, 0.02, weight_decay)
    exit_new = adamw_step(exit_weight, exit_sum, exit_mean, exit_square, 0.15, weight_decay)
    router_new = adamw_step(
        router_weight, router_sum, router_mean, router_square, 0.01, weight_decay
    )
    expand_new = adamw_step(
        expand_weight, expand_sum, expand_mean, expand_square, 0.02, weight_decay
    )
    shrink_new = adamw_step(
        shrink_weight, shrink_sum, shrink_mean, shrink_square, 0.12, weight_decay
    )
    gains_new = adamw_step(norm_gains, gains_sum, gains_mean, gains_square, 0.5, 0.0)
    return (
        block_output[None],
        input_grad[None],
        *entry_new,
        *exit_new,
        *router_new,
        *expand_new,
        *shrink_new,
        *gains_new,
    )


def solution(mesh):
    fine = Mesh(mesh.devices.reshape(4, 4, 4, 2), ("seq", "x", "y", "core"))
    rows = P(FSDP, "seq", None)
    lists = P(FSDP, None)
    owned = P(("seq",) + FSDP, None)
    experts = P("seq", FSDP, None)
    gains = P(None, ("seq",) + FSDP)
    return jax.shard_map(
        on_device,
        mesh=fine,
        in_specs=(rows, rows, lists, lists, rows)
        + (owned,) * 9
        + (experts,) * 6
        + (gains,) * 3,
        out_specs=(rows, rows) + (owned,) * 9 + (experts,) * 6 + (gains,) * 3,
        check_vma=False,
    )
```

time: 792 us -> 451 us (0.57)
  waiting for transfers between devices: 267 us -> 9.25 us
  Pallas kernels: 177 us -> 287 us
  matrix products: 145 us -> 56.4 us
  local copies, waits for them, and re-layouts: 101 us -> 32.4 us
  other arithmetic: 65.9 us -> 35.2 us
    reduce_scatter x3 -> x0, waiting for transfers between devices: 188 us -> none  [the longest x1 103 us: on_device(): lax.psum_scatter(expand_grad.astype(bf16), PLANE, scatter_dimension=1, ti...]
    pallas_call x9, Pallas kernels: 177 us -> 287 us  [the longest x1 55.8 us: gather_weights(): pl.pallas_call(weights_kernel, out_shape=[jax.ShapeDtypeStruct((D, 640),...]
    dot_general x10 -> x0, matrix products: 86.9 us -> none  [the longest x1 14.4 us: on_device(): jnp.einsum('est,esd->td', pick, row_grad.astype(bf16), preferred_element_...]
    all_gather x3 -> x1, waiting for transfers between devices: 71.8 us -> 0.01 us  [on_device(): weights = lax.all_gather(packed, PLANE, axis=0, tiled=False)]
    reshape x18 -> x9, local copies, waits for them, and re-layouts: 33.1 us -> 2.13 us  [the longest x1 1.69 us: on_device(): expert_sum[:, 128:].reshape(LOCAL_E, 16, 2, 512).transpose(2, 0, 1, 3)]
    slice x19 -> x8, local copies, waits for them, and re-layouts: 23.6 us -> 4.35 us  [the longest x1 1.79 us: on_device(): expert_sum[:, 128:].reshape(LOCAL_E, 16, 2, 512).transpose(2, 0, 1, 3)]
    convert_element_type x16 -> x6, other arithmetic: 18.8 us -> 2.12 us  [the longest x1 1.38 us: on_device(): shrink_b = shrink_weight.astype(bf16)]
    convert_element_type x13 -> x1, local copies, waits for them, and re-layouts: 11.2 us -> 0.92 us  [on_device(): attended = jnp.einsum('hgqk,khd->qhgd', probs_b, values, preferred_elemen...]
  transfers between devices with their start and end apart: 16 -> 11, of which waited for: 9 -> 3; matrix products, arithmetic and copies ran while one was open for 21% -> 23% of each run, Pallas kernels for 9% -> 59%
where the time goes in v2:
time: 451 us; the launch traced here: 444 us
  Pallas kernels  287 us (64%)
  matrix products  56.4 us (13%)
  other arithmetic  35.2 us (8%)
  local copies, waits for them, and re-layouts  32.4 us (7%)
  between operations  15.7 us (3%)
  waiting for transfers between devices  9.25 us (2%)
  starting transfers between devices  8.84 us (2%)
    pallas_call x1, Pallas kernels, gather_weights(): pl.pallas_call(weights_kernel, out_shape=[jax.ShapeDtypeStruct((D, 640),...  55.8 us
    pallas_call x1, Pallas kernels, sum_to_owners(): pl.pallas_call(owners_kernel, out_shape=[jax.ShapeDtypeStruct((4,) + bloc...  39.7 us
    pallas_call x1, Pallas kernels, turn(): pl.pallas_call(turn_kernel, out_shape=[jax.ShapeDtypeStruct((TOK_DEV, D),...  39.5 us
    pallas_call x1, Pallas kernels, middle_tokens(): pl.pallas_call(middle_kernel, out_shape=[jax.ShapeDtypeStruct((TOK_DEV, D...  36.3 us
    pallas_call x1, Pallas kernels, gather_inputs(): pl.pallas_call(inputs_kernel, out_shape=[jax.ShapeDtypeStruct((N_SEQ, TOK...  31.3 us
    pallas_call x1, Pallas kernels, combine(): pl.pallas_call(combine_kernel, grid=(LOCAL_E + 1,), in_specs=[pl.BlockSpe...  26.4 us
    pallas_call x1, Pallas kernels, expert_grads(): pl.pallas_call(grads_kernel, grid=(LOCAL_E,), in_specs=[pl.BlockSpec((1,...  26.3 us
    pallas_call x1, Pallas kernels, input_back(): pl.pallas_call(input_kernel, out_shape=[jax.ShapeDtypeStruct((TOK_DEV, D)...  18.4 us
  transfers between devices with their start and end apart: 11, of which 3 were waited for; matrix products, arithmetic and copies ran while one was open for 23% of the time, Pallas kernels for 59%

profile of v2, /device:TPU:1, one launch (start us, length us, event | category | flops | bytes accessed | tf_op | source)
XLA Modules:
  0.0 444.5 jit_solution(10696597007156703155)
XLA Ops:
  13.5 1.5 collective-permute-done.1
  21.5 55.8 %shard_map.375 = (bf16[1536,640]{1,0:T(8,128)(2,1)}, bf16[1536,128]{1,0:T(8,128)(2,1)}, bf16[384,1536]{1,0:T(8,128)(2,1)}) custom-call(bf16[4,16,768]{2,1,0:T(8,128)(2,1)} %fusion.67.entry_ref, bf16[2,16,768]{2,1,0:T(8,128)(2,1)} %pad.18.exit_ref), custom_call_target="tpu_custom_call" | custom-call | tf_op jit(solution)/shard_map/pallas_call | solution.py:500
  81.3 31.3 %shard_map.374 = (bf16[4,128,1536]{2,1,0:T(8,128)(2,1)}, bf16[2,4,128,1536]{3,2,1,0:T(8,128)(2,1)}, bf16[4,128,128]{2,1,0:T(8,128)(2,1)}) custom-call(bf16[128,1536]{1,0:T(8,128)(2,1)} %bitcast.226, bf16[128,1536]{1,0:T(8,128)(2,1)} %bitcast.244, bf16[128,128]{1,0:T(8,128)(2,1)} %convert_element_type.123.hit_ref), custom_call_target="tpu_custom_call" | custom-call | tf_op jit(solution)/shard_map/pallas_call | solution.py:255
  112.6 1.9 multiply_reduce_fusion
  124.1 6.1 %fusion.104 = (f32[2,3,512]{2,1,0:T(4,128)S(1)}, f32[2,3,512,512]{2,3,1,0:T(8,128)}) fusion(pred[512,512]{0,1:T(8,128)(4,1)} %fusion.35, bf16[512,2,3,32]{0,3,2,1:T(8,128)(2,1)} %bitcast.261, bf16[512,2,3,32]{0,3,2,1:T(8,128)(2,1)} %bitcast.259, bf16[512,2,32]{0,2,1:T(8,128)(2,1)S(1)} %get-tuple-element.211, bf16[512,2,32]{0,2,1:T(8,128)(2,1)S(1)} %get-tuple-element.210), kind=kOutput, calls=%fused_computation.208 | convolution fusion | flops 208667136 | bytes 7090176 | tf_op jit(solution)/shard_map/sub | solution.py:926
  130.2 3.7 fusion.22
  134.7 2.1 convolution_convert_fusion.1
  136.8 36.3 %shard_map.376 = (f32[128,1536]{1,0:T(8,128)}, bf16[2,4,128,1536]{3,2,1,0:T(8,128)(2,1)}) custom-call(bf16[4,128,1536]{2,1,0:T(8,128)(2,1)} %bitcast.225, bf16[128,1536]{1,0:T(8,128)(2,1)} %bitcast.227, f32[1,1536]{1,0:T(1,128)} %get-tuple-element.222.gain_ref), custom_call_target="tpu_custom_call" | custom-call | tf_op jit(solution)/shard_map/pallas_call | solution.py:296
  174.1 2.9 fusion.93
  184.1 13.1 %shard_map.377 = (bf16[5,256,1536]{2,1,0:T(8,128)(2,1)}, bf16[5,256,1536]{2,1,0:T(8,128)(2,1)}, f32[5,256,1]{2,1,0:T(8,128)}) custom-call(s32[5,1,1024]{2,1,0:T(1,128)} %copy.230.rank_ref, f32[5,1,1024]{2,1,0:T(1,128)} %copy.231.gate_ref, bf16[1024,1536]{1,0:T(8,128)(2,1)} %bitcast.273, bf16[1024,1536]{1,0:T(8,128)(2,1)} %bitcast.274), custom_call_target="tpu_custom_call" | custom-call | flops 8053063680 | bytes 16777216 | tf_op jit(solution)/shard_map/pallas_call | solution.py:642
  197.3 26.3 %shard_map.378 = (bf16[5,256,512]{2,1,0:T(8,128)(2,1)}, bf16[5,256,1024]{2,1,0:T(8,128)(2,1)}, bf16[16,5,144,1024]{3,2,1,0:T(8,128)(2,1)}) custom-call(bf16[5,256,1536]{2,1,0:T(8,128)(2,1)} %get-tuple-element.57.rows_ref, bf16[5,256,1536]{2,1,0:T(8,128)(2,1)} %get-tuple-element.58.cot_ref, f32[5,256,1]{2,1,0:T(8,128)} %get-tuple-element.59.gate_ref, ...), custom_call_target="tpu_custom_call" | custom-call | flops 12079595520 | bytes 62914560 | tf_op jit(solution)/shard_map/pallas_call | solution.py:700
  226.1 26.4 %shard_map.379 = (bf16[1024,1664]{1,0:T(8,128)(2,1)}, bf16[1024,1536]{1,0:T(8,128)(2,1)}) custom-call(s32[1]{0:T(128)} %bitcast.28.first_ref, s32[1024,5]{1,0:T(8,128)} %copy-done.10, bf16[5,256,1024]{2,1,0:T(8,128)(2,1)} %get-tuple-element.61.up_ref, bf16[5,256,512]{2,1,0:T(8,128)(2,1)} %get-tuple-element.62.hidden_ref, ...), custom_call_target="tpu_custom_call" | custom-call | flops 14092861440 | bytes 41943040 | tf_op jit(solution)/shard_map/pallas_call | solution.py:761
  252.5 39.5 %shard_map.380 = (f32[128,1536]{1,0:T(8,128)}, bf16[4,128,1536]{2,1,0:T(8,128)(2,1)}, bf16[128,128]{1,0:T(8,128)(2,1)}, f32[1,1536]{1,0:T(1,128)}) custom-call(bf16[2,4,128,1664]{3,2,1,0:T(8,128)(2,1)} %bitcast.229, f32[128,1536]{1,0:T(8,128)} %get-tuple-element.53.middle_ref, bf16[128,1536]{1,0:T(8,128)(2,1)} %bitcast.245, f32[128,128]{1,0:T(8,128)} %pad.19.gate_ref, ...), custom_call_target="tpu_custom_call" | custom-call | tf_op jit(solution)/shard_map/pallas_call | solution.py:364
  292.1 2.3 convolution_convert_fusion.2
  295.1 3.8 fusion.68
  298.8 11.6 %fusion.14 = f32[2,64,3,512]{3,1,2,0:T(8,128)S(1)} fusion(f32[2,512,512,3]{2,1,3,0:T(8,128)} %fusion.68, bf16[512,2,32]{0,2,1:T(8,128)(2,1)S(1)} %get-tuple-element.211, bf16[512,2,32]{0,2,1:T(8,128)(2,1)S(1)} %get-tuple-element.210, f32[2,3,512,512]{2,3,1,0:T(8,128)} %get-tuple-element.227, f32[2,3,512]{2,1,0:T(4,128)S(1)} %get-tuple-element.226), kind=kOutput, calls=%fused_computation.25 | convolution fusion | flops 212602368 | bytes 13512704 | tf_op jit(solution)/shard_map/hgqk,khd->qhgd/dot_general | solution.py:982
  311.4 11.0 %fusion.28 = f32[512,2,64]{0,2,1:T(8,128)S(1)} fusion(f32[2,512,512,3]{2,1,3,0:T(8,128)} %fusion.68, bf16[512,2,3,32]{0,3,2,1:T(8,128)(2,1)} %bitcast.262, bf16[512,2,3,32]{0,3,2,1:T(8,128)(2,1)S(1)} %bitcast.260, f32[2,3,512,512]{2,3,1,0:T(8,128)} %get-tuple-element.227, f32[2,3,512]{2,1,0:T(4,128)S(1)} %copy-done.53), kind=kOutput, calls=%fused_computation.50 | convolution fusion | flops 213126656 | bytes 13250560 | tf_op jit(solution)/shard_map/hgqk,qhgd->khd/dot_general | solution.py:983
  322.5 4.0 fusion.32
  326.7 4.2 convolution_convert_fusion
  330.9 18.4 %shard_map.381 = (bf16[128,1536]{1,0:T(8,128)(2,1)}, f32[1,1536]{1,0:T(1,128)}) custom-call(bf16[4,128,1536]{2,1,0:T(8,128)(2,1)} %bitcast.240, bf16[128,1536]{1,0:T(8,128)(2,1)} %bitcast.228, f32[128,1536]{1,0:T(8,128)} %get-tuple-element.66.grad_ref, f32[1,1536]{1,0:T(1,128)} %get-tuple-element.220.gain_ref), custom_call_target="tpu_custom_call" | custom-call | tf_op jit(solution)/shard_map/pallas_call | solution.py:404
  351.0 2.3 fusion.16.shared_ref
  353.3 39.7 %shard_map.382 = (f32[4,16,768]{2,1,0:T(8,128)}, f32[2,16,768]{2,1,0:T(8,128)}) custom-call(bf16[512,1536]{1,0:T(8,128)(2,1)} %copy-done.1, bf16[512,640]{1,0:T(8,128)(2,1)} %pad_maximum_fusion.1.mixed_ref, bf16[512,384]{1,0:T(8,128)(2,1)} %copy.238.attended_ref, bf16[512,1536]{1,0:T(8,128)(2,1)} %bitcast.239, bf16[1536,128]{1,0:T(8,128)(2,1)} %fusion.16.shared_ref), custom_call_target="tpu_custom_call" | custom-call | tf_op jit(solution)/shard_map/pallas_call | solution.py:601
  395.0 1.6 dynamic-slice_bitcast_fusion
  396.6 1.6 collective-permute-start.3
  403.6 2.2 collective-permute-start.5
  405.8 1.7 collective-permute-start.6
  408.7 1.8 fusion.101
  413.6 1.7 reshape.335
  416.7 7.1 %collective-permute-done.5 = bf16[128,1536]{1,0:T(8,128)(2,1)} collective-permute-done((bf16[128,1536]{1,0:T(8,128)(2,1)}, bf16[128,1536]{1,0:T(8,128)(2,1)}, u32[]{:S(2)}, u32[]{:S(2)}) %collective-permute-start.5) | collective-permute-done | bytes 393248 | tf_op jit(solution)/shard_map/ppermute | solution.py:973
  424.4 2.4 fusion.53
  430.6 3.7 multiply_subtract_fusion
  434.3 2.1 multiply_subtract_fusion.1
  (247 shorter events, 58.7 us)
Async XLA Ops:
  7.2 190.0 %all-gather.3.cloned.1.call-start = ((), (), s32[]{:S(2)}) async-start(), calls=%async_computation.1 | async-start | bytes 25067520 | tf_op jit(solution)/shard_map/all_gather | solution.py:876
  10.5 4.5 %collective-permute-start = (bf16[5,64,1024]{2,1,0:T(8,128)(2,1)}, bf16[5,64,1024]{2,1,0:T(8,128)(2,1)}, u32[]{:S(2)}, u32[]{:S(2)}) collective-permute-start(bf16[5,64,1024]{2,1,0:T(8,128)(2,1)} %fusion.43), channel_id=1, source_target_pairs={{0,1},{1,0},{2,3},{3,2},{4,5},{5,4},{6,7},{7,6},{8,9},{9,8},{10,11... | collective-permute-start | bytes 1966088 | tf_op jit(solution)/shard_map/ppermute | solution.py:795
  13.5 1.5 collective-permute-start.1
  17.8 60.7 %copy-start.50 = (s32[1,3]{1,0:T(1,128)S(1)}, s32[1,3]{1,0:T(1,128)}, u32[]{:S(2)}) copy-start(s32[1,3]{1,0:T(1,128)} %param.25) | copy-start | bytes 40
  17.8 389.7 %reduce-scatter.4.cloned.1.call-start = ((), (), s32[]{:S(2)}) async-start(), calls=%async_computation.2 | async-start | bytes 25067520
  119.7 53.5 %collective-permute-start.2 = (bf16[512,128]{1,0:T(8,128)(2,1)}, bf16[512,128]{1,0:T(8,128)(2,1)}, u32[]{:S(2)}, u32[]{:S(2)}) collective-permute-start(bf16[512,128]{1,0:T(8,128)(2,1)} %convolution_convert_fusion.3), channel_id=1, source_target_pairs={{0,1},{1,0},{2,3},{3,2},{4,5},{5,4},{6,7},{7,6},{8,9},{9,8},{10,11... | collective-permute-start | bytes 393224 | tf_op jit(solution)/shard_map/ppermute | solution.py:795
  122.0 8.1 %copy-start.11 = (f32[512,256]{0,1:T(8,128)}, f32[512,256]{0,1:T(8,128)S(1)}, u32[]{:S(2)}) copy-start(f32[512,256]{0,1:T(8,128)S(1)} %copy.222) | copy-start | bytes 1572868
  130.2 168.7 %copy-start.52 = (f32[2,3,512]{2,1,0:T(4,128)}, f32[2,3,512]{2,1,0:T(4,128)S(1)}, u32[]{:S(2)}) copy-start(f32[2,3,512]{2,1,0:T(4,128)S(1)} %get-tuple-element.226) | copy-start | bytes 36868
  136.8 37.3 %copy-start.19 = (bf16[1536,128]{1,0:T(8,128)(2,1)S(1)}, bf16[1536,128]{1,0:T(8,128)(2,1)}, u32[]{:S(2)}) copy-start(bf16[1536,128]{1,0:T(8,128)(2,1)} %get-tuple-element.50.router_ref) | copy-start | bytes 1179652
  183.3 13.9 %copy-start.10 = (s32[1024,5]{1,0:T(8,128)}, s32[1024,5]{1,0:T(8,128)S(1)}, u32[]{:S(2)}) copy-start(s32[1024,5]{1,0:T(8,128)S(1)} %bitcast_select_fusion.4.rank_ref) | copy-start | bytes 61444
  252.5 39.5 %copy-start.21 = (bf16[384,1536]{1,0:T(8,128)(2,1)S(1)}, bf16[384,1536]{1,0:T(8,128)(2,1)}, u32[]{:S(2)}) copy-start(bf16[384,1536]{1,0:T(8,128)(2,1)} %get-tuple-element.52) | copy-start | bytes 3538948
  298.8 11.6 %copy-start.25 = (f32[512,32]{0,1:T(8,128)S(1)}, f32[512,32]{0,1:T(8,128)}, u32[]{:S(2)}) copy-start(f32[512,32]{0,1:T(8,128)} %get-tuple-element.223) | copy-start | bytes 196612
  311.4 11.1 %copy-start.31 = (bf16[512,384]{0,1:T(8,128)(2,1)S(1)}, bf16[512,384]{0,1:T(8,128)(2,1)}, u32[]{:S(2)}) copy-start(bf16[512,384]{0,1:T(8,128)(2,1)} %copy-done.30) | copy-start | bytes 1179652
  311.4 11.1 %copy-start.54 = (f32[2,3,512]{2,1,0:T(4,128)S(1)}, f32[2,3,512]{2,1,0:T(4,128)}, u32[]{:S(2)}) copy-start(f32[2,3,512]{2,1,0:T(4,128)} %copy-done.52) | copy-start | bytes 36868
  330.9 19.2 %copy-start.41 = (f32[1,1536]{1,0:T(1,128)S(1)}, f32[1,1536]{1,0:T(1,128)}, u32[]{:S(2)}) copy-start(f32[1,1536]{1,0:T(1,128)} %get-tuple-element.68) | copy-start | bytes 18436
  330.9 20.1 %copy-start.48 = (bf16[128,128]{1,0:T(8,128)(2,1)S(1)}, bf16[128,128]{1,0:T(8,128)(2,1)}, u32[]{:S(2)}) copy-start(bf16[128,128]{1,0:T(8,128)(2,1)} %get-tuple-element.70) | copy-start | bytes 98308
  330.9 20.1 %copy-start.51 = (pred[128]{0:T(512)(128)(4,1)S(1)}, pred[128]{0:T(512)(128)(4,1)}, u32[]{:S(2)}) copy-start(pred[128]{0:T(512)(128)(4,1)} %get-tuple-element.231) | copy-start | bytes 388
  394.9 5.7 %copy-start.29 = (f32[12,1536]{1,0:T(8,128)S(1)}, f32[12,1536]{1,0:T(8,128)}, u32[]{:S(2)}) copy-start(f32[12,1536]{1,0:T(8,128)} %param.31) | copy-start | bytes 221188
  394.9 5.7 %copy-start.36 = (f32[12,1536]{1,0:T(8,128)S(1)}, f32[12,1536]{1,0:T(8,128)}, u32[]{:S(2)}) copy-start(f32[12,1536]{1,0:T(8,128)} %param.33) | copy-start | bytes 221188
  394.9 5.6 %copy-start.37 = (f32[12,1536]{1,0:T(8,128)S(1)}, f32[12,1536]{1,0:T(8,128)}, u32[]{:S(2)}) copy-start(f32[12,1536]{1,0:T(8,128)} %param.32) | copy-start | bytes 221188
  394.9 6.4 %copy-start.24 = (f32[12,2560]{1,0:T(8,128)S(1)}, f32[12,2560]{1,0:T(8,128)}, u32[]{:S(2)}) copy-start(f32[12,2560]{1,0:T(8,128)} %param.28) | copy-start | bytes 368644
  394.9 6.4 %copy-start.33 = (f32[12,2560]{1,0:T(8,128)S(1)}, f32[12,2560]{1,0:T(8,128)}, u32[]{:S(2)}) copy-start(f32[12,2560]{1,0:T(8,128)} %param.30) | copy-start | bytes 368644
  395.0 6.4 %copy-start.34 = (f32[12,2560]{1,0:T(8,128)S(1)}, f32[12,2560]{1,0:T(8,128)}, u32[]{:S(2)}) copy-start(f32[12,2560]{1,0:T(8,128)} %param.29) | copy-start | bytes 368644
  396.6 5.6 %copy-start.8 = (bf16[1024,1536]{1,0:T(8,128)(2,1)S(1)}, bf16[1024,1536]{1,0:T(8,128)(2,1)}, u32[]{:S(2)}) copy-start(bf16[1024,1536]{1,0:T(8,128)(2,1)} %get-tuple-element.63) | copy-start | bytes 9437188
  396.6 5.6 %collective-permute-start.3 = (bf16[512,1536]{1,0:T(8,128)(2,1)S(1)}, bf16[512,1536]{1,0:T(8,128)(2,1)S(1)}, u32[]{:S(2)}, u32[]{:S(2)}) collective-permute-start(bf16[512,1536]{1,0:T(8,128)(2,1)S(1)} %dynamic-slice_bitcast_fusion), channel_id=1, source_target_pairs={{0,1},{1,0},{2,3},{3,2},{4,5},{5,4},{6,7},{7,6},{8,9},{9,8},{10,11... | collective-permute-start | bytes 4718600 | tf_op jit(solution)/shard_map/ppermute | solution.py:795
  403.6 13.1 %collective-permute-start.4 = (bf16[128,1536]{1,0:T(8,128)(2,1)}, bf16[128,1536]{1,0:T(8,128)(2,1)}, u32[]{:S(2)}, u32[]{:S(2)}) collective-permute-start(bf16[128,1536]{1,0:T(8,128)(2,1)} %get-tuple-element.196), channel_id=1, source_target_pairs={{0,32},{32,64},{64,96},{96,0},{1,33},{33,65},{65,97},{97,1},{2,34}... | collective-permute-start | bytes 1179656 | tf_op jit(solution)/shard_map/ppermute | solution.py:973
  403.6 20.2 %collective-permute-start.5 = (bf16[128,1536]{1,0:T(8,128)(2,1)}, bf16[128,1536]{1,0:T(8,128)(2,1)}, u32[]{:S(2)}, u32[]{:S(2)}) collective-permute-start(bf16[128,1536]{1,0:T(8,128)(2,1)} %get-tuple-element.198), channel_id=1, source_target_pairs={{0,64},{32,96},{64,0},{96,32},{1,65},{33,97},{65,1},{97,33},{2,66}... | collective-permute-start | bytes 1179656 | tf_op jit(solution)/shard_map/ppermute | solution.py:973
  405.8 18.6 %collective-permute-start.6 = (bf16[128,1536]{1,0:T(8,128)(2,1)}, bf16[128,1536]{1,0:T(8,128)(2,1)}, u32[]{:S(2)}, u32[]{:S(2)}) collective-permute-start(bf16[128,1536]{1,0:T(8,128)(2,1)} %get-tuple-element.197), channel_id=1, source_target_pairs={{0,96},{32,0},{64,32},{96,64},{1,97},{33,1},{65,33},{97,65},{2,98}... | collective-permute-start | bytes 1179656 | tf_op jit(solution)/shard_map/ppermute | solution.py:973
  412.5 14.4 %collective-permute-start.7 = (bf16[5,64,1024]{2,1,0:T(8,128)(2,1)}, bf16[5,64,1024]{2,1,0:T(8,128)(2,1)}, u32[]{:S(2)}, u32[]{:S(2)}) collective-permute-start(bf16[5,64,1024]{2,1,0:T(8,128)(2,1)} %fusion.46), channel_id=1, source_target_pairs={{0,1},{1,0},{2,3},{3,2},{4,5},{5,4},{6,7},{7,6},{8,9},{9,8},{10,11... | collective-permute-start | bytes 1966088 | tf_op jit(solution)/shard_map/ppermute | solution.py:795
  416.6 10.4 %copy-start.4 = (bf16[1,5,64,1024]{3,2,1,0:T(8,128)(2,1)S(1)}, bf16[1,5,64,1024]{3,2,1,0:T(8,128)(2,1)}, u32[]{:S(2)}) copy-start(bf16[1,5,64,1024]{3,2,1,0:T(8,128)(2,1)} %copy-done.3) | copy-start | bytes 1966084
  416.6 10.4 %copy-start.6 = (bf16[1,5,64,1024]{3,2,1,0:T(8,128)(2,1)S(1)}, bf16[1,5,64,1024]{3,2,1,0:T(8,128)(2,1)}, u32[]{:S(2)}) copy-start(bf16[1,5,64,1024]{3,2,1,0:T(8,128)(2,1)} %copy-done.5) | copy-start | bytes 1966084
  416.6 10.2 %collective-permute-start.8 = (bf16[5,16,512]{2,1,0:T(8,128)(2,1)S(1)}, bf16[5,16,512]{2,1,0:T(8,128)(2,1)S(1)}, u32[]{:S(2)}, u32[]{:S(2)}) collective-permute-start(bf16[5,16,512]{2,1,0:T(8,128)(2,1)S(1)} %bitcast.266), channel_id=1, source_target_pairs={{0,1},{1,0},{2,3},{3,2},{4,5},{5,4},{6,7},{7,6},{8,9},{9,8},{10,11... | collective-permute-start | bytes 245768 | tf_op jit(solution)/shard_map/ppermute | solution.py:795
  (34 other events, 87.0 us)
Sparse Core Ops, SparseCore 0:
  17.9 160.5 all-gather.2
  223.7 141.9 reduce-scatter.3

commit v3 on v2

v3 whole, which is shorter than its diff:
```python
import jax
import jax.numpy as jnp
from jax import lax
from jax.experimental import pallas as pl
from jax.experimental.pallas import tpu as pltpu
from jax.sharding import Mesh, PartitionSpec as P

D = 1536
QH = 24
KVH = 8
HD = 64
FF = 512
EXPERTS = 40
TOP = 8
STEP = 10
CAP = 29

N_SEQ = 4
TOK_DEV = 128
GROUP = 512
PAIR_TOK = 2 * GROUP
LOCAL_E = EXPERTS // (2 * N_SEQ)
SLOTS = 256
Q_OWN = QH * HD // N_SEQ
KV_OWN = 2 * KVH * HD // N_SEQ
MIX_OWN = Q_OWN + KV_OWN
HEADS_OWN = QH // N_SEQ
KV_HEADS_OWN = KVH // N_SEQ
PER_KV = QH // KVH
ROWS = 12

norm_eps = 1e-06
rope_base = 10000.0
beta_first = 0.9
beta_second = 0.95
adam_eps = 1e-08
weight_decay = 0.1

FSDP = ("x", "y", "core")
PLANE = ("x", "y")
f32 = jnp.float32
bf16 = jnp.bfloat16


BIG = 56 * 1024 * 1024
HALF = TOK_DEV // 2
QOWN = Q_OWN
MESH = pl.DeviceIdType.MESH
ANY = pl.BlockSpec(memory_space=pl.ANY)
VMEM = pl.BlockSpec(memory_space=pltpu.VMEM)


def dot(a, b, dims):
    return lax.dot_general(a, b, (dims, ((), ())), preferred_element_type=f32)


def greet(peers):
    barrier = pltpu.get_barrier_semaphore()
    for axis, peer in peers:
        pl.semaphore_signal(barrier, inc=1, device_id={axis: peer}, device_id_type=MESH)
    pl.semaphore_wait(barrier, len(peers))


def sender(send_sem, recv_sem):
    def send(src, dst, index, axis, peer):
        copy = pltpu.make_async_remote_copy(
            src_ref=src,
            dst_ref=dst,
            send_sem=send_sem.at[index],
            recv_sem=recv_sem.at[index],
            device_id={axis: peer},
            device_id_type=MESH,
        )
        copy.start()
        return copy

    return send


def sems(count):
    return [pltpu.SemaphoreType.DMA((count,)), pltpu.SemaphoreType.DMA((count,))]


def ring(me):
    right, left = lax.rem(me + 1, 4), lax.rem(me + 3, 4)
    return right, left, lax.rem(me + 2, 4)


def near(axis):
    right, left, _ = ring(lax.axis_index(axis))
    return [(axis, right), (axis, left)]


def sibling():
    return ("core", 1 - lax.axis_index("core"))


def half_rows(ref, half):
    size = ref.shape[0] // 2
    return ref.at[pl.ds(half * size, size)]


def half_lanes(ref, half):
    size = ref.shape[-1] // 2
    return ref.at[(slice(None),) * (len(ref.shape) - 1) + (pl.ds(half * size, size),)]


class Gather:
    def __init__(self, send, base, axis, mine, slot, cut):
        self.send, self.base, self.axis, self.slot, self.cut = send, base, axis, slot, cut
        me = lax.axis_index(axis)
        self.right, self.left, self.far = ring(me)
        here = slot(me)
        self.first = [
            send(cut(mine, 0), cut(here, 0), base, axis, self.right),
            send(cut(mine, 1), cut(here, 1), base + 1, axis, self.left),
            send(cut(mine, 1), cut(here, 1), base + 2, axis, self.right),
            send(cut(mine, 0), cut(here, 0), base + 3, axis, self.left),
        ]
        self.later = []

    def relay(self):
        self.first[0].wait_recv()
        part = self.cut(self.slot(self.left), 0)
        self.later.append(self.send(part, part, self.base + 4, self.axis, self.right))
        self.first[1].wait_recv()
        part = self.cut(self.slot(self.right), 1)
        self.later.append(self.send(part, part, self.base + 5, self.axis, self.left))

    def wait_left(self):
        self.first[2].wait_recv()

    def wait_right(self):
        self.first[3].wait_recv()

    def wait_far(self):
        for copy in self.later:
            copy.wait_recv()

    def finish(self):
        self.wait_left()
        self.wait_right()
        self.wait_far()

    def drain(self):
        for copy in self.first + self.later:
            copy.wait_send()


def hand_over(send, base, mine, out, gather):
    me, core = lax.axis_index("seq"), lax.axis_index("core")
    other = 1 - core
    copies = [send(mine, out.at[core, me], base, "core", other)]
    gather.relay()
    gather.wait_left()
    block = out.at[core, gather.left]
    copies.append(send(block, block, base + 1, "core", other))
    gather.wait_right()
    block = out.at[core, gather.right]
    copies.append(send(block, block, base + 2, "core", other))
    gather.wait_far()
    block = out.at[core, gather.far]
    copies.append(send(block, block, base + 3, "core", other))
    return copies


def reduce_scratch(block, half):
    return [pltpu.VMEM(half, bf16)] * 4 + [pltpu.VMEM(block, bf16)] * 2


def added(target, first, second):
    target[...] = (first[...].astype(f32) + second[...].astype(f32)).astype(bf16)


class Reduce:
    def __init__(self, send, base, axis, block, bufs, cut):
        self.send, self.base, self.axis, self.block = send, base, axis, block
        self.bufs, self.cut = bufs, cut
        self.me = lax.axis_index(axis)
        self.right, self.left, self.far = ring(self.me)

    def start_far(self):
        far = self.block(self.far)
        self.copies = [
            self.send(self.cut(far, 0), self.bufs[0], self.base, self.axis, self.right),
            self.send(self.cut(far, 1), self.bufs[1], self.base + 1, self.axis, self.left),
        ]

    def start_near(self):
        source, target = self.cut(self.block(self.right), 1), self.cut(self.bufs[4], 1)
        self.copies.append(self.send(source, target, self.base + 2, self.axis, self.right))
        source, target = self.cut(self.block(self.left), 0), self.cut(self.bufs[5], 0)
        self.copies.append(self.send(source, target, self.base + 3, self.axis, self.left))

    def relay(self):
        from_left, from_right, to_right, to_left, got_left, got_right = self.bufs
        self.copies[0].wait_recv()
        added(to_right, self.cut(self.block(self.right), 0), from_left)
        target = self.cut(got_left, 0)
        self.copies.append(self.send(to_right, target, self.base + 4, self.axis, self.right))
        self.copies[1].wait_recv()
        added(to_left, self.cut(self.block(self.left), 1), from_right)
        target = self.cut(got_right, 1)
        self.copies.append(self.send(to_left, target, self.base + 5, self.axis, self.left))

    def total(self):
        for copy in self.copies[2:]:
            copy.wait_recv()
        mine = self.block(self.me)[...].astype(f32)
        return mine + self.bufs[4][...].astype(f32) + self.bufs[5][...].astype(f32)

    def drain(self):
        for copy in self.copies:
            copy.wait_send()


def remote_params(call_id):
    return pltpu.CompilerParams(
        collective_id=call_id, has_side_effects=True, vmem_limit_bytes=BIG
    )


def unit_scale(vector):
    return lax.rsqrt(jnp.mean(vector * vector, axis=-1, keepdims=True) + norm_eps)


def norm_back(vector, gain, grad):
    scale = unit_scale(vector)
    unit = vector * scale
    pulled = grad * gain
    back = scale * (pulled - unit * jnp.mean(pulled * unit, axis=-1, keepdims=True))
    return back, jnp.sum(unit * grad, axis=0, keepdims=True)


def pack_kernel(expand_ref, shrink_ref, out_ref, stage, stage_end, send_sem, recv_sem):
    core = lax.axis_index("core")
    greet([sibling()])
    send = sender(send_sem, recv_sem)
    other = 1 - core
    for e in range(LOCAL_E):
        theirs = other * LOCAL_E + e
        stage[e, :48] = expand_ref[theirs].astype(bf16)
        stage[e, 48:] = shrink_ref[theirs, :, :1024].astype(bf16)
        stage_end[e] = shrink_ref[theirs, :, 1024:].astype(bf16)
    main = pl.ds(pl.multiple_of(core * 48, 16), 48)
    left = pl.ds(pl.multiple_of(96 + core * 16, 16), 16)
    ends = pl.ds(pl.multiple_of(core * 512, 512), 512)
    copies = [
        send(stage.at[:, pl.ds(0, 48)], out_ref.at[:, main], 0, "core", other),
        send(stage.at[:, pl.ds(48, 16)], out_ref.at[:, left], 1, "core", other),
        send(stage_end, out_ref.at[:, pl.ds(128, 16), ends], 2, "core", other),
    ]
    for e in range(LOCAL_E):
        mine = core * LOCAL_E + e
        out_ref[e, main, :] = expand_ref[mine].astype(bf16)
        out_ref[e, left, :] = shrink_ref[mine, :, :1024].astype(bf16)
        out_ref[e, pl.ds(128, 16), ends] = shrink_ref[mine, :, 1024:].astype(bf16)
    for copy in copies:
        copy.wait()


def pack_experts(expand, shrink):
    return pl.pallas_call(
        pack_kernel,
        out_shape=jax.ShapeDtypeStruct((LOCAL_E, 144, 1024), bf16),
        in_specs=[VMEM] * 2,
        out_specs=VMEM,
        scratch_shapes=[
            pltpu.VMEM((LOCAL_E, 64, 1024), bf16),
            pltpu.VMEM((LOCAL_E, 16, 512), bf16),
        ]
        + sems(3),
        compiler_params=remote_params(1),
    )(expand, shrink)


def row_pick(shape, padded_axis):
    padded = lax.broadcasted_iota(jnp.int32, shape, padded_axis)
    plain = lax.broadcasted_iota(jnp.int32, shape, 1 - padded_axis)
    row = lax.rem(padded, 16)
    return ((plain == lax.div(padded, 16) * 12 + row) & (row < 12)).astype(bf16)


def start_kernel(
    in_ref, cot_ref, hit_ref, entry_ref, exit_ref,
    in_all, cot_all, hit_all, entry_out, shared_out, exit_out,
    hold, full, send_sem, recv_sem, copy_sem,
):
    z, x, y, c = (lax.axis_index(a) for a in ("seq", "x", "y", "core"))
    right, left, far = ring(z)
    greet(near("seq") + [("seq", far)] + near("x") + near("y") + [sibling()])
    send = sender(send_sem, recv_sem)
    columns = [
        send(entry_ref.at[peer], hold.at[z], k, "seq", peer)
        for k, peer in enumerate((right, far, left))
    ]
    hits = Gather(send, 3, "seq", hit_ref, lambda i: hit_all.at[i], half_rows)
    rows = Gather(send, 9, "seq", in_ref, lambda i: in_all.at[i], half_rows)
    local = [
        pltpu.make_async_copy(entry_ref.at[z], hold.at[z], copy_sem.at[0]),
        pltpu.make_async_copy(exit_ref, hold.at[pl.ds(4, 2)], copy_sem.at[1]),
        pltpu.make_async_copy(hit_ref, hit_all.at[z], copy_sem.at[2]),
        pltpu.make_async_copy(in_ref, in_all.at[z], copy_sem.at[3]),
        pltpu.make_async_copy(cot_ref, cot_all.at[c, z], copy_sem.at[4]),
    ]
    for copy in local:
        copy.start()
    local[0].wait()
    local[1].wait()
    for copy in columns:
        copy.wait_recv()
    own = pltpu.make_async_copy(hold, full.at[:, x, y, c], copy_sem.at[5])
    own.start()
    low, high = pl.ds(0, 3), pl.ds(3, 3)
    low_x = Gather(send, 15, "x", hold.at[low], lambda i: full.at[low, i, y, c], half_lanes)
    high_y = Gather(send, 21, "y", hold.at[high], lambda i: full.at[high, x, i, c], half_lanes)
    hits.relay()
    low_x.relay()
    high_y.relay()
    rows.relay()
    cots = Gather(send, 27, "seq", cot_ref, lambda i: cot_all.at[c, i], half_rows)
    own.wait()
    low_x.finish()

    def cut_low(ref, half):
        return ref.at[:, pl.ds(2 * half, 2)]

    low_y = Gather(
        send, 33, "y", full.at[low, :, y, c], lambda i: full.at[low, :, i, c], cut_low
    )
    high_y.finish()
    high_x = Gather(
        send, 39, "x", full.at[high, x, :, c], lambda i: full.at[high, i, :, c], cut_low
    )
    low_y.relay()
    high_x.relay()
    pairs = hand_over(send, 45, cot_ref, cot_all, cots)
    low_y.finish()
    half = full.at[low, :, :, c]
    last = [send(half, half, 49, "core", 1 - c)]
    high_x.finish()
    half = full.at[high, :, :, c]
    last.append(send(half, half, 50, "core", 1 - c))
    pick = row_pick((QOWN, 512), 1)
    for copy in last:
        copy.wait_recv()
    for block in range(4):
        got = dot(pick, full[block].reshape(512, WIDE), ((1,), (0,))).astype(bf16)
        entry_out[QOWN * block : QOWN * (block + 1), :] = got[:, :MIX_OWN]
        shared_out[QOWN * block : QOWN * (block + 1), :] = got[:, MIX_OWN:]
    for block in range(2):
        got = dot(pick, full[4 + block].reshape(512, WIDE), ((1,), (0,))).astype(bf16)
        exit_out[:, WIDE * block : WIDE * (block + 1)] = got
    hits.finish()
    rows.finish()
    for copy in pairs:
        copy.wait()
    for gather in (hits, rows, cots, low_x, high_y, low_y, high_x):
        gather.drain()
    for copy in columns + last:
        copy.wait_send()
    for copy in local[2:]:
        copy.wait()


def start(rows, cots, hits, entry_cols, exit_cols):
    return pl.pallas_call(
        start_kernel,
        out_shape=[
            jax.ShapeDtypeStruct((N_SEQ, TOK_DEV, D), bf16),
            jax.ShapeDtypeStruct((2, N_SEQ, TOK_DEV, D), bf16),
            jax.ShapeDtypeStruct((N_SEQ, TOK_DEV, 128), bf16),
            jax.ShapeDtypeStruct((D, MIX_OWN), bf16),
            jax.ShapeDtypeStruct((D, 128), bf16),
            jax.ShapeDtypeStruct((QOWN, D), bf16),
        ],
        in_specs=[ANY] * 3 + [VMEM] * 2,
        out_specs=[ANY] * 3 + [VMEM] * 3,
        scratch_shapes=[
            pltpu.VMEM((6, PAD_ROWS, WIDE), bf16),
            pltpu.VMEM((6, 4, 4, 2, PAD_ROWS, WIDE), bf16),
        ]
        + sems(51)
        + [pltpu.SemaphoreType.DMA((6,))],
        compiler_params=remote_params(2),
    )(rows, cots, hits, entry_cols, exit_cols)


def middle_kernel(part_ref, in_ref, gain_ref, middle_ref, tokens_ref, mine, *rest):
    bufs, (send_sem, recv_sem, copy_sem) = rest[:6], rest[6:]
    me, core = lax.axis_index("seq"), lax.axis_index("core")
    greet(near("seq") + [sibling()])
    send = sender(send_sem, recv_sem)
    reduce = Reduce(send, 0, "seq", lambda i: part_ref.at[i], bufs, half_rows)
    reduce.start_far()
    reduce.start_near()
    reduce.relay()
    middle = in_ref[...].astype(f32) + reduce.total()
    middle_ref[...] = middle
    mine[...] = (middle * unit_scale(middle) * gain_ref[...]).astype(bf16)
    gather = Gather(send, 6, "seq", mine, lambda i: tokens_ref.at[core, i], half_rows)
    local = pltpu.make_async_copy(mine, tokens_ref.at[core, me], copy_sem)
    local.start()
    pairs = hand_over(send, 12, mine, tokens_ref, gather)
    for copy in pairs:
        copy.wait()
    gather.drain()
    reduce.drain()
    local.wait()


def middle_tokens(part, rows, gain):
    return pl.pallas_call(
        middle_kernel,
        out_shape=[
            jax.ShapeDtypeStruct((TOK_DEV, D), f32),
            jax.ShapeDtypeStruct((2, N_SEQ, TOK_DEV, D), bf16),
        ],
        in_specs=[VMEM] * 3,
        out_specs=[VMEM, ANY],
        scratch_shapes=[pltpu.VMEM((TOK_DEV, D), bf16)]
        + reduce_scratch((TOK_DEV, D), (HALF, D))
        + sems(16)
        + [pltpu.SemaphoreType.DMA],
        compiler_params=remote_params(3),
    )(part, rows, gain)


def turn_kernel(
    rank_ref, up_ref, hidden_ref, gate_ref, cot_rows_ref, w_ref,
    middle_ref, cot_ref, my_gate_ref, router_ref, gain_ref,
    grad_ref, branch_ref, logit_ref, gain_grad_ref, out_sum_ref,
    back_s, out_s, other_back, from_core, part, other_out, out_core, mine, *rest
):
    bufs, (send_sem, recv_sem, copy_sem) = rest[:6], rest[6:]
    e = pl.program_id(0)
    me, core = lax.axis_index("seq"), lax.axis_index("core")

    @pl.when(e == 0)
    def _():
        greet(near("seq") + [sibling()])

    @pl.when(e < LOCAL_E)
    def _():
        expand, left, right = weights_of(w_ref)
        at = pl.ds(pl.multiple_of(e * SLOTS, SLOTS), SLOTS)
        back_s[at, :D] = dot(up_ref[0], expand, ((1,), (1,))).astype(bf16)
        hidden = hidden_ref[0]
        expert_out = jnp.concatenate(
            [dot(hidden, left, ((1,), (0,))), dot(hidden, right, ((1,), (0,)))], axis=1
        )
        expert_out = expert_out.astype(bf16).astype(f32)
        gate_grad = jnp.sum(expert_out * cot_rows_ref[0].astype(f32), axis=1, keepdims=True)
        lane = lax.broadcasted_iota(jnp.int32, (SLOTS, 128), 1)
        column = (me * 2 + core) * LOCAL_E + e
        back_s[at, D:] = jnp.where(lane == column, gate_grad, 0.0).astype(bf16)
        out_s[at, :] = (gate_ref[0] * expert_out).astype(bf16)

    @pl.when(e == LOCAL_E)
    def _():
        send = sender(send_sem, recv_sem)
        other = 1 - core
        right, left, far = ring(me)
        slot = lax.broadcasted_iota(jnp.int32, (GROUP, SLOTS), 1)

        def picks(group):
            at = pl.ds(pl.multiple_of(group * GROUP, GROUP), GROUP)
            ranks = rank_ref[at, :]
            return jnp.concatenate(
                [(ranks[:, k : k + 1] == slot).astype(bf16) for k in range(LOCAL_E)], axis=1
            )

        theirs, ours = picks(other), picks(core)
        order = (far, right, left, me)
        other_back[...] = (
            dot(theirs, back_s[...], ((1,), (0,))).astype(bf16).reshape(other_back.shape)
        )
        swaps = [
            send(other_back.at[block], from_core.at[block], 12 + i, "core", other)
            for i, block in enumerate(order)
        ]
        part[...] = dot(ours, back_s[...], ((1,), (0,))).astype(bf16).reshape(part.shape)
        reduce = Reduce(send, 0, "seq", lambda i: part.at[i], bufs, half_rows)
        for i, block in enumerate(order):
            swaps[i].wait_recv()
            added(part.at[block], part.at[block], from_core.at[block])
            if i == 0:
                reduce.start_far()
            if i == 2:
                reduce.start_near()
        other_out[...] = (
            dot(theirs, out_s[...], ((1,), (0,))).astype(bf16).reshape(other_out.shape)
        )
        out_swap = send(other_out, out_core, 16, "core", other)
        reduce.relay()
        out_sum_ref[...] = (
            dot(ours, out_s[...], ((1,), (0,))).astype(bf16).reshape(out_sum_ref.shape)
        )
        total = reduce.total()
        gates, gate_grad = my_gate_ref[...], total[:, D:]
        mean_term = jnp.sum(gates * gate_grad, axis=1, keepdims=True)
        logit_grad = (gates * (gate_grad - mean_term)).astype(bf16)
        logit_ref[...] = logit_grad
        normed_grad = total[:, :D] + dot(logit_grad, router_ref[...], ((1,), (1,)))
        back, gain_grad = norm_back(middle_ref[...], gain_ref[...], normed_grad)
        gain_grad_ref[...] = gain_grad
        middle_grad = cot_ref[...].astype(f32) + back
        grad_ref[...] = middle_grad
        mine[...] = middle_grad.astype(bf16)
        gather = Gather(send, 6, "seq", mine, lambda i: branch_ref.at[i], half_rows)
        local = pltpu.make_async_copy(mine, branch_ref.at[me], copy_sem)
        local.start()
        out_swap.wait_recv()
        added(out_sum_ref, out_sum_ref, out_core)
        gather.relay()
        gather.finish()
        gather.drain()
        reduce.drain()
        for copy in swaps + [out_swap]:
            copy.wait_send()
        local.wait()


BACK_WIDTH = D + 128


def turn(rank, up_grad, hidden, row_gates, cot_rows, weights, middle, cot, gates, router, gain):
    last = LOCAL_E - 1
    one = lambda e: (jnp.minimum(e, last), 0, 0)
    wide = lambda e: (0, jnp.minimum(e, last), 0, 0)
    whole = lambda e: (0, 0)
    blocks = lambda e: (0, 0, 0)
    row_block = pl.BlockSpec((TOK_DEV, D), whole)
    lane_block = pl.BlockSpec((TOK_DEV, 128), whole)
    gain_block = pl.BlockSpec((1, D), whole)
    group = pltpu.VMEM((N_SEQ, TOK_DEV, BACK_WIDTH), bf16)
    group_out = pltpu.VMEM((N_SEQ, TOK_DEV, D), bf16)
    return pl.pallas_call(
        turn_kernel,
        grid=(LOCAL_E + 1,),
        in_specs=[
            pl.BlockSpec((PAIR_TOK, LOCAL_E), whole),
            pl.BlockSpec((1, SLOTS, 2 * FF), one),
            pl.BlockSpec((1, SLOTS, FF), one),
            pl.BlockSpec((1, SLOTS, 1), one),
            pl.BlockSpec((1, SLOTS, D), one),
            pl.BlockSpec((16, 1, 144, 1024), wide),
            row_block,
            row_block,
            lane_block,
            pl.BlockSpec((D, 128), whole),
            gain_block,
        ],
        out_specs=[
            row_block,
            ANY,
            lane_block,
            gain_block,
            pl.BlockSpec((N_SEQ, TOK_DEV, D), blocks),
        ],
        out_shape=[
            jax.ShapeDtypeStruct((TOK_DEV, D), f32),
            jax.ShapeDtypeStruct((N_SEQ, TOK_DEV, D), bf16),
            jax.ShapeDtypeStruct((TOK_DEV, 128), bf16),
            jax.ShapeDtypeStruct((1, D), f32),
            jax.ShapeDtypeStruct((N_SEQ, TOK_DEV, D), bf16),
        ],
        scratch_shapes=[
            pltpu.VMEM((LOCAL_E * SLOTS, BACK_WIDTH), bf16),
            pltpu.VMEM((LOCAL_E * SLOTS, D), bf16),
            group,
            group,
            group,
            group_out,
            group_out,
            pltpu.VMEM((TOK_DEV, D), bf16),
        ]
        + reduce_scratch((TOK_DEV, BACK_WIDTH), (HALF, BACK_WIDTH))
        + sems(17)
        + [pltpu.SemaphoreType.DMA],
        compiler_params=remote_params(4),
        cost_estimate=pl.CostEstimate(
            flops=6 * LOCAL_E * SLOTS * D * FF + 4 * LOCAL_E * SLOTS * PAIR_TOK * D,
            bytes_accessed=40 << 20,
            transcendentals=0,
        ),
    )(rank, up_grad, hidden, row_gates, cot_rows, weights, middle, cot, gates, router, gain)


PAD_ROWS = 16
WIDE = 768
HALF_WIDE = 2304


def closing_kernel(
    part_ref, in_ref, grad_ref, gain_ref, normed_ref, mixed_ref, attended_ref, branch_ref,
    router_grad_ref, gain_two_ref, out_sum_ref, middle_ref,
    input_ref, block_ref, entry_out, exit_out,
    full, from_core, chip, line, final, give, got_z, *rest
):
    bufs, (send_sem, recv_sem) = [rest[6 * i : 6 * i + 6] for i in range(6)], rest[36:]
    z, x, y, c = (lax.axis_index(a) for a in ("seq", "x", "y", "core"))
    right, left, far = ring(z)
    greet(near("seq") + [("seq", far)] + near("x") + near("y") + [sibling()])
    send = sender(send_sem, recv_sem)
    rows = Reduce(send, 0, "seq", lambda i: part_ref.at[i], bufs[0], half_rows)
    rows.start_far()
    rows.start_near()
    pick = row_pick((512, QOWN), 0)

    def spread(grad):
        wide = dot(pick, grad, ((1,), (0,))).astype(bf16)
        return wide.reshape(16, 2, PAD_ROWS, grad.shape[1])

    def swap(side):
        return send(full.at[side, :, 1 - c], from_core.at[side], 36 + side, "core", 1 - c)

    def entry_rows(block):
        rows_of = slice(QOWN * block, QOWN * (block + 1))
        grad = dot(normed_ref[:, rows_of], mixed_ref[...], ((0,), (0,))).astype(bf16)
        return spread(grad)

    for block in range(3):
        cols = slice(512 * block, 512 * (block + 1))
        grad = dot(attended_ref[...], branch_ref[:, cols], ((0,), (0,))).astype(bf16)
        full[0, :, :, :, cols] = spread(grad)
    full[0, :, :, :, 1536:2176] = entry_rows(0)
    second = entry_rows(1)
    full[0, :, :, :, 2176:2304] = second[..., :128]
    swaps = [swap(0)]
    rows.relay()
    full[1, :, :, :, :512] = second[..., 128:]
    full[1, :, :, :, 512:1152] = entry_rows(2)
    full[1, :, :, :, 1152:1792] = entry_rows(3)
    back, gain_one = norm_back(in_ref[...].astype(f32), gain_ref[...], rows.total())
    input_ref[...] = (grad_ref[...] + back).astype(bf16)
    row_of = lax.broadcasted_iota(jnp.int32, (128, D), 0)
    gains = jnp.where(row_of == EXPERTS, gain_one, 0.0)
    gains = jnp.where(row_of == EXPERTS + 1, gain_two_ref[...], gains)
    shared = router_grad_ref[...] + gains.T
    for block in range(4):
        part = shared[QOWN * block : QOWN * (block + 1), :].astype(bf16)
        full[1, :, :, :, 1792 + 128 * block : 1920 + 128 * block] = spread(part)
    swaps.append(swap(1))
    outs = Reduce(send, 6, "seq", lambda i: out_sum_ref.at[i], bufs[1], half_rows)
    outs.start_far()
    outs.start_near()
    swaps[0].wait_recv()
    for plane in range(16):
        added(chip.at[0, plane // 4, plane % 4], full.at[0, plane, c], from_core.at[0, plane])
    low_x = Reduce(send, 12, "x", lambda i: chip.at[0, i], bufs[2], half_rows)
    low_x.start_far()
    low_x.start_near()
    swaps[1].wait_recv()
    for plane in range(16):
        added(chip.at[1, plane % 4, plane // 4], full.at[1, plane, c], from_core.at[1, plane])
    high_y = Reduce(send, 18, "y", lambda i: chip.at[1, i], bufs[3], half_rows)
    high_y.start_far()
    high_y.start_near()
    low_x.relay()
    high_y.relay()
    outs.relay()
    line[0] = low_x.total().astype(bf16)
    low_y = Reduce(send, 24, "y", lambda i: line.at[0, i], bufs[4], half_lanes)
    low_y.start_far()
    low_y.start_near()
    line[1] = high_y.total().astype(bf16)
    high_x = Reduce(send, 30, "x", lambda i: line.at[1, i], bufs[5], half_lanes)
    high_x.start_far()
    high_x.start_near()
    low_y.relay()
    high_x.relay()
    block_ref[...] = (middle_ref[...] + outs.total()).astype(bf16)
    final[0] = low_y.total()
    final[1] = high_x.total()
    exit_out[...] = final[0, :, :1536]
    give[0, :, :MIX_OWN] = final[0, :, 1536:2176]
    give[1, :, :128] = final[0, :, 2176:2304]
    give[1, :, 128:MIX_OWN] = final[1, :, :512]
    give[2, :, :MIX_OWN] = final[1, :, 512:1152]
    give[3, :, :MIX_OWN] = final[1, :, 1152:1792]
    for block in range(4):
        give[block, :, MIX_OWN:] = final[1, :, 1792 + 128 * block : 1920 + 128 * block]
    peers = (right, far, left)
    home = [
        send(give.at[peer], got_z.at[k], 38 + k, "seq", peer) for k, peer in enumerate(peers)
    ]
    entry_out[z] = give[z]
    for k, source in enumerate((left, far, right)):
        home[k].wait_recv()
        entry_out[source] = got_z[k]
    for copy in swaps + home:
        copy.wait_send()
    for reduce in (rows, outs, low_x, high_y, low_y, high_x):
        reduce.drain()


def closing(*operands):
    row_bufs = reduce_scratch((TOK_DEV, D), (HALF, D))
    chip_bufs = reduce_scratch((4, PAD_ROWS, HALF_WIDE), (2, PAD_ROWS, HALF_WIDE))
    line_bufs = reduce_scratch((PAD_ROWS, HALF_WIDE), (PAD_ROWS, HALF_WIDE // 2))
    tile = (PAD_ROWS, HALF_WIDE)
    return pl.pallas_call(
        closing_kernel,
        out_shape=[
            jax.ShapeDtypeStruct((TOK_DEV, D), bf16),
            jax.ShapeDtypeStruct((TOK_DEV, D), bf16),
            jax.ShapeDtypeStruct((4, PAD_ROWS, WIDE), f32),
            jax.ShapeDtypeStruct((PAD_ROWS, D), f32),
        ],
        in_specs=[VMEM] * 12,
        out_specs=[VMEM] * 4,
        scratch_shapes=[
            pltpu.VMEM((2, 16, 2) + tile, bf16),
            pltpu.VMEM((2, 16) + tile, bf16),
            pltpu.VMEM((2, 4, 4) + tile, bf16),
            pltpu.VMEM((2, 4) + tile, bf16),
            pltpu.VMEM((2,) + tile, f32),
            pltpu.VMEM((4, PAD_ROWS, WIDE), f32),
            pltpu.VMEM((3, PAD_ROWS, WIDE), f32),
        ]
        + row_bufs * 2
        + chip_bufs * 2
        + line_bufs * 2
        + sems(41),
        compiler_params=remote_params(5),
    )(*operands)


def dispatch_kernel(rank_ref, gate_ref, tokens_ref, cots_ref, rows_ref, cot_rows_ref, row_gate_ref):
    slot = lax.broadcasted_iota(jnp.int32, (SLOTS, PAIR_TOK), 0)
    match = rank_ref[0] == slot
    row_gate_ref[0] = jnp.sum(jnp.where(match, gate_ref[0], 0.0), axis=1, keepdims=True)
    pick = match.astype(bf16)
    for j in range(3):
        cols = slice(512 * j, 512 * (j + 1))
        rows_ref[0, :, cols] = dot(pick, tokens_ref[:, cols], ((1,), (0,))).astype(bf16)
        cot_rows_ref[0, :, cols] = dot(pick, cots_ref[:, cols], ((1,), (0,))).astype(bf16)

def dispatch(rank, gates, tokens, cots):
    one = lambda e: (e, 0, 0)
    whole = lambda e: (0, 0)
    return pl.pallas_call(
        dispatch_kernel,
        grid=(LOCAL_E,),
        in_specs=[
            pl.BlockSpec((1, 1, PAIR_TOK), one),
            pl.BlockSpec((1, 1, PAIR_TOK), one),
            pl.BlockSpec((PAIR_TOK, D), whole),
            pl.BlockSpec((PAIR_TOK, D), whole),
        ],
        out_specs=[
            pl.BlockSpec((1, SLOTS, D), one),
            pl.BlockSpec((1, SLOTS, D), one),
            pl.BlockSpec((1, SLOTS, 1), one),
        ],
        out_shape=[
            jax.ShapeDtypeStruct((LOCAL_E, SLOTS, D), bf16),
            jax.ShapeDtypeStruct((LOCAL_E, SLOTS, D), bf16),
            jax.ShapeDtypeStruct((LOCAL_E, SLOTS, 1), f32),
        ],
        compiler_params=pltpu.CompilerParams(vmem_limit_bytes=BIG),
        cost_estimate=pl.CostEstimate(
            flops=4 * LOCAL_E * SLOTS * PAIR_TOK * D, bytes_accessed=16 << 20, transcendentals=0
        ),
    )(rank[:, None], gates[:, None], tokens, cots)

def weights_of(w_ref):
    expand = w_ref[:, 0, :96, :].reshape(D, 2 * FF)
    left = w_ref[:, 0, 96:128, :].reshape(FF, 1024)
    right = jnp.concatenate([w_ref[:, 0, 128:144, :512], w_ref[:, 0, 128:144, 512:]], axis=1)
    return expand, left, right.reshape(FF, 512)

def grads_kernel(rows_ref, cot_ref, gate_ref, w_ref, hidden_ref, up_ref, out_ref):
    expand, left, right = weights_of(w_ref)
    grad_rows = (gate_ref[0] * cot_ref[0].astype(f32)).astype(bf16)
    rows = rows_ref[0]
    gate_pre = dot(rows, expand[:, :FF], ((1,), (0,)))
    up_part = dot(rows, expand[:, FF:], ((1,), (0,)))
    sig = jax.nn.sigmoid(gate_pre)
    hidden = (gate_pre * sig * up_part).astype(bf16)
    hidden_ref[0] = hidden
    hidden_grad = dot(grad_rows[:, :1024], left, ((1,), (1,))) + dot(
        grad_rows[:, 1024:], right, ((1,), (1,))
    )
    up_ref[0, :, :FF] = (hidden_grad * up_part * sig * (1.0 + gate_pre * (1.0 - sig))).astype(bf16)
    up_ref[0, :, FF:] = (hidden_grad * gate_pre * sig).astype(bf16)
    grad_left = dot(hidden, grad_rows[:, :1024], ((0,), (0,))).astype(bf16)
    out_ref[:, 0, 96:128, :] = grad_left.reshape(16, 32, 1024)
    grad_right = dot(hidden, grad_rows[:, 1024:], ((0,), (0,))).astype(bf16).reshape(16, 32, 512)
    out_ref[:, 0, 128:144, :512] = grad_right[:, :16]
    out_ref[:, 0, 128:144, 512:] = grad_right[:, 16:]
    up_grad = up_ref[0]
    for j in range(4):
        part = dot(rows[:, 384 * j : 384 * (j + 1)], up_grad, ((0,), (0,))).astype(bf16)
        out_ref[4 * j : 4 * (j + 1), 0, :96, :] = part.reshape(4, 96, 1024)

def expert_grads(rows, cot_rows, row_gates, weights):
    one = lambda e: (e, 0, 0)
    wide = lambda e: (0, e, 0, 0)
    return pl.pallas_call(
        grads_kernel,
        grid=(LOCAL_E,),
        in_specs=[
            pl.BlockSpec((1, SLOTS, D), one),
            pl.BlockSpec((1, SLOTS, D), one),
            pl.BlockSpec((1, SLOTS, 1), one),
            pl.BlockSpec((16, 1, 144, 1024), wide),
        ],
        out_specs=[
            pl.BlockSpec((1, SLOTS, FF), one),
            pl.BlockSpec((1, SLOTS, 2 * FF), one),
            pl.BlockSpec((16, 1, 144, 1024), wide),
        ],
        out_shape=[
            jax.ShapeDtypeStruct((LOCAL_E, SLOTS, FF), bf16),
            jax.ShapeDtypeStruct((LOCAL_E, SLOTS, 2 * FF), bf16),
            jax.ShapeDtypeStruct((16, LOCAL_E, 144, 1024), bf16),
        ],
        compiler_params=pltpu.CompilerParams(vmem_limit_bytes=BIG),
        cost_estimate=pl.CostEstimate(
            flops=12 * LOCAL_E * SLOTS * D * FF, bytes_accessed=60 << 20, transcendentals=0
        ),
    )(rows, cot_rows, row_gates, weights)


def core_swap(value):
    return lax.ppermute(value, "core", [(0, 1), (1, 0)])


def core_order(core, mine, other, axis):
    return jnp.concatenate(
        [jnp.where(core == 0, mine, other), jnp.where(core == 0, other, mine)], axis=axis
    )


def norm_apply(vector, gain):
    scale = lax.rsqrt(jnp.mean(vector * vector, axis=-1, keepdims=True) + norm_eps)
    return vector * scale * gain


def adamw_step(weight, gradient, mean_old, square_old, rate, decay):
    drift = beta_first * mean_old + (1.0 - beta_first) * gradient
    spread = beta_second * square_old + (1.0 - beta_second) * gradient * gradient
    mean_hat = drift / (1.0 - beta_first**STEP)
    square_hat = spread / (1.0 - beta_second**STEP)
    master = weight - rate * (mean_hat / (jnp.sqrt(square_hat) + adam_eps) + decay * weight)
    return (drift, spread, master)


def rotate(vector, cosine, sine):
    first, second = vector[..., : HD // 2], vector[..., HD // 2 :]
    return jnp.concatenate(
        [first * cosine - second * sine, second * cosine + first * sine], axis=-1
    )


def on_device(
    activations,
    cotangent,
    seq_lengths,
    deal_order,
    routes,
    entry_weight,
    entry_mean,
    entry_square,
    exit_weight,
    exit_mean,
    exit_square,
    router_weight,
    router_mean,
    router_square,
    expand_weight,
    expand_mean,
    expand_square,
    shrink_weight,
    shrink_mean,
    shrink_square,
    norm_gains,
    gains_mean,
    gains_square,
):
    seq = lax.axis_index("seq")
    core = lax.axis_index("core")
    first = (seq * 2 + core) * LOCAL_E

    packed = pack_experts(expand_weight, shrink_weight)
    packed, rows_in, cots_in = lax.optimization_barrier((packed, activations[0], cotangent[0]))
    weights = lax.all_gather(packed, PLANE, axis=0, tiled=False)

    entry_b = entry_weight.astype(bf16)
    shared_b = jnp.concatenate([router_weight, norm_gains.T], axis=1).astype(bf16)
    shared_b = jnp.pad(shared_b, ((0, 0), (0, 128 - EXPERTS - 2)))
    entry_cols = jnp.concatenate(
        [
            entry_b[:, : QH * HD].reshape(ROWS, N_SEQ, Q_OWN).transpose(1, 0, 2),
            entry_b[:, QH * HD :].reshape(ROWS, N_SEQ, KV_OWN).transpose(1, 0, 2),
            jnp.broadcast_to(shared_b[None], (N_SEQ, ROWS, 128)),
        ],
        axis=2,
    )
    exit_cols = exit_weight.astype(bf16).reshape(ROWS, 2, WIDE).transpose(1, 0, 2)
    pad = ((0, 0), (0, PAD_ROWS - ROWS), (0, 0))
    expert_ids = jnp.arange(128, dtype=jnp.int32)
    hit_slots = jnp.any(routes[0][:, :, None] == expert_ids[None, None, :], axis=1).astype(bf16)
    in_all, cots, hit_slots, entry_own, shared, exit_own = start(
        rows_in, cots_in, hit_slots, jnp.pad(entry_cols, pad), jnp.pad(exit_cols, pad)
    )
    in_all = in_all.reshape(GROUP, D)
    gains_full = shared[:, EXPERTS : EXPERTS + 2].astype(f32).T

    order_row = deal_order[0]
    token = jnp.arange(GROUP, dtype=jnp.int32)
    back_hot = (order_row[None, :] == token[:, None]).astype(bf16)
    hit = dot(back_hot, hit_slots.reshape(GROUP, 128), ((1,), (0,))).astype(bf16)
    hits = core_order(core, hit, core_swap(hit), 0)[:, :EXPERTS]
    own_hits = lax.dynamic_slice_in_dim(hits, first, LOCAL_E, 1)
    rank = jnp.cumsum(own_hits.astype(jnp.int32), axis=0) - 1
    rank = jnp.where(own_hits > 0, rank, -1)
    seq_ends = jnp.cumsum(seq_lengths[0])
    starts = seq_ends - seq_lengths[0]
    seq_ids = jnp.sum((token[:, None] >= seq_ends[None, :]).astype(jnp.int32), axis=1)
    seq_match = seq_ids[:, None] == jnp.arange(seq_ends.shape[0], dtype=jnp.int32)[None, :]
    positions = token - jnp.sum(jnp.where(seq_match, starts[None, :], 0), axis=1)
    frequency = rope_base ** (-jnp.arange(HD // 2, dtype=f32) * 2.0 / HD)
    phase = positions.astype(f32)[:, None] * frequency[None, :]
    cosine, sine = jnp.cos(phase)[:, None, :], jnp.sin(phase)[:, None, :]
    allowed = (seq_ids[:, None] == seq_ids[None, :]) & (token[None, :] <= token[:, None])

    normed = norm_apply(in_all.astype(f32), gains_full[0]).astype(bf16)
    mixed = dot(normed, entry_own, ((1,), (0,)))
    queries = rotate(mixed[:, :Q_OWN].reshape(GROUP, HEADS_OWN, HD), cosine, sine)
    pairs = mixed[:, Q_OWN:].reshape(GROUP, KV_HEADS_OWN, 2, HD)
    keys = rotate(pairs[:, :, 0], cosine, sine)
    queries = queries.astype(bf16).reshape(GROUP, KV_HEADS_OWN, PER_KV, HD)
    keys, values = keys.astype(bf16), pairs[:, :, 1].astype(bf16)
    scores = jnp.einsum("qhgd,khd->hgqk", queries, keys, preferred_element_type=f32) * HD**-0.5
    scores = jnp.where(allowed[None, None], scores, -1e30)
    peak = jnp.max(scores, axis=-1, keepdims=True)
    expo = jnp.exp(scores - peak)
    probs = expo / jnp.sum(expo, axis=-1, keepdims=True)
    probs_b = probs.astype(bf16)
    attended = (
        jnp.einsum("hgqk,khd->qhgd", probs_b, values, preferred_element_type=f32)
        .reshape(GROUP, Q_OWN)
        .astype(bf16)
    )
    branch_part = dot(attended, exit_own, ((1,), (0,))).astype(bf16)
    middle, tokens = middle_tokens(
        branch_part.reshape(N_SEQ, TOK_DEV, D), activations[0], gains_full[1:2]
    )
    normed_two = lax.dynamic_slice(tokens, (core, seq, 0, 0), (1, 1, TOK_DEV, D))[0, 0]
    tokens = tokens.reshape(PAIR_TOK, D)

    logits = dot(tokens, shared[:, :EXPERTS], ((1,), (0,)))
    masked = jnp.where(hits > 0, logits, -jnp.inf)
    gate_expo = jnp.exp(masked - jnp.max(masked, axis=1, keepdims=True))
    gates = gate_expo / jnp.sum(gate_expo, axis=1, keepdims=True)
    own_gates = lax.dynamic_slice_in_dim(gates, first, LOCAL_E, 1)
    rows, cot_rows, row_gates = dispatch(rank.T, own_gates.T, tokens, cots.reshape(PAIR_TOK, D))
    hidden, up_grad, expert_grad = expert_grads(rows, cot_rows, row_gates, weights)
    expert_sum = lax.psum_scatter(expert_grad, PLANE, scatter_dimension=0, tiled=False)
    my_gates = lax.dynamic_slice_in_dim(gates, core * GROUP + seq * TOK_DEV, TOK_DEV, 0)
    my_gates = jnp.pad(my_gates, ((0, 0), (0, 128 - EXPERTS)))
    middle_grad, branch_grad, logit_grad, gain_two_grad, out_sum = turn(
        rank,
        up_grad,
        hidden,
        row_gates,
        cot_rows,
        weights,
        middle,
        cotangent[0],
        my_gates,
        shared,
        gains_full[1:2],
    )
    branch_grad = branch_grad.reshape(GROUP, D)
    router_grad = dot(normed_two, logit_grad, ((0,), (0,)))

    attended_grad = dot(branch_grad, exit_own, ((1,), (1,))).astype(bf16)
    attended_grad = attended_grad.reshape(GROUP, KV_HEADS_OWN, PER_KV, HD)
    prob_grad = jnp.einsum("qhgd,khd->hgqk", attended_grad, values, preferred_element_type=f32)
    delta = jnp.sum(probs * prob_grad, axis=-1, keepdims=True)
    score_grad = (probs * (prob_grad - delta) * HD**-0.5).astype(bf16)
    query_grad = jnp.einsum("hgqk,khd->qhgd", score_grad, keys, preferred_element_type=f32)
    key_grad = jnp.einsum("hgqk,qhgd->khd", score_grad, queries, preferred_element_type=f32)
    value_grad = jnp.einsum("hgqk,qhgd->khd", probs_b, attended_grad, preferred_element_type=f32)
    query_grad = rotate(query_grad.reshape(GROUP, HEADS_OWN, HD), cosine, -sine)
    key_grad = rotate(key_grad, cosine, -sine)
    mixed_grad = jnp.concatenate(
        [
            query_grad.reshape(GROUP, Q_OWN),
            jnp.stack([key_grad, value_grad], axis=2).reshape(GROUP, KV_OWN),
        ],
        axis=1,
    ).astype(bf16)
    normed_part = dot(mixed_grad, entry_own, ((1,), (1,))).astype(bf16)
    input_grad, block_output, entry_got, exit_got = closing(
        normed_part.reshape(N_SEQ, TOK_DEV, D),
        activations[0],
        middle_grad,
        gains_full[0:1],
        normed,
        mixed_grad,
        attended,
        branch_grad,
        router_grad,
        gain_two_grad,
        out_sum,
        middle,
    )

    entry_got = entry_got[:, :ROWS]
    entry_sum = jnp.concatenate(
        [
            entry_got[:, :, :Q_OWN].transpose(1, 0, 2).reshape(ROWS, QH * HD),
            entry_got[:, :, Q_OWN:MIX_OWN].transpose(1, 0, 2).reshape(ROWS, 2 * KVH * HD),
        ],
        axis=1,
    )
    shared_sum = jnp.sum(entry_got[:, :, MIX_OWN:], axis=0)
    router_sum = shared_sum[:, :EXPERTS]
    gains_sum = shared_sum[:, EXPERTS : EXPERTS + 2].T
    exit_sum = exit_got[:ROWS]

    ends = expert_sum[:, 128:].reshape(LOCAL_E, 16, 2, 512).transpose(2, 0, 1, 3)
    rows_of = jnp.stack(
        [
            jnp.concatenate([expert_sum[:, :48], expert_sum[:, 96:112]], axis=1),
            jnp.concatenate([expert_sum[:, 48:96], expert_sum[:, 112:128]], axis=1),
        ]
    )

    def to_owner(value):
        mine = lax.dynamic_index_in_dim(value, core, 0, keepdims=False)
        other = core_swap(lax.dynamic_index_in_dim(value, 1 - core, 0, keepdims=False))
        return core_order(core, mine, other, 0).astype(f32)

    rows_of, ends = to_owner(rows_of), to_owner(ends)
    expand_sum = rows_of[:, :48]
    shrink_sum = jnp.concatenate([rows_of[:, 48:], ends], axis=2)
    entry_new = adamw_step(entry_weight, entry_sum, entry_mean, entry_square, 0.02, weight_decay)
    exit_new = adamw_step(exit_weight, exit_sum, exit_mean, exit_square, 0.15, weight_decay)
    router_new = adamw_step(
        router_weight, router_sum, router_mean, router_square, 0.01, weight_decay
    )
    expand_new = adamw_step(
        expand_weight, expand_sum, expand_mean, expand_square, 0.02, weight_decay
    )
    shrink_new = adamw_step(
        shrink_weight, shrink_sum, shrink_mean, shrink_square, 0.12, weight_decay
    )
    gains_new = adamw_step(norm_gains, gains_sum, gains_mean, gains_square, 0.5, 0.0)
    return (
        block_output[None],
        input_grad[None],
        *entry_new,
        *exit_new,
        *router_new,
        *expand_new,
        *shrink_new,
        *gains_new,
    )


def solution(mesh):
    fine = Mesh(mesh.devices.reshape(4, 4, 4, 2), ("seq", "x", "y", "core"))
    rows = P(FSDP, "seq", None)
    lists = P(FSDP, None)
    owned = P(("seq",) + FSDP, None)
    experts = P("seq", FSDP, None)
    gains = P(None, ("seq",) + FSDP)
    return jax.shard_map(
        on_device,
        mesh=fine,
        in_specs=(rows, rows, lists, lists, rows)
        + (owned,) * 9
        + (experts,) * 6
        + (gains,) * 3,
        out_specs=(rows, rows) + (owned,) * 9 + (experts,) * 6 + (gains,) * 3,
        check_vma=False,
    )
```

time: 451 us -> 387 us (0.86)
  Pallas kernels: 287 us -> 247 us
  waiting for transfers between devices: 9.25 us -> 26 us
  other arithmetic: 35.2 us -> 21.2 us
  local copies, waits for them, and re-layouts: 32.4 us -> 19.2 us
  starting transfers between devices: 8.84 us -> 1.2 us
    pallas_call x6 -> x4, Pallas kernels: 211 us -> 172 us  [the longest x1 60.7 us: closing(): pl.pallas_call(closing_kernel, out_shape=[jax.ShapeDtypeStruct((TOK_DEV,...]
    all_gather x1, waiting for transfers between devices: 0.01 us -> 25.5 us  [on_device(): weights = lax.all_gather(packed, PLANE, axis=0, tiled=False)]
    ppermute x3 -> x0, waiting for transfers between devices: 7.7 us -> none  [on_device(): lax.ppermute(block, 'seq', [(i, (i + step) % N_SEQ) for i in range(N_SEQ)])]
    unnamed x124 -> x91, local copies, waits for them, and re-layouts: 9.69 us -> 6.05 us
  transfers between devices with their start and end apart: 11 -> 5, of which waited for: 3 -> 2; matrix products, arithmetic and copies ran while one was open for 23% -> 21% of each run, Pallas kernels for 59% -> 56%
where the time goes in v3:
time: 387 us; the launch traced here: 383 us
  Pallas kernels  247 us (64%)
  matrix products  53.3 us (14%)
  waiting for transfers between devices  26 us (7%)
  other arithmetic  21.2 us (5%)
  local copies, waits for them, and re-layouts  19.2 us (5%)
  between operations  15.2 us (4%)
    pallas_call x1, Pallas kernels, closing(): pl.pallas_call(closing_kernel, out_shape=[jax.ShapeDtypeStruct((TOK_DEV,...  60.7 us
    pallas_call x1, Pallas kernels, turn(): pl.pallas_call(turn_kernel, grid=(LOCAL_E + 1,), in_specs=[pl.BlockSpec((...  55.2 us
    pallas_call x1, Pallas kernels, start(): pl.pallas_call(start_kernel, out_shape=[jax.ShapeDtypeStruct((N_SEQ, TOK_...  49.7 us
    pallas_call x1, Pallas kernels, middle_tokens(): pl.pallas_call(middle_kernel, out_shape=[jax.ShapeDtypeStruct((TOK_DEV, D...  35.3 us
    pallas_call x1, Pallas kernels, expert_grads(): pl.pallas_call(grads_kernel, grid=(LOCAL_E,), in_specs=[pl.BlockSpec((1,...  26.3 us
    all_gather x1, waiting for transfers between devices, on_device(): weights = lax.all_gather(packed, PLANE, axis=0, tiled=False)  25.5 us
    dot_general x7, matrix products, dot(): return lax.dot_general(a, b, (dims, ((), ())), preferred_element_type=f32)  15 us
    pallas_call x1, Pallas kernels, dispatch(): pl.pallas_call(dispatch_kernel, grid=(LOCAL_E,), in_specs=[pl.BlockSpec((...  13.3 us
  transfers between devices with their start and end apart: 5, of which 2 were waited for; matrix products, arithmetic and copies ran while one was open for 21% of the time, Pallas kernels for 56%

profile of v3, /device:TPU:1, one launch (start us, length us, event | category | flops | bytes accessed | tf_op | source)
XLA Modules:
  0.0 382.9 jit_solution(13211435819800186463)
XLA Ops:
  7.3 6.4 %shard_map.374 = bf16[5,144,1024]{2,1,0:T(8,128)(2,1)} custom-call(f32[10,48,1024]{2,1,0:T(8,128)} %expand_ref.1, f32[10,16,1536]{2,1,0:T(8,128)} %shrink_ref.1), custom_call_target="tpu_custom_call" | custom-call | tf_op jit(solution)/shard_map/pallas_call | solution.py:263
  17.0 49.7 %shard_map.375 = (bf16[4,128,1536]{2,1,0:T(8,128)(2,1)}, bf16[2,4,128,1536]{3,2,1,0:T(8,128)(2,1)}, bf16[4,128,128]{2,1,0:T(8,128)(2,1)}, bf16[1536,640]{1,0:T(8...) custom-call(bf16[128,1536]{1,0:T(8,128)(2,1)} %bitcast.200, bf16[128,1536]{1,0:T(8,128)(2,1)} %bitcast.223, ...), custom_call_target="tpu_custom_call" | custom-call | tf_op jit(solution)/shard_map/pallas_call | solution.py:367
  66.8 1.3 convolution_convert_fusion.3
  68.4 1.2 copy.217
  69.6 1.8 multiply_reduce_fusion
  72.9 1.4 fusion.96
  77.7 4.9 %fusion.95 = (f32[2,3,512]{2,1,0:T(4,128)S(1)}, f32[2,3,512,512]{2,3,1,0:T(8,128)}) fusion(pred[512,512]{0,1:T(8,128)(4,1)S(1)} %fusion.32, bf16[512,2,3,32]{0,3,2,1:T(8,128)(2,1)S(1)} %bitcast.231, bf16[512,2,3,32]{0,3,2,1:T(8,128)(2,1)S(1)} %bitcast.229, bf16[512,2,32]{0,2,1:T(8,128)(2,1)S(1)} %get-tuple-element.204, ...), kind=kOutput, calls=%fused_computation.175 | convolution fusion | flops 208667136 | bytes 7090176 | tf_op jit(solution)/shard_map/sub | solution.py:940
  82.7 3.6 fusion.19
  86.3 2.1 convolution_convert_fusion.1
  88.4 35.3 %shard_map.376 = (f32[128,1536]{1,0:T(8,128)}, bf16[2,4,128,1536]{3,2,1,0:T(8,128)(2,1)}) custom-call(bf16[4,128,1536]{2,1,0:T(8,128)(2,1)} %bitcast.199, bf16[128,1536]{1,0:T(8,128)(2,1)} %bitcast.201, f32[1,1536]{1,0:T(1,128)} %get-tuple-element.213.gain_ref), custom_call_target="tpu_custom_call" | custom-call | tf_op jit(solution)/shard_map/pallas_call | solution.py:413
  123.7 0.9 broadcast_select_fusion.3
  125.0 1.6 reduce-window.11
  128.3 2.9 fusion.84
  133.1 13.3 %shard_map.377 = (bf16[5,256,1536]{2,1,0:T(8,128)(2,1)}, bf16[5,256,1536]{2,1,0:T(8,128)(2,1)}, f32[5,256,1]{2,1,0:T(8,128)}) custom-call(s32[5,1,1024]{2,1,0:T(1,128)} %copy.226.rank_ref, f32[5,1,1024]{2,1,0:T(1,128)} %copy.227.gate_ref, bf16[1024,1536]{1,0:T(8,128)(2,1)} %bitcast.238, bf16[1024,1536]{1,0:T(8,128)(2,1)} %bitcast.244), custom_call_target="tpu_custom_call" | custom-call | flops 8053063680 | bytes 16777216 | tf_op jit(solution)/shard_map/pallas_call | solution.py:743
  146.4 25.5 %all-gather.3.cloned.1.call-done = bf16[80,144,1024]{2,1,0:T(8,128)(2,1)} async-done(((bf16[5,144,1024]{2,1,0:T(8,128)(2,1)}), bf16[80,144,1024]{2,1,0:T(8,128)(2,1)}) %all-gather.3.cloned.1.call-update) | async-done | bytes 23592976 | tf_op jit(solution)/shard_map/all_gather | solution.py:889
  171.9 26.3 %shard_map.378 = (bf16[5,256,512]{2,1,0:T(8,128)(2,1)}, bf16[5,256,1024]{2,1,0:T(8,128)(2,1)}, bf16[16,5,144,1024]{3,2,1,0:T(8,128)(2,1)}) custom-call(bf16[5,256,1536]{2,1,0:T(8,128)(2,1)} %get-tuple-element.55.rows_ref, bf16[5,256,1536]{2,1,0:T(8,128)(2,1)} %get-tuple-element.56.cot_ref.cot_rows_ref, f32[5,256,1]{2,1,0:T(8,128)} %get-tuple-element.57.gate_ref, ...), custom_call_target="tpu_custom_call" | custom-call | flops 12079595520 | bytes 62914560 | tf_op jit(solution)/shard_map/pallas_call | solution.py:801
  198.2 0.9 copy.234.attended_ref
  199.7 55.2 %shard_map.379 = (f32[128,1536]{1,0:T(8,128)}, bf16[4,128,1536]{2,1,0:T(8,128)(2,1)}, bf16[128,128]{1,0:T(8,128)(2,1)}, f32[1,1536]{1,0:T(1,128)}, bf16[4,128,1536]{2,1,0:T(8,128)(2,1)}) custom-call(s32[1024,5]{1,0:T(8,128)} %copy-done.4, bf16[5,256,1024]{2,1,0:T(8,128)(2,1)} %get-tuple-element.59.up_ref, bf16[5,256,512]{2,1,0:T(8,128)(2,1)} %get-tuple-element.60.hidden_ref, ...), custom_call_target="tpu_custom_call" | custom-call | flops 14092861440 | bytes 41943040 | tf_op jit(solution)/shard_map/pallas_call | solution.py:538
  254.9 2.5 convolution_convert_fusion.2
  257.4 3.7 fusion.59
  261.1 10.7 %fusion.25 = f32[512,2,64]{0,2,1:T(8,128)S(1)} fusion(f32[2,512,512,3]{2,1,3,0:T(8,128)} %fusion.59, bf16[512,2,3,32]{0,3,2,1:T(8,128)(2,1)S(1)} %bitcast.232, bf16[512,2,3,32]{0,3,2,1:T(8,128)(2,1)S(1)} %bitcast.230, f32[2,3,512,512]{2,3,1,0:T(8,128)} %get-tuple-element.218, f32[2,3,512]{2,1,0:T(4,128)S(1)} %get-tuple-element.217), kind=kOutput, calls=%fused_computation.40 | convolution fusion | flops 213126656 | bytes 13250560 | tf_op jit(solution)/shard_map/hgqk,qhgd->khd/dot_general | solution.py:987
  271.9 4.0 %fusion.29 = bf16[512,2,1,64]{0,3,1,2:T(8,128)(2,1)S(1)} fusion(bf16[512,2,3,64]{0,3,2,1:T(8,128)(2,1)S(1)} %bitcast.226, f32[2,3,512,512]{2,3,1,0:T(8,128)} %get-tuple-element.218, f32[2,3,512]{2,1,0:T(4,128)S(1)} %get-tuple-element.217), kind=kOutput, calls=%fused_computation.43 | convolution fusion | flops 204537856 | bytes 6828032 | tf_op jit(solution)/shard_map/hgqk,qhgd->khd/dot_general | solution.py:988
  276.2 11.4 %fusion.13 = f32[2,64,3,512]{3,1,2,0:T(8,128)S(1)} fusion(f32[2,512,512,3]{2,1,3,0:T(8,128)} %fusion.59, bf16[512,2,32]{0,2,1:T(8,128)(2,1)S(1)} %copy-done.28, bf16[512,2,32]{0,2,1:T(8,128)(2,1)S(1)} %copy-done.26, f32[2,3,512,512]{2,3,1,0:T(8,128)} %get-tuple-element.218, f32[2,3,512]{2,1,0:T(4,128)S(1)} %get-tuple-element.217), kind=kOutput, calls=%fused_computation.23 | convolution fusion | flops 212602368 | bytes 13512704 | tf_op jit(solution)/shard_map/hgqk,khd->qhgd/dot_general | solution.py:986
  288.9 2.2 fusion.44.router_grad_ref
  291.1 2.6 convolution_convert_fusion
  293.7 60.7 %shard_map.380 = (bf16[128,1536]{1,0:T(8,128)(2,1)}, bf16[128,1536]{1,0:T(8,128)(2,1)}, f32[4,16,768]{2,1,0:T(8,128)}, f32[16,1536]{1,0:T(8,128)}) custom-call(bf16[4,128,1536]{2,1,0:T(8,128)(2,1)} %bitcast.214, bf16[128,1536]{1,0:T(8,128)(2,1)} %bitcast.202, f32[128,1536]{1,0:T(8,128)} %get-tuple-element.63.grad_ref, ...), custom_call_target="tpu_custom_call" | custom-call | tf_op jit(solution)/shard_map/pallas_call | solution.py:703
  357.9 1.6 multiply_subtract_fusion.3
  360.4 1.1 fusion.92
  361.5 1.2 fusion.93
  366.2 1.0 copy-done.7
  368.5 3.7 multiply_subtract_fusion
  372.2 2.1 multiply_subtract_fusion.1
  (182 shorter events, 24.9 us)
Async XLA Ops:
  7.2 6.6 %copy-start.12 = (f32[12,2560]{1,0:T(8,128)S(1)}, f32[12,2560]{1,0:T(8,128)}, u32[]{:S(2)}) copy-start(f32[12,2560]{1,0:T(8,128)} %param.28) | copy-start | bytes 368644
  7.2 6.6 %copy-start.34 = (f32[2,12]{1,0:T(2,128)S(1)}, f32[2,12]{1,0:T(2,128)}, u32[]{:S(2)}) copy-start(f32[2,12]{1,0:T(2,128)} %param.43) | copy-start | bytes 292
  7.2 6.7 %copy-start.30 = (f32[12,40]{1,0:T(8,128)S(1)}, f32[12,40]{1,0:T(8,128)}, u32[]{:S(2)}) copy-start(f32[12,40]{1,0:T(8,128)} %param.34) | copy-start | bytes 5764
  7.2 164.7 %all-gather.3.cloned.1.call-start = ((), (), s32[]{:S(2)}) async-start(), calls=%async_computation.1 | async-start | bytes 25067520 | tf_op jit(solution)/shard_map/all_gather | solution.py:889
  13.7 53.2 %copy-start.39 = (s32[1,512]{1,0:T(1,128)S(1)}, s32[1,512]{1,0:T(1,128)}, u32[]{:S(2)}) copy-start(s32[1,512]{1,0:T(1,128)} %param.26) | copy-start | bytes 6148
  13.7 346.7 %reduce-scatter.4.cloned.1.call-start = ((), (), s32[]{:S(2)}) async-start(), calls=%async_computation.2 | async-start | bytes 25067520
  66.8 5.2 %copy-start.1 = (bf16[4,128,1536]{2,1,0:T(8,128)(2,1)S(1)}, bf16[4,128,1536]{2,1,0:T(8,128)(2,1)}, u32[]{:S(2)}) copy-start(bf16[4,128,1536]{2,1,0:T(8,128)(2,1)} %get-tuple-element.48) | copy-start | bytes 4718596
  68.2 55.5 %collective-permute-start = (bf16[512,128]{1,0:T(8,128)(2,1)S(1)}, bf16[512,128]{1,0:T(8,128)(2,1)}, u32[]{:S(2)}, u32[]{:S(2)}) collective-permute-start(bf16[512,128]{1,0:T(8,128)(2,1)S(1)} %convolution_convert_fusion.3), channel_id=1, source_target_pairs={{0,1},{1,0},{2,3},{3,2},{4,5},{5,4},{6,7},{7,6},{8,9},{9,8},{10,11... | collective-permute-start | bytes 393224 | tf_op jit(solution)/shard_map/ppermute | solution.py:828
  77.6 5.1 %copy-start.25 = (bf16[512,2,32]{0,2,1:T(8,128)(2,1)}, bf16[512,2,32]{0,2,1:T(8,128)(2,1)S(1)}, u32[]{:S(2)}) copy-start(bf16[512,2,32]{0,2,1:T(8,128)(2,1)S(1)} %get-tuple-element.203) | copy-start | bytes 196612
  77.6 5.1 %copy-start.27 = (bf16[512,2,32]{0,2,1:T(8,128)(2,1)}, bf16[512,2,32]{0,2,1:T(8,128)(2,1)S(1)}, u32[]{:S(2)}) copy-start(bf16[512,2,32]{0,2,1:T(8,128)(2,1)S(1)} %get-tuple-element.204) | copy-start | bytes 196612
  77.7 4.9 %copy-start.17 = (bf16[512,6,32]{0,2,1:T(8,128)(2,1)}, bf16[512,6,32]{0,2,1:T(8,128)(2,1)S(1)}, u32[]{:S(2)}) copy-start(bf16[512,6,32]{0,2,1:T(8,128)(2,1)S(1)} %get-tuple-element.199) | copy-start | bytes 589828
  77.7 4.9 %copy-start.19 = (bf16[512,6,32]{0,2,1:T(8,128)(2,1)}, bf16[512,6,32]{0,2,1:T(8,128)(2,1)S(1)}, u32[]{:S(2)}) copy-start(bf16[512,6,32]{0,2,1:T(8,128)(2,1)S(1)} %get-tuple-element.200) | copy-start | bytes 589828
  82.7 3.6 copy-start.8
  124.7 3.7 copy-start.13
  127.5 3.8 copy-start.4
  199.7 55.2 %copy-start.9 = (bf16[384,1536]{1,0:T(8,128)(2,1)S(1)}, bf16[384,1536]{1,0:T(8,128)(2,1)}, u32[]{:S(2)}) copy-start(bf16[384,1536]{1,0:T(8,128)(2,1)} %get-tuple-element.52) | copy-start | bytes 3538948
  257.4 3.7 copy-start.18
  257.4 3.7 copy-start.20
  271.9 4.3 %copy-start.26 = (bf16[512,2,32]{0,2,1:T(8,128)(2,1)S(1)}, bf16[512,2,32]{0,2,1:T(8,128)(2,1)}, u32[]{:S(2)}) copy-start(bf16[512,2,32]{0,2,1:T(8,128)(2,1)} %copy-done.25) | copy-start | bytes 196612
  271.9 4.3 %copy-start.28 = (bf16[512,2,32]{0,2,1:T(8,128)(2,1)S(1)}, bf16[512,2,32]{0,2,1:T(8,128)(2,1)}, u32[]{:S(2)}) copy-start(bf16[512,2,32]{0,2,1:T(8,128)(2,1)} %copy-done.27) | copy-start | bytes 196612
  287.7 3.4 copy-start.38
  293.6 63.6 %copy-start.31 = (f32[12,40]{1,0:T(8,128)S(1)}, f32[12,40]{1,0:T(8,128)}, u32[]{:S(2)}) copy-start(f32[12,40]{1,0:T(8,128)} %param.36) | copy-start | bytes 5764
  293.6 63.6 %copy-start.32 = (f32[12,40]{1,0:T(8,128)S(1)}, f32[12,40]{1,0:T(8,128)}, u32[]{:S(2)}) copy-start(f32[12,40]{1,0:T(8,128)} %param.35) | copy-start | bytes 5764
  293.7 64.3 %copy-start.23 = (f32[12,1536]{1,0:T(8,128)S(1)}, f32[12,1536]{1,0:T(8,128)}, u32[]{:S(2)}) copy-start(f32[12,1536]{1,0:T(8,128)} %param.33) | copy-start | bytes 221188
  293.7 64.3 %copy-start.24 = (f32[12,1536]{1,0:T(8,128)S(1)}, f32[12,1536]{1,0:T(8,128)}, u32[]{:S(2)}) copy-start(f32[12,1536]{1,0:T(8,128)} %param.32) | copy-start | bytes 221188
  354.3 5.2 %copy-start.21 = (f32[12,2560]{1,0:T(8,128)S(1)}, f32[12,2560]{1,0:T(8,128)}, u32[]{:S(2)}) copy-start(f32[12,2560]{1,0:T(8,128)} %param.30) | copy-start | bytes 368644
  354.3 5.2 %copy-start.22 = (f32[12,2560]{1,0:T(8,128)S(1)}, f32[12,2560]{1,0:T(8,128)}, u32[]{:S(2)}) copy-start(f32[12,2560]{1,0:T(8,128)} %param.29) | copy-start | bytes 368644
  363.3 2.4 collective-permute-start.1
  363.8 1.8 collective-permute-start.2
  368.5 3.7 copy-start.3
  368.5 3.7 copy-start.10
  368.5 3.7 copy-start.11
  (14 other events, 23.1 us)
Sparse Core Ops, SparseCore 0:
  13.8 158.0 all-gather.2
  198.3 156.8 reduce-scatter.3

commit v4 on v3

--- a/solution.py
+++ b/solution.py
@@ -386,12 +386,62 @@
     )(rows, cots, hits, entry_cols, exit_cols)
 
 
-def middle_kernel(part_ref, in_ref, gain_ref, middle_ref, tokens_ref, mine, *rest):
+def swap_halves(rows, lower, upper):
+    lane = lax.broadcasted_iota(jnp.int32, rows.shape, 1)
+    ahead = pltpu.roll(rows, rows.shape[1] - HD // 2, 1)
+    behind = pltpu.roll(rows, HD // 2, 1)
+    return jnp.where(lax.rem(lane, HD) < HD // 2, lower * ahead, upper * behind)
+
+
+BLOCK = 256
+
+
+def block_bias(seq_col_ref, seq_row_ref, block):
+    keys = BLOCK * (block + 1)
+    row = lax.broadcasted_iota(jnp.int32, (BLOCK, keys), 0) + BLOCK * block
+    column = lax.broadcasted_iota(jnp.int32, (BLOCK, keys), 1)
+    same = seq_col_ref[BLOCK * block : keys, :] == seq_row_ref[:, :keys]
+    return jnp.where(same & (column <= row), 0.0, -1e30)
+
+
+def head_of(index):
+    return slice(HD * index, HD * (index + 1))
+
+
+def middle_kernel(
+    all_ref, gain_one_ref, entry_ref, cos_ref, sin_ref, seq_col_ref, seq_row_ref, exit_ref,
+    in_ref, gain_ref,
+    normed_ref, qkv_ref, attended_ref, lse_ref, middle_ref, tokens_ref,
+    part, mine, *rest
+):
     bufs, (send_sem, recv_sem, copy_sem) = rest[:6], rest[6:]
     me, core = lax.axis_index("seq"), lax.axis_index("core")
     greet(near("seq") + [sibling()])
     send = sender(send_sem, recv_sem)
-    reduce = Reduce(send, 0, "seq", lambda i: part_ref.at[i], bufs, half_rows)
+    for block in range(N_SEQ):
+        rows = slice(TOK_DEV * block, TOK_DEV * (block + 1))
+        vector = all_ref[block].astype(f32)
+        normed_ref[rows, :] = (vector * unit_scale(vector) * gain_one_ref[...]).astype(bf16)
+    mixed = dot(normed_ref[...], entry_ref[...], ((1,), (0,)))
+    mixed = mixed * cos_ref[...] + swap_halves(mixed, -1.0, 1.0) * sin_ref[...]
+    qkv_ref[...] = mixed.astype(bf16)
+    for block in range(GROUP // BLOCK):
+        bias = block_bias(seq_col_ref, seq_row_ref, block)
+        keys = BLOCK * (block + 1)
+        rows = slice(BLOCK * block, keys)
+        for head in range(HEADS_OWN):
+            pair = Q_OWN + 2 * HD * (head // PER_KV)
+            key = qkv_ref[:keys, pair : pair + HD]
+            value = qkv_ref[:keys, pair + HD : pair + 2 * HD]
+            scores = dot(qkv_ref[rows, head_of(head)], key, ((1,), (1,))) * HD**-0.5 + bias
+            peak = jnp.max(scores, axis=1, keepdims=True)
+            expo = jnp.exp(scores - peak)
+            total = jnp.sum(expo, axis=1, keepdims=True)
+            probs = (expo / total).astype(bf16)
+            attended_ref[rows, head_of(head)] = dot(probs, value, ((1,), (0,))).astype(bf16)
+            lse_ref[rows, head : head + 1] = peak + jnp.log(total)
+    part[...] = dot(attended_ref[...], exit_ref[...], ((1,), (0,))).astype(bf16).reshape(part.shape)
+    reduce = Reduce(send, 0, "seq", lambda i: part.at[i], bufs, half_rows)
     reduce.start_far()
     reduce.start_near()
     reduce.relay()
@@ -409,21 +459,25 @@
     local.wait()
 
 
-def middle_tokens(part, rows, gain):
+def middle_tokens(*operands):
     return pl.pallas_call(
         middle_kernel,
         out_shape=[
+            jax.ShapeDtypeStruct((GROUP, D), bf16),
+            jax.ShapeDtypeStruct((GROUP, MIX_OWN), bf16),
+            jax.ShapeDtypeStruct((GROUP, Q_OWN), bf16),
+            jax.ShapeDtypeStruct((GROUP, HEADS_OWN), f32),
             jax.ShapeDtypeStruct((TOK_DEV, D), f32),
             jax.ShapeDtypeStruct((2, N_SEQ, TOK_DEV, D), bf16),
         ],
-        in_specs=[VMEM] * 3,
-        out_specs=[VMEM, ANY],
-        scratch_shapes=[pltpu.VMEM((TOK_DEV, D), bf16)]
+        in_specs=[VMEM] * 10,
+        out_specs=[VMEM] * 5 + [ANY],
+        scratch_shapes=[pltpu.VMEM((N_SEQ, TOK_DEV, D), bf16), pltpu.VMEM((TOK_DEV, D), bf16)]
         + reduce_scratch((TOK_DEV, D), (HALF, D))
         + sems(16)
         + [pltpu.SemaphoreType.DMA],
         compiler_params=remote_params(3),
-    )(part, rows, gain)
+    )(*operands)
 
 
 def turn_kernel(
@@ -589,23 +643,18 @@
 
 PAD_ROWS = 16
 WIDE = 768
-HALF_WIDE = 2304
-
-
 def closing_kernel(
-    part_ref, in_ref, grad_ref, gain_ref, normed_ref, mixed_ref, attended_ref, branch_ref,
+    qkv_ref, lse_ref, cos_ref, sin_ref, seq_col_ref, seq_row_ref, exit_ref, entry_ref,
+    in_ref, grad_ref, gain_ref, normed_ref, attended_ref, branch_ref,
     router_grad_ref, gain_two_ref, out_sum_ref, middle_ref,
     input_ref, block_ref, entry_out, exit_out,
-    full, from_core, chip, line, final, give, got_z, *rest
+    turned, mixed_grad, part, full, from_core, chip, line, final, give, got_z, *rest
 ):
-    bufs, (send_sem, recv_sem) = [rest[6 * i : 6 * i + 6] for i in range(6)], rest[36:]
+    bufs, (send_sem, recv_sem) = [rest[6 * i : 6 * i + 6] for i in range(8)], rest[48:]
     z, x, y, c = (lax.axis_index(a) for a in ("seq", "x", "y", "core"))
     right, left, far = ring(z)
     greet(near("seq") + [("seq", far)] + near("x") + near("y") + [sibling()])
     send = sender(send_sem, recv_sem)
-    rows = Reduce(send, 0, "seq", lambda i: part_ref.at[i], bufs[0], half_rows)
-    rows.start_far()
-    rows.start_near()
     pick = row_pick((512, QOWN), 0)
 
     def spread(grad):
@@ -613,25 +662,102 @@
         return wide.reshape(16, 2, PAD_ROWS, grad.shape[1])
 
     def swap(side):
-        return send(full.at[side, :, 1 - c], from_core.at[side], 36 + side, "core", 1 - c)
-
-    def entry_rows(block):
-        rows_of = slice(QOWN * block, QOWN * (block + 1))
-        grad = dot(normed_ref[:, rows_of], mixed_ref[...], ((0,), (0,))).astype(bf16)
-        return spread(grad)
+        return send(full.at[side, :, 1 - c], from_core.at[side], 48 + side, "core", 1 - c)
+
+    def chip_sum(side, copy):
+        copy.wait_recv()
+        for plane in range(16):
+            first, second = (plane % 4, plane // 4) if side == 2 else (plane // 4, plane % 4)
+            added(chip.at[side, first, second], full.at[side, plane, c], from_core.at[side, plane])
+
+    def first_sum(side, axis):
+        reduce = Reduce(send, 6 * side, axis, lambda i: chip.at[side, i], bufs[side], half_rows)
+        reduce.start_far()
+        reduce.start_near()
+        return reduce
+
+    def second_sum(side, axis, reduce):
+        line[side] = reduce.total().astype(bf16)
+        reduce = Reduce(
+            send, 18 + 6 * side, axis, lambda i: line.at[side, i], bufs[3 + side], half_lanes
+        )
+        reduce.start_far()
+        reduce.start_near()
+        return reduce
 
     for block in range(3):
         cols = slice(512 * block, 512 * (block + 1))
         grad = dot(attended_ref[...], branch_ref[:, cols], ((0,), (0,))).astype(bf16)
         full[0, :, :, :, cols] = spread(grad)
-    full[0, :, :, :, 1536:2176] = entry_rows(0)
-    second = entry_rows(1)
-    full[0, :, :, :, 2176:2304] = second[..., :128]
     swaps = [swap(0)]
+    outs = Reduce(send, 36, "seq", lambda i: out_sum_ref.at[i], bufs[6], half_rows)
+    outs.start_far()
+    outs.start_near()
+
+    def turn_back(kv):
+        pair = Q_OWN + 2 * HD * kv
+        for head in range(PER_KV * kv, PER_KV * (kv + 1)):
+            grad = dot(branch_ref[...], exit_ref[head_of(head), :], ((1,), (1,))).astype(bf16)
+            attended = attended_ref[:, head_of(head)].astype(f32)
+            delta = jnp.sum(grad.astype(f32) * attended, axis=1, keepdims=True)
+            for block in range(GROUP // BLOCK):
+                bias = block_bias(seq_col_ref, seq_row_ref, block)
+                keys = BLOCK * (block + 1)
+                rows = slice(BLOCK * block, keys)
+                key = qkv_ref[:keys, pair : pair + HD]
+                value = qkv_ref[:keys, pair + HD : pair + 2 * HD]
+                query, grad_rows = qkv_ref[rows, head_of(head)], grad[rows]
+                scores = dot(query, key, ((1,), (1,))) * HD**-0.5 + bias
+                probs = jnp.exp(scores - lse_ref[rows, head : head + 1])
+                prob_grad = dot(grad_rows, value, ((1,), (1,)))
+                score_grad = probs * (prob_grad - delta[rows]) * HD**-0.5
+                score_grad = score_grad.astype(bf16)
+                turned[rows, head_of(head)] = dot(score_grad, key, ((1,), (0,)))
+                key_grad = dot(score_grad, query, ((0,), (0,)))
+                value_grad = dot(probs.astype(bf16), grad_rows, ((0,), (0,)))
+                if head == PER_KV * kv and block == GROUP // BLOCK - 1:
+                    turned[:, pair : pair + HD] = key_grad
+                    turned[:, pair + HD : pair + 2 * HD] = value_grad
+                    turned[:BLOCK, pair : pair + HD] += held[0]
+                    turned[:BLOCK, pair + HD : pair + 2 * HD] += held[1]
+                elif head == PER_KV * kv:
+                    held = (key_grad, value_grad)
+                else:
+                    turned[:keys, pair : pair + HD] += key_grad
+                    turned[:keys, pair + HD : pair + 2 * HD] += value_grad
+
+    turn_back(0)
+    chip_sum(0, swaps[0])
+    first_0 = first_sum(0, "x")
+    outs.relay()
+    turn_back(1)
+    first_0.relay()
+    grads = turned[...]
+    grads = grads * cos_ref[...] + swap_halves(grads, 1.0, -1.0) * sin_ref[...]
+    mixed_grad[...] = grads.astype(bf16)
+    part[...] = (
+        dot(mixed_grad[...], entry_ref[...], ((1,), (1,))).astype(bf16).reshape(part.shape)
+    )
+    rows = Reduce(send, 42, "seq", lambda i: part.at[i], bufs[7], half_rows)
+    rows.start_far()
+    rows.start_near()
+
+    def entry_rows(block):
+        rows_of = slice(QOWN * block, QOWN * (block + 1))
+        grad = dot(normed_ref[:, rows_of], mixed_grad[...], ((0,), (0,))).astype(bf16)
+        return spread(grad)
+
+    full[1, :, :, :, :640] = entry_rows(0)
+    full[1, :, :, :, 640:1280] = entry_rows(1)
+    third = entry_rows(2)
+    full[1, :, :, :, 1280:] = third[..., :256]
+    swaps.append(swap(1))
     rows.relay()
-    full[1, :, :, :, :512] = second[..., 128:]
-    full[1, :, :, :, 512:1152] = entry_rows(2)
-    full[1, :, :, :, 1152:1792] = entry_rows(3)
+    second_0 = second_sum(0, "y", first_0)
+    full[2, :, :, :, :384] = third[..., 256:]
+    full[2, :, :, :, 384:1024] = entry_rows(3)
+    chip_sum(1, swaps[1])
+    first_1 = first_sum(1, "x")
     back, gain_one = norm_back(in_ref[...].astype(f32), gain_ref[...], rows.total())
     input_ref[...] = (grad_ref[...] + back).astype(bf16)
     row_of = lax.broadcasted_iota(jnp.int32, (128, D), 0)
@@ -639,51 +765,32 @@
     gains = jnp.where(row_of == EXPERTS + 1, gain_two_ref[...], gains)
     shared = router_grad_ref[...] + gains.T
     for block in range(4):
-        part = shared[QOWN * block : QOWN * (block + 1), :].astype(bf16)
-        full[1, :, :, :, 1792 + 128 * block : 1920 + 128 * block] = spread(part)
-    swaps.append(swap(1))
-    outs = Reduce(send, 6, "seq", lambda i: out_sum_ref.at[i], bufs[1], half_rows)
-    outs.start_far()
-    outs.start_near()
-    swaps[0].wait_recv()
-    for plane in range(16):
-        added(chip.at[0, plane // 4, plane % 4], full.at[0, plane, c], from_core.at[0, plane])
-    low_x = Reduce(send, 12, "x", lambda i: chip.at[0, i], bufs[2], half_rows)
-    low_x.start_far()
-    low_x.start_near()
-    swaps[1].wait_recv()
-    for plane in range(16):
-        added(chip.at[1, plane % 4, plane // 4], full.at[1, plane, c], from_core.at[1, plane])
-    high_y = Reduce(send, 18, "y", lambda i: chip.at[1, i], bufs[3], half_rows)
-    high_y.start_far()
-    high_y.start_near()
-    low_x.relay()
-    high_y.relay()
-    outs.relay()
-    line[0] = low_x.total().astype(bf16)
-    low_y = Reduce(send, 24, "y", lambda i: line.at[0, i], bufs[4], half_lanes)
-    low_y.start_far()
-    low_y.start_near()
-    line[1] = high_y.total().astype(bf16)
-    high_x = Reduce(send, 30, "x", lambda i: line.at[1, i], bufs[5], half_lanes)
-    high_x.start_far()
-    high_x.start_near()
-    low_y.relay()
-    high_x.relay()
+        shared_rows = shared[QOWN * block : QOWN * (block + 1), :].astype(bf16)
+        full[2, :, :, :, 1024 + 128 * block : 1152 + 128 * block] = spread(shared_rows)
+    swaps.append(swap(2))
+    second_0.relay()
     block_ref[...] = (middle_ref[...] + outs.total()).astype(bf16)
-    final[0] = low_y.total()
-    final[1] = high_x.total()
-    exit_out[...] = final[0, :, :1536]
-    give[0, :, :MIX_OWN] = final[0, :, 1536:2176]
-    give[1, :, :128] = final[0, :, 2176:2304]
-    give[1, :, 128:MIX_OWN] = final[1, :, :512]
-    give[2, :, :MIX_OWN] = final[1, :, 512:1152]
-    give[3, :, :MIX_OWN] = final[1, :, 1152:1792]
+    chip_sum(2, swaps[2])
+    first_2 = first_sum(2, "y")
+    first_1.relay()
+    first_2.relay()
+    exit_out[...] = second_0.total()
+    second_1 = second_sum(1, "y", first_1)
+    second_2 = second_sum(2, "x", first_2)
+    second_1.relay()
+    second_2.relay()
+    final[0] = second_1.total()
+    final[1] = second_2.total()
+    give[0, :, :MIX_OWN] = final[0, :, :640]
+    give[1, :, :MIX_OWN] = final[0, :, 640:1280]
+    give[2, :, :256] = final[0, :, 1280:]
+    give[2, :, 256:MIX_OWN] = final[1, :, :384]
+    give[3, :, :MIX_OWN] = final[1, :, 384:1024]
     for block in range(4):
-        give[block, :, MIX_OWN:] = final[1, :, 1792 + 128 * block : 1920 + 128 * block]
-    peers = (right, far, left)
+        give[block, :, MIX_OWN:] = final[1, :, 1024 + 128 * block : 1152 + 128 * block]
     home = [
-        send(give.at[peer], got_z.at[k], 38 + k, "seq", peer) for k, peer in enumerate(peers)
+        send(give.at[peer], got_z.at[k], 51 + k, "seq", peer)
+        for k, peer in enumerate((right, far, left))
     ]
     entry_out[z] = give[z]
     for k, source in enumerate((left, far, right)):
@@ -691,15 +798,15 @@
         entry_out[source] = got_z[k]
     for copy in swaps + home:
         copy.wait_send()
-    for reduce in (rows, outs, low_x, high_y, low_y, high_x):
+    for reduce in (rows, outs, first_0, first_1, first_2, second_0, second_1, second_2):
         reduce.drain()
 
 
 def closing(*operands):
     row_bufs = reduce_scratch((TOK_DEV, D), (HALF, D))
-    chip_bufs = reduce_scratch((4, PAD_ROWS, HALF_WIDE), (2, PAD_ROWS, HALF_WIDE))
-    line_bufs = reduce_scratch((PAD_ROWS, HALF_WIDE), (PAD_ROWS, HALF_WIDE // 2))
-    tile = (PAD_ROWS, HALF_WIDE)
+    chip_bufs = reduce_scratch((4, PAD_ROWS, D), (2, PAD_ROWS, D))
+    line_bufs = reduce_scratch((PAD_ROWS, D), (PAD_ROWS, D // 2))
+    tile = (PAD_ROWS, D)
     return pl.pallas_call(
         closing_kernel,
         out_shape=[
@@ -708,23 +815,67 @@
             jax.ShapeDtypeStruct((4, PAD_ROWS, WIDE), f32),
             jax.ShapeDtypeStruct((PAD_ROWS, D), f32),
         ],
-        in_specs=[VMEM] * 12,
+        in_specs=[VMEM] * len(operands),
         out_specs=[VMEM] * 4,
         scratch_shapes=[
-            pltpu.VMEM((2, 16, 2) + tile, bf16),
-            pltpu.VMEM((2, 16) + tile, bf16),
-            pltpu.VMEM((2, 4, 4) + tile, bf16),
-            pltpu.VMEM((2, 4) + tile, bf16),
+            pltpu.VMEM((GROUP, MIX_OWN), f32),
+            pltpu.VMEM((GROUP, MIX_OWN), bf16),
+            pltpu.VMEM((N_SEQ, TOK_DEV, D), bf16),
+            pltpu.VMEM((3, 16, 2) + tile, bf16),
+            pltpu.VMEM((3, 16) + tile, bf16),
+            pltpu.VMEM((3, 4, 4) + tile, bf16),
+            pltpu.VMEM((3, 4) + tile, bf16),
             pltpu.VMEM((2,) + tile, f32),
             pltpu.VMEM((4, PAD_ROWS, WIDE), f32),
             pltpu.VMEM((3, PAD_ROWS, WIDE), f32),
         ]
+        + chip_bufs * 3
+        + line_bufs * 3
         + row_bufs * 2
-        + chip_bufs * 2
-        + line_bufs * 2
-        + sems(41),
+        + sems(54),
         compiler_params=remote_params(5),
     )(*operands)
+
+
+def owner_kernel(sum_ref, expand_ref, shrink_ref, send_sem, recv_sem, copy_sem):
+    core = lax.axis_index("core")
+    greet([sibling()])
+    send = sender(send_sem, recv_sem)
+    experts = pl.ds(core * LOCAL_E, LOCAL_E)
+
+    def pieces(owner):
+        main = pl.ds(pl.multiple_of(owner * 48, 16), 48)
+        left = pl.ds(pl.multiple_of(96 + owner * 16, 16), 16)
+        ends = pl.ds(pl.multiple_of(owner * 512, 512), 512)
+        return [
+            (sum_ref.at[:, main], expand_ref.at[experts]),
+            (sum_ref.at[:, left], shrink_ref.at[experts, :, pl.ds(0, 1024)]),
+            (sum_ref.at[:, pl.ds(128, 16), ends], shrink_ref.at[experts, :, pl.ds(1024, 512)]),
+        ]
+
+    copies = [
+        send(source, target, k, "core", 1 - core)
+        for k, (source, target) in enumerate(pieces(1 - core))
+    ]
+    for k, (source, target) in enumerate(pieces(core)):
+        copies.append(pltpu.make_async_copy(source, target, copy_sem.at[k]))
+        copies[-1].start()
+    for copy in copies:
+        copy.wait()
+
+
+def to_owners(summed):
+    return pl.pallas_call(
+        owner_kernel,
+        out_shape=[
+            jax.ShapeDtypeStruct((2 * LOCAL_E, 48, 1024), bf16),
+            jax.ShapeDtypeStruct((2 * LOCAL_E, 16, D), bf16),
+        ],
+        in_specs=[VMEM],
+        out_specs=[VMEM] * 2,
+        scratch_shapes=sems(3) + [pltpu.SemaphoreType.DMA((3,))],
+        compiler_params=remote_params(6),
+    )(summed)
 
 
 def dispatch_kernel(rank_ref, gate_ref, tokens_ref, cots_ref, rows_ref, cot_rows_ref, row_gate_ref):
@@ -906,7 +1057,6 @@
     in_all, cots, hit_slots, entry_own, shared, exit_own = start(
         rows_in, cots_in, hit_slots, jnp.pad(entry_cols, pad), jnp.pad(exit_cols, pad)
     )
-    in_all = in_all.reshape(GROUP, D)
     gains_full = shared[:, EXPERTS : EXPERTS + 2].astype(f32).T
 
     order_row = deal_order[0]
@@ -924,30 +1074,24 @@
     positions = token - jnp.sum(jnp.where(seq_match, starts[None, :], 0), axis=1)
     frequency = rope_base ** (-jnp.arange(HD // 2, dtype=f32) * 2.0 / HD)
     phase = positions.astype(f32)[:, None] * frequency[None, :]
-    cosine, sine = jnp.cos(phase)[:, None, :], jnp.sin(phase)[:, None, :]
-    allowed = (seq_ids[:, None] == seq_ids[None, :]) & (token[None, :] <= token[:, None])
-
-    normed = norm_apply(in_all.astype(f32), gains_full[0]).astype(bf16)
-    mixed = dot(normed, entry_own, ((1,), (0,)))
-    queries = rotate(mixed[:, :Q_OWN].reshape(GROUP, HEADS_OWN, HD), cosine, sine)
-    pairs = mixed[:, Q_OWN:].reshape(GROUP, KV_HEADS_OWN, 2, HD)
-    keys = rotate(pairs[:, :, 0], cosine, sine)
-    queries = queries.astype(bf16).reshape(GROUP, KV_HEADS_OWN, PER_KV, HD)
-    keys, values = keys.astype(bf16), pairs[:, :, 1].astype(bf16)
-    scores = jnp.einsum("qhgd,khd->hgqk", queries, keys, preferred_element_type=f32) * HD**-0.5
-    scores = jnp.where(allowed[None, None], scores, -1e30)
-    peak = jnp.max(scores, axis=-1, keepdims=True)
-    expo = jnp.exp(scores - peak)
-    probs = expo / jnp.sum(expo, axis=-1, keepdims=True)
-    probs_b = probs.astype(bf16)
-    attended = (
-        jnp.einsum("hgqk,khd->qhgd", probs_b, values, preferred_element_type=f32)
-        .reshape(GROUP, Q_OWN)
-        .astype(bf16)
-    )
-    branch_part = dot(attended, exit_own, ((1,), (0,))).astype(bf16)
-    middle, tokens = middle_tokens(
-        branch_part.reshape(N_SEQ, TOK_DEV, D), activations[0], gains_full[1:2]
+    ones = jnp.ones((GROUP, HD), f32)
+    cosine, sine = jnp.tile(jnp.cos(phase), (1, 2)), jnp.tile(jnp.sin(phase), (1, 2))
+    cosine = jnp.concatenate(
+        [jnp.tile(cosine, (1, HEADS_OWN))] + [cosine, ones] * KV_HEADS_OWN, axis=1
+    )
+    sine = jnp.concatenate(
+        [jnp.tile(sine, (1, HEADS_OWN))] + [sine, 0.0 * ones] * KV_HEADS_OWN, axis=1
+    )
+    angles = (cosine, sine, seq_ids[:, None], seq_ids[None, :])
+
+    normed, qkv, attended, lse, middle, tokens = middle_tokens(
+        in_all,
+        gains_full[0:1],
+        entry_own,
+        *angles,
+        exit_own,
+        activations[0],
+        gains_full[1:2],
     )
     normed_two = lax.dynamic_slice(tokens, (core, seq, 0, 0), (1, 1, TOK_DEV, D))[0, 0]
     tokens = tokens.reshape(PAIR_TOK, D)
@@ -978,31 +1122,16 @@
     branch_grad = branch_grad.reshape(GROUP, D)
     router_grad = dot(normed_two, logit_grad, ((0,), (0,)))
 
-    attended_grad = dot(branch_grad, exit_own, ((1,), (1,))).astype(bf16)
-    attended_grad = attended_grad.reshape(GROUP, KV_HEADS_OWN, PER_KV, HD)
-    prob_grad = jnp.einsum("qhgd,khd->hgqk", attended_grad, values, preferred_element_type=f32)
-    delta = jnp.sum(probs * prob_grad, axis=-1, keepdims=True)
-    score_grad = (probs * (prob_grad - delta) * HD**-0.5).astype(bf16)
-    query_grad = jnp.einsum("hgqk,khd->qhgd", score_grad, keys, preferred_element_type=f32)
-    key_grad = jnp.einsum("hgqk,qhgd->khd", score_grad, queries, preferred_element_type=f32)
-    value_grad = jnp.einsum("hgqk,qhgd->khd", probs_b, attended_grad, preferred_element_type=f32)
-    query_grad = rotate(query_grad.reshape(GROUP, HEADS_OWN, HD), cosine, -sine)
-    key_grad = rotate(key_grad, cosine, -sine)
-    mixed_grad = jnp.concatenate(
-        [
-            query_grad.reshape(GROUP, Q_OWN),
-            jnp.stack([key_grad, value_grad], axis=2).reshape(GROUP, KV_OWN),
-        ],
-        axis=1,
-    ).astype(bf16)
-    normed_part = dot(mixed_grad, entry_own, ((1,), (1,))).astype(bf16)
     input_grad, block_output, entry_got, exit_got = closing(
-        normed_part.reshape(N_SEQ, TOK_DEV, D),
+        qkv,
+        lse,
+        *angles,
+        exit_own,
+        entry_own,
         activations[0],
         middle_grad,
         gains_full[0:1],
         normed,
-        mixed_grad,
         attended,
         branch_grad,
         router_grad,
@@ -1024,22 +1153,8 @@
     gains_sum = shared_sum[:, EXPERTS : EXPERTS + 2].T
     exit_sum = exit_got[:ROWS]
 
-    ends = expert_sum[:, 128:].reshape(LOCAL_E, 16, 2, 512).transpose(2, 0, 1, 3)
-    rows_of = jnp.stack(
-        [
-            jnp.concatenate([expert_sum[:, :48], expert_sum[:, 96:112]], axis=1),
-            jnp.concatenate([expert_sum[:, 48:96], expert_sum[:, 112:128]], axis=1),
-        ]
-    )
-
-    def to_owner(value):
-        mine = lax.dynamic_index_in_dim(value, core, 0, keepdims=False)
-        other = core_swap(lax.dynamic_index_in_dim(value, 1 - core, 0, keepdims=False))
-        return core_order(core, mine, other, 0).astype(f32)
-
-    rows_of, ends = to_owner(rows_of), to_owner(ends)
-    expand_sum = rows_of[:, :48]
-    shrink_sum = jnp.concatenate([rows_of[:, 48:], ends], axis=2)
+    expand_sum, shrink_sum = to_owners(expert_sum)
+    expand_sum, shrink_sum = expand_sum.astype(f32), shrink_sum.astype(f32)
     entry_new = adamw_step(entry_weight, entry_sum, entry_mean, entry_square, 0.02, weight_decay)
     exit_new = adamw_step(exit_weight, exit_sum, exit_mean, exit_square, 0.15, weight_decay)
     router_new = adamw_step(

time: 387 us -> 385 us (level)
  matrix products: 53.3 us -> 6.52 us
  Pallas kernels: 247 us -> 274 us
  waiting for transfers between devices: 26 us -> 48.3 us
    dot_general x5 -> x0, matrix products: 33.4 us -> none  [the longest x1 11.4 us: on_device(): jnp.einsum('hgqk,khd->qhgd', score_grad, keys, preferred_element_type=f32)]
    unnamed x3, waiting for transfers between devices: 0.03 us -> 22 us
    pallas_call x1 -> x2, Pallas kernels: 35.3 us -> 53.4 us  [the longest x1 48.4 us: middle_tokens(): pl.pallas_call(middle_kernel, out_shape=[jax.ShapeDtypeStruct((GROUP, D),...]
    pallas_call x1, Pallas kernels: 60.7 us -> 69.3 us  [closing(): pl.pallas_call(closing_kernel, out_shape=[jax.ShapeDtypeStruct((TOK_DEV,...]
    dot_general x7 -> x3, matrix products: 15 us -> 6.52 us  [dot(): return lax.dot_general(a, b, (dims, ((), ())), preferred_element_type=f32)]
    sub x1 -> x0, matrix products: 4.91 us -> none  [on_device(): expo = jnp.exp(scores - peak)]
    sub x6, other arithmetic: 9.54 us -> 13.7 us  [adamw_step(): weight - rate * (mean_hat / (jnp.sqrt(square_hat) + adam_eps) + decay * w...]
  transfers between devices with their start and end apart: 5 -> 3, of which waited for: 2 -> 2; matrix products, arithmetic and copies ran while one was open for 21% -> 8% of each run, Pallas kernels for 56% -> 62%
where the time goes in v4:
time: 385 us; the launch traced here: 380 us
  Pallas kernels  274 us (71%)
  waiting for transfers between devices  48.3 us (13%)
  other arithmetic  19.6 us (5%)
  local copies, waits for them, and re-layouts  16 us (4%)
  between operations  15.1 us (4%)
  matrix products  6.52 us (2%)
    pallas_call x1, Pallas kernels, closing(): pl.pallas_call(closing_kernel, out_shape=[jax.ShapeDtypeStruct((TOK_DEV,...  69.3 us
    pallas_call x1, Pallas kernels, turn(): pl.pallas_call(turn_kernel, grid=(LOCAL_E + 1,), in_specs=[pl.BlockSpec((...  55.9 us
    pallas_call x1, Pallas kernels, start(): pl.pallas_call(start_kernel, out_shape=[jax.ShapeDtypeStruct((N_SEQ, TOK_...  49.6 us
    pallas_call x1, Pallas kernels, middle_tokens(): pl.pallas_call(middle_kernel, out_shape=[jax.ShapeDtypeStruct((GROUP, D),...  48.4 us
    pallas_call x1, Pallas kernels, expert_grads(): pl.pallas_call(grads_kernel, grid=(LOCAL_E,), in_specs=[pl.BlockSpec((1,...  26.4 us
    all_gather x1, waiting for transfers between devices, on_device(): weights = lax.all_gather(packed, PLANE, axis=0, tiled=False)  26.3 us
    unnamed x3, waiting for transfers between devices  22 us
    sub x6, other arithmetic, adamw_step(): weight - rate * (mean_hat / (jnp.sqrt(square_hat) + adam_eps) + decay * w...  13.7 us
  transfers between devices with their start and end apart: 3, of which 2 were waited for; matrix products, arithmetic and copies ran while one was open for 8% of the time, Pallas kernels for 62%

profile of v4, /device:TPU:1, one launch (start us, length us, event | category | flops | bytes accessed | tf_op | source)
XLA Modules:
  0.0 380.1 jit_solution(2177845628133268964)
XLA Ops:
  7.3 6.4 %shard_map.374 = bf16[5,144,1024]{2,1,0:T(8,128)(2,1)} custom-call(f32[10,48,1024]{2,1,0:T(8,128)} %expand_ref.1, f32[10,16,1536]{2,1,0:T(8,128)} %shrink_ref.1), custom_call_target="tpu_custom_call" | custom-call | tf_op jit(solution)/shard_map/pallas_call | solution.py:263
  16.4 0.7 fusion.20.entry_ref
  17.1 49.6 %shard_map.375 = (bf16[4,128,1536]{2,1,0:T(8,128)(2,1)}, bf16[2,4,128,1536]{3,2,1,0:T(8,128)(2,1)}, bf16[4,128,128]{2,1,0:T(8,128)(2,1)}, bf16[1536,640]{1,0:T(8...) custom-call(bf16[128,1536]{1,0:T(8,128)(2,1)} %bitcast.78, bf16[128,1536]{1,0:T(8,128)(2,1)} %bitcast.95, ...), custom_call_target="tpu_custom_call" | custom-call | tf_op jit(solution)/shard_map/pallas_call | solution.py:367
  66.7 1.2 convolution_convert_fusion
  68.3 0.9 copy.160.seq_col_ref
  69.1 1.2 copy.153
  72.4 1.8 concatenate.22.sin_ref
  74.2 1.3 concatenate.21.cos_ref
  75.6 48.4 %shard_map.376 = (bf16[512,1536]{1,0:T(8,128)(2,1)}, bf16[512,640]{1,0:T(8,128)(2,1)}, bf16[512,384]{1,0:T(8,128)(2,1)}, f32[512,6]{1,0:T(8,128)}, f32[128,1536]...) custom-call(bf16[4,128,1536]{2,1,0:T(8,128)(2,1)} %get-tuple-element.54.all_ref, ...), custom_call_target="tpu_custom_call" | custom-call | tf_op jit(solution)/shard_map/pallas_call | solution.py:463
  124.4 1.4 reduce-window.11
  126.7 0.8 copy.164.rank_ref
  127.5 3.1 fusion.30
  131.5 0.8 copy.165.gate_ref
  132.3 13.4 %shard_map.377 = (bf16[5,256,1536]{2,1,0:T(8,128)(2,1)}, bf16[5,256,1536]{2,1,0:T(8,128)(2,1)}, f32[5,256,1]{2,1,0:T(8,128)}) custom-call(s32[5,1,1024]{2,1,0:T(1,128)} %copy.164.rank_ref, f32[5,1,1024]{2,1,0:T(1,128)} %copy.165.gate_ref, bf16[1024,1536]{1,0:T(8,128)(2,1)} %bitcast.106, bf16[1024,1536]{1,0:T(8,128)(2,1)} %bitcast.112), custom_call_target="tpu_custom_call" | custom-call | flops 8053063680 | bytes 16777216 | tf_op jit(solution)/shard_map/pallas_call | solution.py:894
  145.7 26.3 %all-gather.3.cloned.1.call-done = bf16[80,144,1024]{2,1,0:T(8,128)(2,1)} async-done(((bf16[5,144,1024]{2,1,0:T(8,128)(2,1)}), bf16[80,144,1024]{2,1,0:T(8,128)(2,1)}) %all-gather.3.cloned.1.call-update) | async-done | bytes 23592976 | tf_op jit(solution)/shard_map/all_gather | solution.py:1040
  171.9 26.4 %shard_map.378 = (bf16[5,256,512]{2,1,0:T(8,128)(2,1)}, bf16[5,256,1024]{2,1,0:T(8,128)(2,1)}, bf16[16,5,144,1024]{3,2,1,0:T(8,128)(2,1)}) custom-call(bf16[5,256,1536]{2,1,0:T(8,128)(2,1)} %get-tuple-element.63.rows_ref, bf16[5,256,1536]{2,1,0:T(8,128)(2,1)} %get-tuple-element.64.cot_ref.cot_rows_ref, f32[5,256,1]{2,1,0:T(8,128)} %get-tuple-element.65.gate_ref, ...), custom_call_target="tpu_custom_call" | custom-call | flops 12079595520 | bytes 62914560 | tf_op jit(solution)/shard_map/pallas_call | solution.py:952
  199.0 55.9 %shard_map.379 = (f32[128,1536]{1,0:T(8,128)}, bf16[4,128,1536]{2,1,0:T(8,128)(2,1)}, bf16[128,128]{1,0:T(8,128)(2,1)}, f32[1,1536]{1,0:T(1,128)}, bf16[4,128,1536]{2,1,0:T(8,128)(2,1)}) custom-call(s32[1024,5]{1,0:T(8,128)} %copy-done.2, bf16[5,256,1024]{2,1,0:T(8,128)(2,1)} %get-tuple-element.67.up_ref, bf16[5,256,512]{2,1,0:T(8,128)(2,1)} %get-tuple-element.68.hidden_ref, ...), custom_call_target="tpu_custom_call" | custom-call | flops 14092861440 | bytes 41943040 | tf_op jit(solution)/shard_map/pallas_call | solution.py:592
  255.0 2.2 fusion.8.router_grad_ref
  257.2 69.3 %shard_map.380 = (bf16[128,1536]{1,0:T(8,128)(2,1)}, bf16[128,1536]{1,0:T(8,128)(2,1)}, f32[4,16,768]{2,1,0:T(8,128)}, f32[16,1536]{1,0:T(8,128)}) custom-call(bf16[512,640]{1,0:T(8,128)(2,1)} %get-tuple-element.58.qkv_ref, f32[512,6]{1,0:T(8,128)} %get-tuple-element.59.lse_ref, f32[512,640]{1,0:T(8,128)} %concatenate.21.cos_ref, ...), custom_call_target="tpu_custom_call" | custom-call | tf_op jit(solution)/shard_map/pallas_call | solution.py:810
  326.6 0.8 slice_reduce_fusion
  328.2 0.9 slice_bitcast_fusion
  329.1 0.9 slice_bitcast_fusion.1
  330.2 1.5 multiply_subtract_fusion.5
  331.6 1.3 multiply_subtract_fusion.4
  333.0 1.7 multiply_subtract_fusion.3
  334.7 0.8 multiply_subtract_fusion.2
  335.6 22.0 %reduce-scatter.4.cloned.1.call-done = bf16[1,5,144,1024]{3,2,1,0:T(8,128)(2,1)} async-done(((bf16[16,5,144,1024]{3,2,1,0:T(8,128)(2,1)}), bf16[1,5,144,1024]{3,2,1,0:T(8,128)(2,1)}) %reduce-scatter.4.cloned.1.call-update) | async-done | bytes 1474576
  357.6 5.0 %shard_map.381 = (bf16[10,48,1024]{2,1,0:T(8,128)(2,1)}, bf16[10,16,1536]{2,1,0:T(8,128)(2,1)}) custom-call(bf16[5,144,1024]{2,1,0:T(8,128)(2,1)} %bitcast.86), custom_call_target="tpu_custom_call" | custom-call | tf_op jit(solution)/shard_map/pallas_call | solution.py:868
  362.7 3.3 multiply_subtract_fusion.1
  366.3 5.0 %multiply_subtract_fusion = (f32[10,48,1024]{2,1,0:T(8,128)}, f32[10,48,1024]{2,1,0:T(8,128)}, f32[10,48,1024]{2,1,0:T(8,128)}) fusion(f32[10,48,1024]{2,1,0:T(8,128)S(1)} %copy-done, bf16[10,48,1024]{2,1,0:T(8,128)(2,1)} %get-tuple-element.82, f32[10,48,1024]{2,1,0:T(8,128)S(1)} %copy-done.3, f32[10,48,1024]{2,1,0:T(8,128)S(1)} %copy-done.4), kind=kLoop, calls=%fused_computation.4 | loop fusion | flops 7864320 | bytes 12779520 | tf_op jit(solution)/shard_map/sub | solution.py:998
  371.3 0.7 copy.183
  372.1 0.7 copy.184
  (107 shorter events, 9.1 us)
Async XLA Ops:
  7.2 6.6 %copy-start.7 = (f32[12,2560]{1,0:T(8,128)S(1)}, f32[12,2560]{1,0:T(8,128)}, u32[]{:S(2)}) copy-start(f32[12,2560]{1,0:T(8,128)} %param.28) | copy-start | bytes 368644
  7.2 6.6 %copy-start.17 = (f32[2,12]{1,0:T(2,128)S(1)}, f32[2,12]{1,0:T(2,128)}, u32[]{:S(2)}) copy-start(f32[2,12]{1,0:T(2,128)} %param.43) | copy-start | bytes 292
  7.2 6.7 %copy-start.15 = (f32[12,40]{1,0:T(8,128)S(1)}, f32[12,40]{1,0:T(8,128)}, u32[]{:S(2)}) copy-start(f32[12,40]{1,0:T(8,128)} %param.34) | copy-start | bytes 5764
  7.2 164.7 %all-gather.3.cloned.1.call-start = ((), (), s32[]{:S(2)}) async-start(), calls=%async_computation.1 | async-start | bytes 25067520 | tf_op jit(solution)/shard_map/all_gather | solution.py:1040
  13.7 0.9 copy-start.11
  13.7 0.9 copy-start.16
  13.7 53.0 %copy-start.18 = (s32[1,512]{1,0:T(1,128)S(1)}, s32[1,512]{1,0:T(1,128)}, u32[]{:S(2)}) copy-start(s32[1,512]{1,0:T(1,128)} %param.26) | copy-start | bytes 6148
  13.7 54.3 %copy-start.19 = (s32[1,3]{1,0:T(1,128)S(1)}, s32[1,3]{1,0:T(1,128)}, u32[]{:S(2)}) copy-start(s32[1,3]{1,0:T(1,128)} %param.25) | copy-start | bytes 40
  13.7 343.8 %reduce-scatter.4.cloned.1.call-start = ((), (), s32[]{:S(2)}) async-start(), calls=%async_computation.2 | async-start | bytes 25067520
  67.9 56.1 %collective-permute-start = (bf16[512,128]{1,0:T(8,128)(2,1)S(1)}, bf16[512,128]{1,0:T(8,128)(2,1)S(1)}, u32[]{:S(2)}, u32[]{:S(2)}) collective-permute-start(bf16[512,128]{1,0:T(8,128)(2,1)S(1)} %convolution_convert_fusion), channel_id=1, source_target_pairs={{0,1},{1,0},{2,3},{3,2},{4,5},{5,4},{6,7},{7,6},{8,9},{9,8},{10,11... | collective-permute-start | bytes 393224 | tf_op jit(solution)/shard_map/ppermute | solution.py:979
  68.3 3.8 copy-start.14
  124.0 3.5 copy-start.8
  126.7 3.9 %copy-start.2 = (s32[1024,5]{1,0:T(8,128)}, s32[1024,5]{1,0:T(8,128)S(1)}, u32[]{:S(2)}) copy-start(s32[1024,5]{1,0:T(8,128)S(1)} %bitcast_select_fusion.rank_ref) | copy-start | bytes 61444
  326.6 8.1 %copy-start.12 = (f32[12,2560]{1,0:T(8,128)S(1)}, f32[12,2560]{1,0:T(8,128)}, u32[]{:S(2)}) copy-start(f32[12,2560]{1,0:T(8,128)} %param.30) | copy-start | bytes 368644
  326.6 8.1 %copy-start.13 = (f32[12,2560]{1,0:T(8,128)S(1)}, f32[12,2560]{1,0:T(8,128)}, u32[]{:S(2)}) copy-start(f32[12,2560]{1,0:T(8,128)} %param.29) | copy-start | bytes 368644
  330.1 32.6 %copy-start.1 = (f32[10,16,1536]{2,1,0:T(8,128)S(1)}, f32[10,16,1536]{2,1,0:T(8,128)}, u32[]{:S(2)}) copy-start(f32[10,16,1536]{2,1,0:T(8,128)} %shrink_ref.1) | copy-start | bytes 2949124
  330.1 32.6 %copy-start.5 = (f32[10,16,1536]{2,1,0:T(8,128)S(1)}, f32[10,16,1536]{2,1,0:T(8,128)}, u32[]{:S(2)}) copy-start(f32[10,16,1536]{2,1,0:T(8,128)} %param.42) | copy-start | bytes 2949124
  330.1 32.6 %copy-start.6 = (f32[10,16,1536]{2,1,0:T(8,128)S(1)}, f32[10,16,1536]{2,1,0:T(8,128)}, u32[]{:S(2)}) copy-start(f32[10,16,1536]{2,1,0:T(8,128)} %param.41) | copy-start | bytes 2949124
  362.7 3.3 copy-start
  362.7 3.3 copy-start.3
  362.7 3.6 copy-start.4
  366.3 5.0 %copy-start.10 = (bf16[128,1536]{1,0:T(8,128)(2,1)S(1)}, bf16[128,1536]{1,0:T(8,128)(2,1)}, u32[]{:S(2)}) copy-start(bf16[128,1536]{1,0:T(8,128)(2,1)} %get-tuple-element.77) | copy-start | bytes 1179652
  366.3 5.7 %copy-start.9 = (bf16[128,1536]{1,0:T(8,128)(2,1)S(1)}, bf16[128,1536]{1,0:T(8,128)(2,1)}, u32[]{:S(2)}) copy-start(bf16[128,1536]{1,0:T(8,128)(2,1)} %get-tuple-element.78) | copy-start | bytes 1179652
Sparse Core Ops, SparseCore 0:
  13.9 158.0 all-gather.2
  198.5 159.0 reduce-scatter.3

commit v5 on v4

--- a/solution.py
+++ b/solution.py
@@ -42,7 +42,7 @@
 bf16 = jnp.bfloat16
 
 
-BIG = 56 * 1024 * 1024
+BIG = 60 * 1024 * 1024
 HALF = TOK_DEV // 2
 QOWN = Q_OWN
 MESH = pl.DeviceIdType.MESH
@@ -61,9 +61,9 @@
     pl.semaphore_wait(barrier, len(peers))
 
 
-def sender(send_sem, recv_sem):
-    def send(src, dst, index, axis, peer):
-        copy = pltpu.make_async_remote_copy(
+def planner(send_sem, recv_sem):
+    def plan(src, dst, index, axis, peer):
+        return pltpu.make_async_remote_copy(
             src_ref=src,
             dst_ref=dst,
             send_sem=send_sem.at[index],
@@ -71,6 +71,15 @@
             device_id={axis: peer},
             device_id_type=MESH,
         )
+
+    return plan
+
+
+def sender(send_sem, recv_sem):
+    plan = planner(send_sem, recv_sem)
+
+    def send(*args):
+        copy = plan(*args)
         copy.start()
         return copy
 
@@ -106,26 +115,31 @@
 
 
 class Gather:
-    def __init__(self, send, base, axis, mine, slot, cut):
-        self.send, self.base, self.axis, self.slot, self.cut = send, base, axis, slot, cut
+    def __init__(self, plan, base, axis, mine, slot, cut):
         me = lax.axis_index(axis)
-        self.right, self.left, self.far = ring(me)
-        here = slot(me)
+        right, left, self.far = ring(me)
+        self.right, self.left = right, left
+        here, from_left, from_right = slot(me), cut(slot(left), 0), cut(slot(right), 1)
         self.first = [
-            send(cut(mine, 0), cut(here, 0), base, axis, self.right),
-            send(cut(mine, 1), cut(here, 1), base + 1, axis, self.left),
-            send(cut(mine, 1), cut(here, 1), base + 2, axis, self.right),
-            send(cut(mine, 0), cut(here, 0), base + 3, axis, self.left),
+            plan(cut(mine, 0), cut(here, 0), base, axis, right),
+            plan(cut(mine, 1), cut(here, 1), base + 1, axis, left),
+            plan(cut(mine, 1), cut(here, 1), base + 2, axis, right),
+            plan(cut(mine, 0), cut(here, 0), base + 3, axis, left),
         ]
-        self.later = []
+        self.later = [
+            plan(from_left, from_left, base + 4, axis, right),
+            plan(from_right, from_right, base + 5, axis, left),
+        ]
+
+    def start(self):
+        for copy in self.first:
+            copy.start()
+        return self
 
     def relay(self):
-        self.first[0].wait_recv()
-        part = self.cut(self.slot(self.left), 0)
-        self.later.append(self.send(part, part, self.base + 4, self.axis, self.right))
-        self.first[1].wait_recv()
-        part = self.cut(self.slot(self.right), 1)
-        self.later.append(self.send(part, part, self.base + 5, self.axis, self.left))
+        for got, on in zip(self.first, self.later):
+            got.wait_recv()
+            on.start()
 
     def wait_left(self):
         self.first[2].wait_recv()
@@ -173,44 +187,58 @@
 
 
 class Reduce:
-    def __init__(self, send, base, axis, block, bufs, cut):
-        self.send, self.base, self.axis, self.block = send, base, axis, block
-        self.bufs, self.cut = bufs, cut
-        self.me = lax.axis_index(axis)
-        self.right, self.left, self.far = ring(self.me)
+    def __init__(self, plan, base, axis, block, bufs, cut):
+        me = lax.axis_index(axis)
+        right, left, far = ring(me)
+        from_left, from_right, to_right, to_left, got_left, got_right = bufs
+        far, on_right, on_left = block(far), block(right), block(left)
+        self.mine, self.got = block(me), (got_left, got_right)
+        self.hops = (
+            (to_right, cut(on_right, 0), from_left),
+            (to_left, cut(on_left, 1), from_right),
+        )
+        self.far = [
+            plan(cut(far, 0), from_left, base, axis, right),
+            plan(cut(far, 1), from_right, base + 1, axis, left),
+        ]
+        self.near = [
+            plan(cut(on_right, 1), cut(got_left, 1), base + 2, axis, right),
+            plan(cut(on_left, 0), cut(got_right, 0), base + 3, axis, left),
+        ]
+        self.later = [
+            plan(to_right, cut(got_left, 0), base + 4, axis, right),
+            plan(to_left, cut(got_right, 1), base + 5, axis, left),
+        ]
 
     def start_far(self):
-        far = self.block(self.far)
-        self.copies = [
-            self.send(self.cut(far, 0), self.bufs[0], self.base, self.axis, self.right),
-            self.send(self.cut(far, 1), self.bufs[1], self.base + 1, self.axis, self.left),
-        ]
+        for copy in self.far:
+            copy.start()
 
     def start_near(self):
-        source, target = self.cut(self.block(self.right), 1), self.cut(self.bufs[4], 1)
-        self.copies.append(self.send(source, target, self.base + 2, self.axis, self.right))
-        source, target = self.cut(self.block(self.left), 0), self.cut(self.bufs[5], 0)
-        self.copies.append(self.send(source, target, self.base + 3, self.axis, self.left))
+        for copy in self.near:
+            copy.start()
+
+    def start(self):
+        self.start_far()
+        self.start_near()
+        return self
 
     def relay(self):
-        from_left, from_right, to_right, to_left, got_left, got_right = self.bufs
-        self.copies[0].wait_recv()
-        added(to_right, self.cut(self.block(self.right), 0), from_left)
-        target = self.cut(got_left, 0)
-        self.copies.append(self.send(to_right, target, self.base + 4, self.axis, self.right))
-        self.copies[1].wait_recv()
-        added(to_left, self.cut(self.block(self.left), 1), from_right)
-        target = self.cut(got_right, 1)
-        self.copies.append(self.send(to_left, target, self.base + 5, self.axis, self.left))
+        for got, hop, on in zip(self.far, self.hops, self.later):
+            got.wait_recv()
+            added(*hop)
+            on.start()
 
     def total(self):
-        for copy in self.copies[2:]:
+        for copy in self.near + self.later:
             copy.wait_recv()
-        mine = self.block(self.me)[...].astype(f32)
-        return mine + self.bufs[4][...].astype(f32) + self.bufs[5][...].astype(f32)
+        total = self.mine[...].astype(f32)
+        for part in self.got:
+            total += part[...].astype(f32)
+        return total
 
     def drain(self):
-        for copy in self.copies:
+        for copy in self.far + self.near + self.later:
             copy.wait_send()
 
 
@@ -232,7 +260,10 @@
     return back, jnp.sum(unit * grad, axis=0, keepdims=True)
 
 
-def pack_kernel(expand_ref, shrink_ref, out_ref, stage, stage_end, send_sem, recv_sem):
+MAIN_E = LOCAL_E - 1
+
+
+def pack_kernel(expand_ref, shrink_ref, main_ref, extra_ref, stage, stage_end, send_sem, recv_sem):
     core = lax.axis_index("core")
     greet([sibling()])
     send = sender(send_sem, recv_sem)
@@ -242,19 +273,24 @@
         stage[e, :48] = expand_ref[theirs].astype(bf16)
         stage[e, 48:] = shrink_ref[theirs, :, :1024].astype(bf16)
         stage_end[e] = shrink_ref[theirs, :, 1024:].astype(bf16)
-    main = pl.ds(pl.multiple_of(core * 48, 16), 48)
+    rows = pl.ds(pl.multiple_of(core * 48, 16), 48)
     left = pl.ds(pl.multiple_of(96 + core * 16, 16), 16)
     ends = pl.ds(pl.multiple_of(core * 512, 512), 512)
+    low, most = pl.ds(128, 16), pl.ds(0, MAIN_E)
     copies = [
-        send(stage.at[:, pl.ds(0, 48)], out_ref.at[:, main], 0, "core", other),
-        send(stage.at[:, pl.ds(48, 16)], out_ref.at[:, left], 1, "core", other),
-        send(stage_end, out_ref.at[:, pl.ds(128, 16), ends], 2, "core", other),
+        send(stage.at[most, pl.ds(0, 48)], main_ref.at[:, rows], 0, "core", other),
+        send(stage.at[most, pl.ds(48, 16)], main_ref.at[:, left], 1, "core", other),
+        send(stage_end.at[most], main_ref.at[:, low, ends], 2, "core", other),
+        send(stage.at[MAIN_E, pl.ds(0, 48)], extra_ref.at[rows], 3, "core", other),
+        send(stage.at[MAIN_E, pl.ds(48, 16)], extra_ref.at[left], 4, "core", other),
+        send(stage_end.at[MAIN_E], extra_ref.at[low, ends], 5, "core", other),
     ]
     for e in range(LOCAL_E):
         mine = core * LOCAL_E + e
-        out_ref[e, main, :] = expand_ref[mine].astype(bf16)
-        out_ref[e, left, :] = shrink_ref[mine, :, :1024].astype(bf16)
-        out_ref[e, pl.ds(128, 16), ends] = shrink_ref[mine, :, 1024:].astype(bf16)
+        out = main_ref.at[e] if e < MAIN_E else extra_ref
+        out[rows, :] = expand_ref[mine].astype(bf16)
+        out[left, :] = shrink_ref[mine, :, :1024].astype(bf16)
+        out[low, ends] = shrink_ref[mine, :, 1024:].astype(bf16)
     for copy in copies:
         copy.wait()
 
@@ -262,14 +298,17 @@
 def pack_experts(expand, shrink):
     return pl.pallas_call(
         pack_kernel,
-        out_shape=jax.ShapeDtypeStruct((LOCAL_E, 144, 1024), bf16),
+        out_shape=[
+            jax.ShapeDtypeStruct((MAIN_E, 144, 1024), bf16),
+            jax.ShapeDtypeStruct((144, 1024), bf16),
+        ],
         in_specs=[VMEM] * 2,
-        out_specs=VMEM,
+        out_specs=[VMEM] * 2,
         scratch_shapes=[
             pltpu.VMEM((LOCAL_E, 64, 1024), bf16),
             pltpu.VMEM((LOCAL_E, 16, 512), bf16),
         ]
-        + sems(3),
+        + sems(6),
         compiler_params=remote_params(1),
     )(expand, shrink)
 
@@ -289,13 +328,13 @@
     z, x, y, c = (lax.axis_index(a) for a in ("seq", "x", "y", "core"))
     right, left, far = ring(z)
     greet(near("seq") + [("seq", far)] + near("x") + near("y") + [sibling()])
-    send = sender(send_sem, recv_sem)
+    send, plan = sender(send_sem, recv_sem), planner(send_sem, recv_sem)
     columns = [
         send(entry_ref.at[peer], hold.at[z], k, "seq", peer)
         for k, peer in enumerate((right, far, left))
     ]
-    hits = Gather(send, 3, "seq", hit_ref, lambda i: hit_all.at[i], half_rows)
-    rows = Gather(send, 9, "seq", in_ref, lambda i: in_all.at[i], half_rows)
+    hits = Gather(plan, 3, "seq", hit_ref, lambda i: hit_all.at[i], half_rows).start()
+    rows = Gather(plan, 9, "seq", in_ref, lambda i: in_all.at[i], half_rows).start()
     local = [
         pltpu.make_async_copy(entry_ref.at[z], hold.at[z], copy_sem.at[0]),
         pltpu.make_async_copy(exit_ref, hold.at[pl.ds(4, 2)], copy_sem.at[1]),
@@ -312,13 +351,15 @@
     own = pltpu.make_async_copy(hold, full.at[:, x, y, c], copy_sem.at[5])
     own.start()
     low, high = pl.ds(0, 3), pl.ds(3, 3)
-    low_x = Gather(send, 15, "x", hold.at[low], lambda i: full.at[low, i, y, c], half_lanes)
-    high_y = Gather(send, 21, "y", hold.at[high], lambda i: full.at[high, x, i, c], half_lanes)
+    low_x = Gather(plan, 15, "x", hold.at[low], lambda i: full.at[low, i, y, c], half_lanes)
+    low_x.start()
+    high_y = Gather(plan, 21, "y", hold.at[high], lambda i: full.at[high, x, i, c], half_lanes)
+    high_y.start()
     hits.relay()
     low_x.relay()
     high_y.relay()
     rows.relay()
-    cots = Gather(send, 27, "seq", cot_ref, lambda i: cot_all.at[c, i], half_rows)
+    cots = Gather(plan, 27, "seq", cot_ref, lambda i: cot_all.at[c, i], half_rows).start()
     own.wait()
     low_x.finish()
 
@@ -326,12 +367,12 @@
         return ref.at[:, pl.ds(2 * half, 2)]
 
     low_y = Gather(
-        send, 33, "y", full.at[low, :, y, c], lambda i: full.at[low, :, i, c], cut_low
-    )
+        plan, 33, "y", full.at[low, :, y, c], lambda i: full.at[low, :, i, c], cut_low
+    ).start()
     high_y.finish()
     high_x = Gather(
-        send, 39, "x", full.at[high, x, :, c], lambda i: full.at[high, i, :, c], cut_low
-    )
+        plan, 39, "x", full.at[high, x, :, c], lambda i: full.at[high, i, :, c], cut_low
+    ).start()
     low_y.relay()
     high_x.relay()
     pairs = hand_over(send, 45, cot_ref, cot_all, cots)
@@ -410,21 +451,52 @@
 
 def middle_kernel(
     all_ref, gain_one_ref, entry_ref, cos_ref, sin_ref, seq_col_ref, seq_row_ref, exit_ref,
-    in_ref, gain_ref,
-    normed_ref, qkv_ref, attended_ref, lse_ref, middle_ref, tokens_ref,
+    in_ref, gain_ref, extra_ref,
+    normed_ref, qkv_ref, attended_ref, lse_ref, middle_ref, tokens_ref, extra_all,
     part, mine, *rest
 ):
     bufs, (send_sem, recv_sem, copy_sem) = rest[:6], rest[6:]
     me, core = lax.axis_index("seq"), lax.axis_index("core")
-    greet(near("seq") + [sibling()])
-    send = sender(send_sem, recv_sem)
+    x, y = lax.axis_index("x"), lax.axis_index("y")
+    greet(near("seq") + near("x") + near("y") + [sibling()])
+    send, plan = sender(send_sem, recv_sem), planner(send_sem, recv_sem)
+    low, high = pl.ds(0, 512), pl.ds(512, 512)
+    own = pltpu.make_async_copy(extra_ref, extra_all.at[x, y], copy_sem.at[1])
+    own.start()
+    low_x = Gather(
+        plan, 16, "x", extra_ref.at[:, low], lambda i: extra_all.at[i, y, :, low], half_lanes
+    ).start()
+    high_y = Gather(
+        plan, 22, "y", extra_ref.at[:, high], lambda i: extra_all.at[x, i, :, high], half_lanes
+    ).start()
     for block in range(N_SEQ):
         rows = slice(TOK_DEV * block, TOK_DEV * (block + 1))
         vector = all_ref[block].astype(f32)
         normed_ref[rows, :] = (vector * unit_scale(vector) * gain_one_ref[...]).astype(bf16)
+    low_x.relay()
+    high_y.relay()
     mixed = dot(normed_ref[...], entry_ref[...], ((1,), (0,)))
     mixed = mixed * cos_ref[...] + swap_halves(mixed, -1.0, 1.0) * sin_ref[...]
     qkv_ref[...] = mixed.astype(bf16)
+    own.wait()
+    low_x.finish()
+    low_y = Gather(
+        plan,
+        28,
+        "y",
+        extra_all.at[:, y, :, low],
+        lambda i: extra_all.at[:, i, :, low],
+        half_rows,
+    ).start()
+    high_y.finish()
+    high_x = Gather(
+        plan,
+        34,
+        "x",
+        extra_all.at[x, :, :, high],
+        lambda i: extra_all.at[i, :, :, high],
+        half_rows,
+    ).start()
     for block in range(GROUP // BLOCK):
         bias = block_bias(seq_col_ref, seq_row_ref, block)
         keys = BLOCK * (block + 1)
@@ -441,21 +513,23 @@
             attended_ref[rows, head_of(head)] = dot(probs, value, ((1,), (0,))).astype(bf16)
             lse_ref[rows, head : head + 1] = peak + jnp.log(total)
     part[...] = dot(attended_ref[...], exit_ref[...], ((1,), (0,))).astype(bf16).reshape(part.shape)
-    reduce = Reduce(send, 0, "seq", lambda i: part.at[i], bufs, half_rows)
-    reduce.start_far()
-    reduce.start_near()
+    reduce = Reduce(plan, 0, "seq", lambda i: part.at[i], bufs, half_rows).start()
+    low_y.relay()
+    high_x.relay()
     reduce.relay()
     middle = in_ref[...].astype(f32) + reduce.total()
     middle_ref[...] = middle
     mine[...] = (middle * unit_scale(middle) * gain_ref[...]).astype(bf16)
-    gather = Gather(send, 6, "seq", mine, lambda i: tokens_ref.at[core, i], half_rows)
-    local = pltpu.make_async_copy(mine, tokens_ref.at[core, me], copy_sem)
+    gather = Gather(plan, 6, "seq", mine, lambda i: tokens_ref.at[core, i], half_rows).start()
+    local = pltpu.make_async_copy(mine, tokens_ref.at[core, me], copy_sem.at[0])
     local.start()
     pairs = hand_over(send, 12, mine, tokens_ref, gather)
     for copy in pairs:
         copy.wait()
-    gather.drain()
-    reduce.drain()
+    low_y.finish()
+    high_x.finish()
+    for transfer in (gather, reduce, low_x, high_y, low_y, high_x):
+        transfer.drain()
     local.wait()
 
 
@@ -469,33 +543,50 @@
             jax.ShapeDtypeStruct((GROUP, HEADS_OWN), f32),
             jax.ShapeDtypeStruct((TOK_DEV, D), f32),
             jax.ShapeDtypeStruct((2, N_SEQ, TOK_DEV, D), bf16),
-        ],
-        in_specs=[VMEM] * 10,
-        out_specs=[VMEM] * 5 + [ANY],
+            jax.ShapeDtypeStruct((4, 4, 144, 1024), bf16),
+        ],
+        in_specs=[VMEM] * 10 + [ANY],
+        out_specs=[VMEM] * 5 + [ANY] * 2,
         scratch_shapes=[pltpu.VMEM((N_SEQ, TOK_DEV, D), bf16), pltpu.VMEM((TOK_DEV, D), bf16)]
         + reduce_scratch((TOK_DEV, D), (HALF, D))
-        + sems(16)
-        + [pltpu.SemaphoreType.DMA],
+        + sems(40)
+        + [pltpu.SemaphoreType.DMA((2,))],
         compiler_params=remote_params(3),
     )(*operands)
 
 
 def turn_kernel(
     rank_ref, up_ref, hidden_ref, gate_ref, cot_rows_ref, w_ref,
-    middle_ref, cot_ref, my_gate_ref, router_ref, gain_ref,
-    grad_ref, branch_ref, logit_ref, gain_grad_ref, out_sum_ref,
-    back_s, out_s, other_back, from_core, part, other_out, out_core, mine, *rest
+    extra_up_ref, extra_hidden_ref, extra_w_ref, extra_grad_ref, middle_ref, cot_ref, my_gate_ref, router_ref, gain_ref,
+    grad_ref, branch_ref, logit_ref, gain_grad_ref, out_sum_ref, extra_sum_ref,
+    back_s, out_s, other_back, from_core, part, other_out, out_core, mine, line, *rest
 ):
-    bufs, (send_sem, recv_sem, copy_sem) = rest[:6], rest[6:]
+    bufs, (send_sem, recv_sem, copy_sem) = [rest[6 * i : 6 * i + 6] for i in range(5)], rest[30:]
     e = pl.program_id(0)
     me, core = lax.axis_index("seq"), lax.axis_index("core")
+    send, plan = sender(send_sem, recv_sem), planner(send_sem, recv_sem)
+    low, high = pl.ds(0, 512), pl.ds(512, 512)
+    low_x = Reduce(
+        plan, 17, "x", lambda i: extra_grad_ref.at[i, :, :, low], bufs[1], half_rows
+    )
+    high_y = Reduce(
+        plan, 23, "y", lambda i: extra_grad_ref.at[:, i, :, high], bufs[2], half_rows
+    )
+    low_y = Reduce(plan, 29, "y", lambda i: line.at[0, i], bufs[3], half_lanes)
+    high_x = Reduce(plan, 35, "x", lambda i: line.at[1, i], bufs[4], half_lanes)
 
     @pl.when(e == 0)
     def _():
-        greet(near("seq") + [sibling()])
-
-    @pl.when(e < LOCAL_E)
+        greet(near("seq") + near("x") + near("y") + [sibling()])
+        low_x.start()
+        high_y.start()
+
+    @pl.when(e == 2)
     def _():
+        low_x.relay()
+        high_y.relay()
+
+    def expert_rows(up_ref, hidden_ref, w_ref):
         expand, left, right = weights_of(w_ref)
         at = pl.ds(pl.multiple_of(e * SLOTS, SLOTS), SLOTS)
         back_s[at, :D] = dot(up_ref[0], expand, ((1,), (1,))).astype(bf16)
@@ -510,9 +601,16 @@
         back_s[at, D:] = jnp.where(lane == column, gate_grad, 0.0).astype(bf16)
         out_s[at, :] = (gate_ref[0] * expert_out).astype(bf16)
 
+    @pl.when(e < MAIN_E)
+    def _():
+        expert_rows(up_ref, hidden_ref, w_ref)
+
+    @pl.when(e == MAIN_E)
+    def _():
+        expert_rows(extra_up_ref, extra_hidden_ref, extra_w_ref)
+
     @pl.when(e == LOCAL_E)
     def _():
-        send = sender(send_sem, recv_sem)
         other = 1 - core
         right, left, far = ring(me)
         slot = lax.broadcasted_iota(jnp.int32, (GROUP, SLOTS), 1)
@@ -533,8 +631,12 @@
             send(other_back.at[block], from_core.at[block], 12 + i, "core", other)
             for i, block in enumerate(order)
         ]
+        line[0] = low_x.total().astype(bf16)
+        low_y.start()
+        line[1] = high_y.total().astype(bf16)
+        high_x.start()
         part[...] = dot(ours, back_s[...], ((1,), (0,))).astype(bf16).reshape(part.shape)
-        reduce = Reduce(send, 0, "seq", lambda i: part.at[i], bufs, half_rows)
+        reduce = Reduce(plan, 0, "seq", lambda i: part.at[i], bufs[0], half_rows)
         for i, block in enumerate(order):
             swaps[i].wait_recv()
             added(part.at[block], part.at[block], from_core.at[block])
@@ -547,6 +649,8 @@
         )
         out_swap = send(other_out, out_core, 16, "core", other)
         reduce.relay()
+        low_y.relay()
+        high_x.relay()
         out_sum_ref[...] = (
             dot(ours, out_s[...], ((1,), (0,))).astype(bf16).reshape(out_sum_ref.shape)
         )
@@ -561,15 +665,17 @@
         middle_grad = cot_ref[...].astype(f32) + back
         grad_ref[...] = middle_grad
         mine[...] = middle_grad.astype(bf16)
-        gather = Gather(send, 6, "seq", mine, lambda i: branch_ref.at[i], half_rows)
+        gather = Gather(plan, 6, "seq", mine, lambda i: branch_ref.at[i], half_rows).start()
         local = pltpu.make_async_copy(mine, branch_ref.at[me], copy_sem)
         local.start()
         out_swap.wait_recv()
         added(out_sum_ref, out_sum_ref, out_core)
         gather.relay()
+        extra_sum_ref[:, :512] = low_y.total().astype(bf16)
+        extra_sum_ref[:, 512:] = high_x.total().astype(bf16)
         gather.finish()
-        gather.drain()
-        reduce.drain()
+        for transfer in (gather, reduce, low_x, high_y, low_y, high_x):
+            transfer.drain()
         for copy in swaps + [out_swap]:
             copy.wait_send()
         local.wait()
@@ -578,10 +684,11 @@
 BACK_WIDTH = D + 128
 
 
-def turn(rank, up_grad, hidden, row_gates, cot_rows, weights, middle, cot, gates, router, gain):
-    last = LOCAL_E - 1
-    one = lambda e: (jnp.minimum(e, last), 0, 0)
-    wide = lambda e: (0, jnp.minimum(e, last), 0, 0)
+def turn(*operands):
+    one = lambda e: (jnp.minimum(e, MAIN_E - 1), 0, 0)
+    each = lambda e: (jnp.minimum(e, LOCAL_E - 1), 0, 0)
+    wide = lambda e: (0, jnp.minimum(e, MAIN_E - 1), 0, 0)
+    cubes = lambda e: (0, 0, 0, 0)
     whole = lambda e: (0, 0)
     blocks = lambda e: (0, 0, 0)
     row_block = pl.BlockSpec((TOK_DEV, D), whole)
@@ -596,9 +703,13 @@
             pl.BlockSpec((PAIR_TOK, LOCAL_E), whole),
             pl.BlockSpec((1, SLOTS, 2 * FF), one),
             pl.BlockSpec((1, SLOTS, FF), one),
-            pl.BlockSpec((1, SLOTS, 1), one),
-            pl.BlockSpec((1, SLOTS, D), one),
+            pl.BlockSpec((1, SLOTS, 1), each),
+            pl.BlockSpec((1, SLOTS, D), each),
             pl.BlockSpec((16, 1, 144, 1024), wide),
+            pl.BlockSpec((1, SLOTS, 2 * FF), blocks),
+            pl.BlockSpec((1, SLOTS, FF), blocks),
+            pl.BlockSpec((16, 1, 144, 1024), cubes, pipeline_mode=pl.Buffered(1)),
+            pl.BlockSpec((4, 4, 144, 1024), cubes, pipeline_mode=pl.Buffered(1)),
             row_block,
             row_block,
             lane_block,
@@ -611,6 +722,7 @@
             lane_block,
             gain_block,
             pl.BlockSpec((N_SEQ, TOK_DEV, D), blocks),
+            pl.BlockSpec((144, 1024), whole),
         ],
         out_shape=[
             jax.ShapeDtypeStruct((TOK_DEV, D), f32),
@@ -618,6 +730,7 @@
             jax.ShapeDtypeStruct((TOK_DEV, 128), bf16),
             jax.ShapeDtypeStruct((1, D), f32),
             jax.ShapeDtypeStruct((N_SEQ, TOK_DEV, D), bf16),
+            jax.ShapeDtypeStruct((144, 1024), bf16),
         ],
         scratch_shapes=[
             pltpu.VMEM((LOCAL_E * SLOTS, BACK_WIDTH), bf16),
@@ -628,9 +741,12 @@
             group_out,
             group_out,
             pltpu.VMEM((TOK_DEV, D), bf16),
+            pltpu.VMEM((2, 4, 144, 512), bf16),
         ]
         + reduce_scratch((TOK_DEV, BACK_WIDTH), (HALF, BACK_WIDTH))
-        + sems(17)
+        + reduce_scratch((4, 144, 512), (2, 144, 512)) * 2
+        + reduce_scratch((144, 512), (144, 256)) * 2
+        + sems(41)
         + [pltpu.SemaphoreType.DMA],
         compiler_params=remote_params(4),
         cost_estimate=pl.CostEstimate(
@@ -638,7 +754,7 @@
             bytes_accessed=40 << 20,
             transcendentals=0,
         ),
-    )(rank, up_grad, hidden, row_gates, cot_rows, weights, middle, cot, gates, router, gain)
+    )(*operands)
 
 
 PAD_ROWS = 16
@@ -654,7 +770,7 @@
     z, x, y, c = (lax.axis_index(a) for a in ("seq", "x", "y", "core"))
     right, left, far = ring(z)
     greet(near("seq") + [("seq", far)] + near("x") + near("y") + [sibling()])
-    send = sender(send_sem, recv_sem)
+    send, plan = sender(send_sem, recv_sem), planner(send_sem, recv_sem)
     pick = row_pick((512, QOWN), 0)
 
     def spread(grad):
@@ -671,28 +787,22 @@
             added(chip.at[side, first, second], full.at[side, plane, c], from_core.at[side, plane])
 
     def first_sum(side, axis):
-        reduce = Reduce(send, 6 * side, axis, lambda i: chip.at[side, i], bufs[side], half_rows)
-        reduce.start_far()
-        reduce.start_near()
-        return reduce
+        return Reduce(
+            plan, 6 * side, axis, lambda i: chip.at[side, i], bufs[side], half_rows
+        ).start()
 
     def second_sum(side, axis, reduce):
         line[side] = reduce.total().astype(bf16)
-        reduce = Reduce(
-            send, 18 + 6 * side, axis, lambda i: line.at[side, i], bufs[3 + side], half_lanes
-        )
-        reduce.start_far()
-        reduce.start_near()
-        return reduce
+        return Reduce(
+            plan, 18 + 6 * side, axis, lambda i: line.at[side, i], bufs[3 + side], half_lanes
+        ).start()
 
     for block in range(3):
         cols = slice(512 * block, 512 * (block + 1))
         grad = dot(attended_ref[...], branch_ref[:, cols], ((0,), (0,))).astype(bf16)
         full[0, :, :, :, cols] = spread(grad)
     swaps = [swap(0)]
-    outs = Reduce(send, 36, "seq", lambda i: out_sum_ref.at[i], bufs[6], half_rows)
-    outs.start_far()
-    outs.start_near()
+    outs = Reduce(plan, 36, "seq", lambda i: out_sum_ref.at[i], bufs[6], half_rows).start()
 
     def turn_back(kv):
         pair = Q_OWN + 2 * HD * kv
@@ -738,9 +848,7 @@
     part[...] = (
         dot(mixed_grad[...], entry_ref[...], ((1,), (1,))).astype(bf16).reshape(part.shape)
     )
-    rows = Reduce(send, 42, "seq", lambda i: part.at[i], bufs[7], half_rows)
-    rows.start_far()
-    rows.start_near()
+    rows = Reduce(plan, 42, "seq", lambda i: part.at[i], bufs[7], half_rows).start()
 
     def entry_rows(block):
         rows_of = slice(QOWN * block, QOWN * (block + 1))
@@ -759,7 +867,7 @@
     chip_sum(1, swaps[1])
     first_1 = first_sum(1, "x")
     back, gain_one = norm_back(in_ref[...].astype(f32), gain_ref[...], rows.total())
-    input_ref[...] = (grad_ref[...] + back).astype(bf16)
+    input_ref[...] = grad_ref[...] + back
     row_of = lax.broadcasted_iota(jnp.int32, (128, D), 0)
     gains = jnp.where(row_of == EXPERTS, gain_one, 0.0)
     gains = jnp.where(row_of == EXPERTS + 1, gain_two_ref[...], gains)
@@ -769,7 +877,7 @@
         full[2, :, :, :, 1024 + 128 * block : 1152 + 128 * block] = spread(shared_rows)
     swaps.append(swap(2))
     second_0.relay()
-    block_ref[...] = (middle_ref[...] + outs.total()).astype(bf16)
+    block_ref[...] = middle_ref[...] + outs.total()
     chip_sum(2, swaps[2])
     first_2 = first_sum(2, "y")
     first_1.relay()
@@ -810,8 +918,8 @@
     return pl.pallas_call(
         closing_kernel,
         out_shape=[
-            jax.ShapeDtypeStruct((TOK_DEV, D), bf16),
-            jax.ShapeDtypeStruct((TOK_DEV, D), bf16),
+            jax.ShapeDtypeStruct((TOK_DEV, D), f32),
+            jax.ShapeDtypeStruct((TOK_DEV, D), f32),
             jax.ShapeDtypeStruct((4, PAD_ROWS, WIDE), f32),
             jax.ShapeDtypeStruct((PAD_ROWS, D), f32),
         ],
@@ -837,20 +945,24 @@
     )(*operands)
 
 
-def owner_kernel(sum_ref, expand_ref, shrink_ref, send_sem, recv_sem, copy_sem):
+def owner_kernel(sum_ref, extra_ref, expand_ref, shrink_ref, send_sem, recv_sem, copy_sem):
     core = lax.axis_index("core")
     greet([sibling()])
     send = sender(send_sem, recv_sem)
-    experts = pl.ds(core * LOCAL_E, LOCAL_E)
+    most, last = pl.ds(core * LOCAL_E, MAIN_E), core * LOCAL_E + MAIN_E
 
     def pieces(owner):
-        main = pl.ds(pl.multiple_of(owner * 48, 16), 48)
+        rows = pl.ds(pl.multiple_of(owner * 48, 16), 48)
         left = pl.ds(pl.multiple_of(96 + owner * 16, 16), 16)
         ends = pl.ds(pl.multiple_of(owner * 512, 512), 512)
+        low, start, end = pl.ds(128, 16), pl.ds(0, 1024), pl.ds(1024, 512)
         return [
-            (sum_ref.at[:, main], expand_ref.at[experts]),
-            (sum_ref.at[:, left], shrink_ref.at[experts, :, pl.ds(0, 1024)]),
-            (sum_ref.at[:, pl.ds(128, 16), ends], shrink_ref.at[experts, :, pl.ds(1024, 512)]),
+            (sum_ref.at[:, rows], expand_ref.at[most]),
+            (sum_ref.at[:, left], shrink_ref.at[most, :, start]),
+            (sum_ref.at[:, low, ends], shrink_ref.at[most, :, end]),
+            (extra_ref.at[rows], expand_ref.at[last]),
+            (extra_ref.at[left], shrink_ref.at[last, :, start]),
+            (extra_ref.at[low, ends], shrink_ref.at[last, :, end]),
         ]
 
     copies = [
@@ -864,18 +976,18 @@
         copy.wait()
 
 
-def to_owners(summed):
+def to_owners(summed, extra):
     return pl.pallas_call(
         owner_kernel,
         out_shape=[
             jax.ShapeDtypeStruct((2 * LOCAL_E, 48, 1024), bf16),
             jax.ShapeDtypeStruct((2 * LOCAL_E, 16, D), bf16),
         ],
-        in_specs=[VMEM],
+        in_specs=[VMEM] * 2,
         out_specs=[VMEM] * 2,
-        scratch_shapes=sems(3) + [pltpu.SemaphoreType.DMA((3,))],
+        scratch_shapes=sems(6) + [pltpu.SemaphoreType.DMA((6,))],
         compiler_params=remote_params(6),
-    )(summed)
+    )(summed, extra)
 
 
 def dispatch_kernel(rank_ref, gate_ref, tokens_ref, cots_ref, rows_ref, cot_rows_ref, row_gate_ref):
@@ -946,16 +1058,18 @@
         part = dot(rows[:, 384 * j : 384 * (j + 1)], up_grad, ((0,), (0,))).astype(bf16)
         out_ref[4 * j : 4 * (j + 1), 0, :96, :] = part.reshape(4, 96, 1024)
 
-def expert_grads(rows, cot_rows, row_gates, weights):
+def expert_grads(rows, cot_rows, row_gates, weights, first):
+    count = weights.shape[1]
+    at = lambda e: (e + first, 0, 0)
     one = lambda e: (e, 0, 0)
     wide = lambda e: (0, e, 0, 0)
     return pl.pallas_call(
         grads_kernel,
-        grid=(LOCAL_E,),
+        grid=(count,),
         in_specs=[
-            pl.BlockSpec((1, SLOTS, D), one),
-            pl.BlockSpec((1, SLOTS, D), one),
-            pl.BlockSpec((1, SLOTS, 1), one),
+            pl.BlockSpec((1, SLOTS, D), at),
+            pl.BlockSpec((1, SLOTS, D), at),
+            pl.BlockSpec((1, SLOTS, 1), at),
             pl.BlockSpec((16, 1, 144, 1024), wide),
         ],
         out_specs=[
@@ -964,13 +1078,13 @@
             pl.BlockSpec((16, 1, 144, 1024), wide),
         ],
         out_shape=[
-            jax.ShapeDtypeStruct((LOCAL_E, SLOTS, FF), bf16),
-            jax.ShapeDtypeStruct((LOCAL_E, SLOTS, 2 * FF), bf16),
-            jax.ShapeDtypeStruct((16, LOCAL_E, 144, 1024), bf16),
+            jax.ShapeDtypeStruct((count, SLOTS, FF), bf16),
+            jax.ShapeDtypeStruct((count, SLOTS, 2 * FF), bf16),
+            jax.ShapeDtypeStruct((16, count, 144, 1024), bf16),
         ],
         compiler_params=pltpu.CompilerParams(vmem_limit_bytes=BIG),
         cost_estimate=pl.CostEstimate(
-            flops=12 * LOCAL_E * SLOTS * D * FF, bytes_accessed=60 << 20, transcendentals=0
+            flops=12 * count * SLOTS * D * FF, bytes_accessed=count * (12 << 20), transcendentals=0
         ),
     )(rows, cot_rows, row_gates, weights)
 
@@ -1035,7 +1149,7 @@
     core = lax.axis_index("core")
     first = (seq * 2 + core) * LOCAL_E
 
-    packed = pack_experts(expand_weight, shrink_weight)
+    packed, extra = pack_experts(expand_weight, shrink_weight)
     packed, rows_in, cots_in = lax.optimization_barrier((packed, activations[0], cotangent[0]))
     weights = lax.all_gather(packed, PLANE, axis=0, tiled=False)
 
@@ -1084,7 +1198,7 @@
     )
     angles = (cosine, sine, seq_ids[:, None], seq_ids[None, :])
 
-    normed, qkv, attended, lse, middle, tokens = middle_tokens(
+    normed, qkv, attended, lse, middle, tokens, extra_weights = middle_tokens(
         in_all,
         gains_full[0:1],
         entry_own,
@@ -1092,7 +1206,9 @@
         exit_own,
         activations[0],
         gains_full[1:2],
-    )
+        extra,
+    )
+    extra_weights = extra_weights.reshape(16, 1, 144, 1024)
     normed_two = lax.dynamic_slice(tokens, (core, seq, 0, 0), (1, 1, TOK_DEV, D))[0, 0]
     tokens = tokens.reshape(PAIR_TOK, D)
 
@@ -1102,17 +1218,24 @@
     gates = gate_expo / jnp.sum(gate_expo, axis=1, keepdims=True)
     own_gates = lax.dynamic_slice_in_dim(gates, first, LOCAL_E, 1)
     rows, cot_rows, row_gates = dispatch(rank.T, own_gates.T, tokens, cots.reshape(PAIR_TOK, D))
-    hidden, up_grad, expert_grad = expert_grads(rows, cot_rows, row_gates, weights)
+    extra_hidden, extra_up, extra_grad = expert_grads(
+        rows, cot_rows, row_gates, extra_weights, MAIN_E
+    )
+    hidden, up_grad, expert_grad = expert_grads(rows, cot_rows, row_gates, weights, 0)
     expert_sum = lax.psum_scatter(expert_grad, PLANE, scatter_dimension=0, tiled=False)
     my_gates = lax.dynamic_slice_in_dim(gates, core * GROUP + seq * TOK_DEV, TOK_DEV, 0)
     my_gates = jnp.pad(my_gates, ((0, 0), (0, 128 - EXPERTS)))
-    middle_grad, branch_grad, logit_grad, gain_two_grad, out_sum = turn(
+    middle_grad, branch_grad, logit_grad, gain_two_grad, out_sum, extra_sum = turn(
         rank,
         up_grad,
         hidden,
         row_gates,
         cot_rows,
         weights,
+        extra_up,
+        extra_hidden,
+        extra_weights,
+        extra_grad.reshape(4, 4, 144, 1024),
         middle,
         cotangent[0],
         my_gates,
@@ -1122,7 +1245,7 @@
     branch_grad = branch_grad.reshape(GROUP, D)
     router_grad = dot(normed_two, logit_grad, ((0,), (0,)))
 
-    input_grad, block_output, entry_got, exit_got = closing(
+    input_rows, block_rows, entry_got, exit_got = closing(
         qkv,
         lse,
         *angles,
@@ -1140,6 +1263,8 @@
         middle,
     )
 
+    input_grad, block_output = input_rows.astype(bf16), block_rows.astype(bf16)
+
     entry_got = entry_got[:, :ROWS]
     entry_sum = jnp.concatenate(
         [
@@ -1153,7 +1278,7 @@
     gains_sum = shared_sum[:, EXPERTS : EXPERTS + 2].T
     exit_sum = exit_got[:ROWS]
 
-    expand_sum, shrink_sum = to_owners(expert_sum)
+    expand_sum, shrink_sum = to_owners(expert_sum, extra_sum)
     expand_sum, shrink_sum = expand_sum.astype(f32), shrink_sum.astype(f32)
     entry_new = adamw_step(entry_weight, entry_sum, entry_mean, entry_square, 0.02, weight_decay)
     exit_new = adamw_step(exit_weight, exit_sum, exit_mean, exit_square, 0.15, weight_decay)

time: 385 us -> 391 us (1.016)
  Pallas kernels: 274 us -> 317 us
  waiting for transfers between devices: 48.3 us -> 15.5 us
    pallas_call x1, Pallas kernels: 55.9 us -> 87.5 us  [turn(): pl.pallas_call(turn_kernel, grid=(LOCAL_E + 1,), in_specs=[pl.BlockSpec((...]
    unnamed x3, waiting for transfers between devices: 22 us -> 0.03 us
    pallas_call x1, Pallas kernels: 48.4 us -> 60.1 us  [middle_tokens(): pl.pallas_call(middle_kernel, out_shape=[jax.ShapeDtypeStruct((GROUP, D),...]
    all_gather x1, waiting for transfers between devices: 26.3 us -> 15.5 us  [on_device(): weights = lax.all_gather(packed, PLANE, axis=0, tiled=False)]
    pallas_call x2 -> x3, Pallas kernels: 32.8 us -> 34.2 us  [the longest x2 27.8 us: expert_grads(): pl.pallas_call(grads_kernel, grid=(count,), in_specs=[pl.BlockSpec((1, SL...]
  transfers between devices with their start and end apart: 3 -> 3, of which waited for: 2 -> 1; matrix products, arithmetic and copies ran while one was open for 8% -> 8% of each run, Pallas kernels for 62% -> 74%
where the time goes in v5:
time: 391 us; the launch traced here: 386 us
  Pallas kernels  317 us (81%)
  other arithmetic  18.7 us (5%)
  waiting for transfers between devices  15.5 us (4%)
  between operations  14.9 us (4%)
  local copies, waits for them, and re-layouts  13.3 us (3%)
  matrix products  6.34 us (2%)
    pallas_call x1, Pallas kernels, turn(): pl.pallas_call(turn_kernel, grid=(LOCAL_E + 1,), in_specs=[pl.BlockSpec((...  87.5 us
    pallas_call x1, Pallas kernels, closing(): pl.pallas_call(closing_kernel, out_shape=[jax.ShapeDtypeStruct((TOK_DEV,...  66.6 us
    pallas_call x1, Pallas kernels, middle_tokens(): pl.pallas_call(middle_kernel, out_shape=[jax.ShapeDtypeStruct((GROUP, D),...  60.1 us
    pallas_call x1, Pallas kernels, start(): pl.pallas_call(start_kernel, out_shape=[jax.ShapeDtypeStruct((N_SEQ, TOK_...  49.3 us
    pallas_call x2, Pallas kernels, expert_grads(): pl.pallas_call(grads_kernel, grid=(count,), in_specs=[pl.BlockSpec((1, SL...  27.8 us
    all_gather x1, waiting for transfers between devices, on_device(): weights = lax.all_gather(packed, PLANE, axis=0, tiled=False)  15.5 us
    pallas_call x1, Pallas kernels, dispatch(): pl.pallas_call(dispatch_kernel, grid=(LOCAL_E,), in_specs=[pl.BlockSpec((...  13.2 us
    sub x6, other arithmetic, adamw_step(): weight - rate * (mean_hat / (jnp.sqrt(square_hat) + adam_eps) + decay * w...  11.9 us
  transfers between devices with their start and end apart: 3, of which 1 were waited for; matrix products, arithmetic and copies ran while one was open for 8% of the time, Pallas kernels for 74%

profile of v5, /device:TPU:1, one launch (start us, length us, event | category | flops | bytes accessed | tf_op | source)
XLA Modules:
  0.0 386.3 jit_solution(8210464031692230892)
XLA Ops:
  7.3 6.4 %shard_map.374 = (bf16[4,144,1024]{2,1,0:T(8,128)(2,1)}, bf16[144,1024]{1,0:T(8,128)(2,1)}) custom-call(f32[10,48,1024]{2,1,0:T(8,128)} %expand_ref.1, f32[10,16,1536]{2,1,0:T(8,128)} %shrink_ref.1), custom_call_target="tpu_custom_call" | custom-call | tf_op jit(solution)/shard_map/pallas_call | solution.py:299
  14.4 0.6 convert_element_type.46.hit_ref
  15.2 0.6 pad.18.exit_ref
  15.9 0.7 fusion.20.entry_ref
  16.5 49.3 %shard_map.375 = (bf16[4,128,1536]{2,1,0:T(8,128)(2,1)}, bf16[2,4,128,1536]{3,2,1,0:T(8,128)(2,1)}, bf16[4,128,128]{2,1,0:T(8,128)(2,1)}, bf16[1536,640]{1,0:T(8...) custom-call(bf16[128,1536]{1,0:T(8,128)(2,1)} %bitcast.84, bf16[128,1536]{1,0:T(8,128)(2,1)} %bitcast.99, ...), custom_call_target="tpu_custom_call" | custom-call | tf_op jit(solution)/shard_map/pallas_call | solution.py:408
  65.9 1.2 convolution_convert_fusion
  67.5 0.9 copy.160.seq_col_ref
  68.3 1.3 copy.153
  71.7 1.5 concatenate.22.sin_ref
  73.3 1.3 concatenate.21.cos_ref
  74.6 60.1 %shard_map.376 = (bf16[512,1536]{1,0:T(8,128)(2,1)}, bf16[512,640]{1,0:T(8,128)(2,1)}, bf16[512,384]{1,0:T(8,128)(2,1)}, f32[512,6]{1,0:T(8,128)}, f32[128,1536]...) custom-call(bf16[4,128,1536]{2,1,0:T(8,128)(2,1)} %get-tuple-element.62.all_ref, ...), custom_call_target="tpu_custom_call" | custom-call | tf_op jit(solution)/shard_map/pallas_call | solution.py:537
  135.1 1.4 reduce-window.11
  137.4 0.8 copy.164.rank_ref
  138.2 2.9 fusion.30
  142.1 0.8 copy.165.gate_ref
  142.9 13.2 %shard_map.377 = (bf16[5,256,1536]{2,1,0:T(8,128)(2,1)}, bf16[5,256,1536]{2,1,0:T(8,128)(2,1)}, f32[5,256,1]{2,1,0:T(8,128)}) custom-call(s32[5,1,1024]{2,1,0:T(1,128)} %copy.164.rank_ref, f32[5,1,1024]{2,1,0:T(1,128)} %copy.165.gate_ref, bf16[1024,1536]{1,0:T(8,128)(2,1)} %bitcast.110, bf16[1024,1536]{1,0:T(8,128)(2,1)} %bitcast.117), custom_call_target="tpu_custom_call" | custom-call | flops 8053063680 | bytes 16777216 | tf_op jit(solution)/shard_map/pallas_call | solution.py:1006
  156.1 15.5 %all-gather.3.cloned.1.call-done = bf16[64,144,1024]{2,1,0:T(8,128)(2,1)} async-done(((bf16[4,144,1024]{2,1,0:T(8,128)(2,1)}), bf16[64,144,1024]{2,1,0:T(8,128)(2,1)}) %all-gather.3.cloned.1.call-update) | async-done | bytes 18874384 | tf_op jit(solution)/shard_map/all_gather | solution.py:1154
  171.6 19.9 %shard_map.378 = (bf16[4,256,512]{2,1,0:T(8,128)(2,1)}, bf16[4,256,1024]{2,1,0:T(8,128)(2,1)}, bf16[16,4,144,1024]{3,2,1,0:T(8,128)(2,1)}) custom-call(bf16[5,256,1536]{2,1,0:T(8,128)(2,1)} %get-tuple-element.72.rows_ref, bf16[5,256,1536]{2,1,0:T(8,128)(2,1)} %get-tuple-element.73.cot_ref.cot_rows_ref, f32[5,256,1]{2,1,0:T(8,128)} %get-tuple-element.74.gate_ref, ...), custom_call_target="tpu_custom_call" | custom-call | flops 9663676416 | bytes 50331648 | tf_op jit(solution)/shard_map/pallas_call | solution.py:1066
  191.5 0.6 pad.19.my_gate_ref
  192.2 7.9 %shard_map.379 = (bf16[1,256,512]{2,1,0:T(8,128)(2,1)}, bf16[1,256,1024]{2,1,0:T(8,128)(2,1)}, bf16[16,1,144,1024]{3,2,1,0:T(8,128)(2,1)}) custom-call(bf16[5,256,1536]{2,1,0:T(8,128)(2,1)} %get-tuple-element.72.rows_ref, bf16[5,256,1536]{2,1,0:T(8,128)(2,1)} %get-tuple-element.73.cot_ref.cot_rows_ref, f32[5,256,1]{2,1,0:T(8,128)} %get-tuple-element.74.gate_ref, ...), custom_call_target="tpu_custom_call" | custom-call | flops 2415919104 | bytes 12582912 | tf_op jit(solution)/shard_map/pallas_call | solution.py:1066
  200.1 87.5 %shard_map.380 = (f32[128,1536]{1,0:T(8,128)}, bf16[4,128,1536]{2,1,0:T(8,128)(2,1)}, bf16[128,128]{1,0:T(8,128)(2,1)}, f32[1,1536]{1,0:T(1,128)}, bf16[4,128,15...) custom-call(s32[1024,5]{1,0:T(8,128)} %copy-done.2, bf16[4,256,1024]{2,1,0:T(8,128)(2,1)} %get-tuple-element.76.up_ref, ...), custom_call_target="tpu_custom_call" | custom-call | flops 14092861440 | bytes 41943040 | tf_op jit(solution)/shard_map/pallas_call | solution.py:699
  287.6 2.2 fusion.8.router_grad_ref
  289.8 66.6 %shard_map.381 = (f32[128,1536]{1,0:T(8,128)}, f32[128,1536]{1,0:T(8,128)}, f32[4,16,768]{2,1,0:T(8,128)}, f32[16,1536]{1,0:T(8,128)}) custom-call(bf16[512,640]{1,0:T(8,128)(2,1)} %get-tuple-element.67.qkv_ref, f32[512,6]{1,0:T(8,128)} %get-tuple-element.68.lse_ref, f32[512,640]{1,0:T(8,128)} %concatenate.21.cos_ref, f32[512,640]{1,0:T(8,128)} %concatenate.22.sin_ref, ...), custom_call_target="tpu_custom_call" | custom-call | tf_op jit(solution)/shard_map/pallas_call | solution.py:918
  356.4 0.8 slice_reduce_fusion
  357.4 1.0 slice_bitcast_fusion
  358.4 0.8 slice_bitcast_fusion.1
  360.7 1.6 multiply_subtract_fusion.3
  362.4 1.0 convert_bitcast_fusion
  363.3 0.8 multiply_subtract_fusion.2
  364.2 6.4 %shard_map.382 = (bf16[10,48,1024]{2,1,0:T(8,128)(2,1)}, bf16[10,16,1536]{2,1,0:T(8,128)(2,1)}) custom-call(bf16[4,144,1024]{2,1,0:T(8,128)(2,1)} %bitcast.96, bf16[144,1024]{1,0:T(8,128)(2,1)} %get-tuple-element.95.extra_ref), custom_call_target="tpu_custom_call" | custom-call | tf_op jit(solution)/shard_map/pallas_call | solution.py:980
  370.7 3.3 multiply_subtract_fusion.1
  374.3 4.9 %multiply_subtract_fusion = (f32[10,48,1024]{2,1,0:T(8,128)}, f32[10,48,1024]{2,1,0:T(8,128)}, f32[10,48,1024]{2,1,0:T(8,128)}) fusion(f32[10,48,1024]{2,1,0:T(8,128)S(1)} %copy-done, bf16[10,48,1024]{2,1,0:T(8,128)(2,1)} %get-tuple-element.96, f32[10,48,1024]{2,1,0:T(8,128)S(1)} %copy-done.3, f32[10,48,1024]{2,1,0:T(8,128)S(1)} %copy-done.4), kind=kLoop, calls=%fused_computation.4 | loop fusion | flops 7864320 | bytes 12779520 | tf_op jit(solution)/shard_map/sub | solution.py:1112
  (119 shorter events, 7.4 us)
Async XLA Ops:
  7.2 6.6 %copy-start.9 = (f32[12,2560]{1,0:T(8,128)S(1)}, f32[12,2560]{1,0:T(8,128)}, u32[]{:S(2)}) copy-start(f32[12,2560]{1,0:T(8,128)} %param.28) | copy-start | bytes 368644
  7.2 6.7 %copy-start.21 = (f32[2,12]{1,0:T(2,128)S(1)}, f32[2,12]{1,0:T(2,128)}, u32[]{:S(2)}) copy-start(f32[2,12]{1,0:T(2,128)} %param.43) | copy-start | bytes 292
  7.2 6.8 %copy-start.17 = (f32[12,40]{1,0:T(8,128)S(1)}, f32[12,40]{1,0:T(8,128)}, u32[]{:S(2)}) copy-start(f32[12,40]{1,0:T(8,128)} %param.34) | copy-start | bytes 5764
  7.2 6.8 %copy-start.11 = (f32[12,1536]{1,0:T(8,128)S(1)}, f32[12,1536]{1,0:T(8,128)}, u32[]{:S(2)}) copy-start(f32[12,1536]{1,0:T(8,128)} %param.31) | copy-start | bytes 221188
  7.2 6.8 %copy-start.20 = (s32[1,128,8]{1,2,0:T(8,128)S(1)}, s32[1,128,8]{1,2,0:T(8,128)}, u32[]{:S(2)}) copy-start(s32[1,128,8]{1,2,0:T(8,128)} %param.27) | copy-start | bytes 12292
  7.2 164.3 %all-gather.3.cloned.1.call-start = ((), (), s32[]{:S(2)}) async-start(), calls=%async_computation.1 | async-start | bytes 20054016 | tf_op jit(solution)/shard_map/all_gather | solution.py:1154
  13.7 52.2 %copy-start.24 = (s32[1,512]{1,0:T(1,128)S(1)}, s32[1,512]{1,0:T(1,128)}, u32[]{:S(2)}) copy-start(s32[1,512]{1,0:T(1,128)} %param.26) | copy-start | bytes 6148
  13.7 53.5 %copy-start.25 = (s32[1,3]{1,0:T(1,128)S(1)}, s32[1,3]{1,0:T(1,128)}, u32[]{:S(2)}) copy-start(s32[1,3]{1,0:T(1,128)} %param.25) | copy-start | bytes 40
  13.8 350.4 %reduce-scatter.4.cloned.1.call-start = ((), (), s32[]{:S(2)}) async-start(), calls=%async_computation.2 | async-start | bytes 20054016
  67.1 67.6 %collective-permute-start = (bf16[512,128]{1,0:T(8,128)(2,1)S(1)}, bf16[512,128]{1,0:T(8,128)(2,1)S(1)}, u32[]{:S(2)}, u32[]{:S(2)}) collective-permute-start(bf16[512,128]{1,0:T(8,128)(2,1)S(1)} %convolution_convert_fusion), channel_id=1, source_target_pairs={{0,1},{1,0},{2,3},{3,2},{4,5},{5,4},{6,7},{7,6},{8,9},{9,8},{10,11... | collective-permute-start | bytes 393224 | tf_op jit(solution)/shard_map/ppermute | solution.py:1093
  67.5 3.9 %copy-start.16 = (s32[512]{0:T(512)}, s32[512]{0:T(512)S(1)}, u32[]{:S(2)}) copy-start(s32[512]{0:T(512)S(1)} %convert_reduce_fusion) | copy-start | bytes 6148
  134.7 3.5 copy-start.10
  137.4 3.8 copy-start.2
  289.8 69.7 %copy-start.22 = (f32[2,12]{1,0:T(2,128)S(1)}, f32[2,12]{1,0:T(2,128)}, u32[]{:S(2)}) copy-start(f32[2,12]{1,0:T(2,128)} %param.45) | copy-start | bytes 292
  289.8 69.7 %copy-start.23 = (f32[2,12]{1,0:T(2,128)S(1)}, f32[2,12]{1,0:T(2,128)}, u32[]{:S(2)}) copy-start(f32[2,12]{1,0:T(2,128)} %param.44) | copy-start | bytes 292
  289.8 70.3 %copy-start.18 = (f32[12,40]{1,0:T(8,128)S(1)}, f32[12,40]{1,0:T(8,128)}, u32[]{:S(2)}) copy-start(f32[12,40]{1,0:T(8,128)} %param.36) | copy-start | bytes 5764
  289.8 70.3 %copy-start.19 = (f32[12,40]{1,0:T(8,128)S(1)}, f32[12,40]{1,0:T(8,128)}, u32[]{:S(2)}) copy-start(f32[12,40]{1,0:T(8,128)} %param.35) | copy-start | bytes 5764
  289.8 70.9 %copy-start.14 = (f32[12,1536]{1,0:T(8,128)S(1)}, f32[12,1536]{1,0:T(8,128)}, u32[]{:S(2)}) copy-start(f32[12,1536]{1,0:T(8,128)} %param.33) | copy-start | bytes 221188
  289.8 70.9 %copy-start.15 = (f32[12,1536]{1,0:T(8,128)S(1)}, f32[12,1536]{1,0:T(8,128)}, u32[]{:S(2)}) copy-start(f32[12,1536]{1,0:T(8,128)} %param.32) | copy-start | bytes 221188
  357.4 5.0 %copy-start.7 = (f32[128,1536]{1,0:T(8,128)S(1)}, f32[128,1536]{1,0:T(8,128)}, u32[]{:S(2)}) copy-start(f32[128,1536]{1,0:T(8,128)} %get-tuple-element.91) | copy-start | bytes 2359300
  357.4 5.0 %copy-start.8 = (f32[128,1536]{1,0:T(8,128)S(1)}, f32[128,1536]{1,0:T(8,128)}, u32[]{:S(2)}) copy-start(f32[128,1536]{1,0:T(8,128)} %get-tuple-element.90) | copy-start | bytes 2359300
  359.3 4.0 %copy-start.12 = (f32[12,2560]{1,0:T(8,128)S(1)}, f32[12,2560]{1,0:T(8,128)}, u32[]{:S(2)}) copy-start(f32[12,2560]{1,0:T(8,128)} %param.30) | copy-start | bytes 368644
  359.3 4.0 %copy-start.13 = (f32[12,2560]{1,0:T(8,128)S(1)}, f32[12,2560]{1,0:T(8,128)}, u32[]{:S(2)}) copy-start(f32[12,2560]{1,0:T(8,128)} %param.29) | copy-start | bytes 368644
  362.3 8.3 %copy-start.1 = (f32[10,16,1536]{2,1,0:T(8,128)S(1)}, f32[10,16,1536]{2,1,0:T(8,128)}, u32[]{:S(2)}) copy-start(f32[10,16,1536]{2,1,0:T(8,128)} %shrink_ref.1) | copy-start | bytes 2949124
  362.3 8.3 %copy-start.5 = (f32[10,16,1536]{2,1,0:T(8,128)S(1)}, f32[10,16,1536]{2,1,0:T(8,128)}, u32[]{:S(2)}) copy-start(f32[10,16,1536]{2,1,0:T(8,128)} %param.42) | copy-start | bytes 2949124
  362.3 8.3 %copy-start.6 = (f32[10,16,1536]{2,1,0:T(8,128)S(1)}, f32[10,16,1536]{2,1,0:T(8,128)}, u32[]{:S(2)}) copy-start(f32[10,16,1536]{2,1,0:T(8,128)} %param.41) | copy-start | bytes 2949124
  370.6 3.3 copy-start
  370.6 3.3 copy-start.3
  370.6 3.7 copy-start.4
Sparse Core Ops, SparseCore 0:
  13.9 157.6 all-gather.2
  191.6 151.8 reduce-scatter.3

commit v6 on v5

--- a/solution.py
+++ b/solution.py
@@ -263,7 +263,7 @@
 MAIN_E = LOCAL_E - 1
 
 
-def pack_kernel(expand_ref, shrink_ref, main_ref, extra_ref, stage, stage_end, send_sem, recv_sem):
+def pack_kernel(expand_ref, shrink_ref, out_ref, stage, stage_end, send_sem, recv_sem):
     core = lax.axis_index("core")
     greet([sibling()])
     send = sender(send_sem, recv_sem)
@@ -273,24 +273,19 @@
         stage[e, :48] = expand_ref[theirs].astype(bf16)
         stage[e, 48:] = shrink_ref[theirs, :, :1024].astype(bf16)
         stage_end[e] = shrink_ref[theirs, :, 1024:].astype(bf16)
-    rows = pl.ds(pl.multiple_of(core * 48, 16), 48)
+    main = pl.ds(pl.multiple_of(core * 48, 16), 48)
     left = pl.ds(pl.multiple_of(96 + core * 16, 16), 16)
     ends = pl.ds(pl.multiple_of(core * 512, 512), 512)
-    low, most = pl.ds(128, 16), pl.ds(0, MAIN_E)
     copies = [
-        send(stage.at[most, pl.ds(0, 48)], main_ref.at[:, rows], 0, "core", other),
-        send(stage.at[most, pl.ds(48, 16)], main_ref.at[:, left], 1, "core", other),
-        send(stage_end.at[most], main_ref.at[:, low, ends], 2, "core", other),
-        send(stage.at[MAIN_E, pl.ds(0, 48)], extra_ref.at[rows], 3, "core", other),
-        send(stage.at[MAIN_E, pl.ds(48, 16)], extra_ref.at[left], 4, "core", other),
-        send(stage_end.at[MAIN_E], extra_ref.at[low, ends], 5, "core", other),
+        send(stage.at[:, pl.ds(0, 48)], out_ref.at[:, main], 0, "core", other),
+        send(stage.at[:, pl.ds(48, 16)], out_ref.at[:, left], 1, "core", other),
+        send(stage_end, out_ref.at[:, pl.ds(128, 16), ends], 2, "core", other),
     ]
     for e in range(LOCAL_E):
         mine = core * LOCAL_E + e
-        out = main_ref.at[e] if e < MAIN_E else extra_ref
-        out[rows, :] = expand_ref[mine].astype(bf16)
-        out[left, :] = shrink_ref[mine, :, :1024].astype(bf16)
-        out[low, ends] = shrink_ref[mine, :, 1024:].astype(bf16)
+        out_ref[e, main, :] = expand_ref[mine].astype(bf16)
+        out_ref[e, left, :] = shrink_ref[mine, :, :1024].astype(bf16)
+        out_ref[e, pl.ds(128, 16), ends] = shrink_ref[mine, :, 1024:].astype(bf16)
     for copy in copies:
         copy.wait()
 
@@ -298,17 +293,14 @@
 def pack_experts(expand, shrink):
     return pl.pallas_call(
         pack_kernel,
-        out_shape=[
-            jax.ShapeDtypeStruct((MAIN_E, 144, 1024), bf16),
-            jax.ShapeDtypeStruct((144, 1024), bf16),
-        ],
+        out_shape=jax.ShapeDtypeStruct((LOCAL_E, 144, 1024), bf16),
         in_specs=[VMEM] * 2,
-        out_specs=[VMEM] * 2,
+        out_specs=VMEM,
         scratch_shapes=[
             pltpu.VMEM((LOCAL_E, 64, 1024), bf16),
             pltpu.VMEM((LOCAL_E, 16, 512), bf16),
         ]
-        + sems(6),
+        + sems(3),
         compiler_params=remote_params(1),
     )(expand, shrink)
 
@@ -451,52 +443,21 @@
 
 def middle_kernel(
     all_ref, gain_one_ref, entry_ref, cos_ref, sin_ref, seq_col_ref, seq_row_ref, exit_ref,
-    in_ref, gain_ref, extra_ref,
-    normed_ref, qkv_ref, attended_ref, lse_ref, middle_ref, tokens_ref, extra_all,
+    in_ref, gain_ref,
+    normed_ref, qkv_ref, attended_ref, lse_ref, middle_ref, tokens_ref,
     part, mine, *rest
 ):
     bufs, (send_sem, recv_sem, copy_sem) = rest[:6], rest[6:]
     me, core = lax.axis_index("seq"), lax.axis_index("core")
-    x, y = lax.axis_index("x"), lax.axis_index("y")
-    greet(near("seq") + near("x") + near("y") + [sibling()])
+    greet(near("seq") + [sibling()])
     send, plan = sender(send_sem, recv_sem), planner(send_sem, recv_sem)
-    low, high = pl.ds(0, 512), pl.ds(512, 512)
-    own = pltpu.make_async_copy(extra_ref, extra_all.at[x, y], copy_sem.at[1])
-    own.start()
-    low_x = Gather(
-        plan, 16, "x", extra_ref.at[:, low], lambda i: extra_all.at[i, y, :, low], half_lanes
-    ).start()
-    high_y = Gather(
-        plan, 22, "y", extra_ref.at[:, high], lambda i: extra_all.at[x, i, :, high], half_lanes
-    ).start()
     for block in range(N_SEQ):
         rows = slice(TOK_DEV * block, TOK_DEV * (block + 1))
         vector = all_ref[block].astype(f32)
         normed_ref[rows, :] = (vector * unit_scale(vector) * gain_one_ref[...]).astype(bf16)
-    low_x.relay()
-    high_y.relay()
     mixed = dot(normed_ref[...], entry_ref[...], ((1,), (0,)))
     mixed = mixed * cos_ref[...] + swap_halves(mixed, -1.0, 1.0) * sin_ref[...]
     qkv_ref[...] = mixed.astype(bf16)
-    own.wait()
-    low_x.finish()
-    low_y = Gather(
-        plan,
-        28,
-        "y",
-        extra_all.at[:, y, :, low],
-        lambda i: extra_all.at[:, i, :, low],
-        half_rows,
-    ).start()
-    high_y.finish()
-    high_x = Gather(
-        plan,
-        34,
-        "x",
-        extra_all.at[x, :, :, high],
-        lambda i: extra_all.at[i, :, :, high],
-        half_rows,
-    ).start()
     for block in range(GROUP // BLOCK):
         bias = block_bias(seq_col_ref, seq_row_ref, block)
         keys = BLOCK * (block + 1)
@@ -514,21 +475,17 @@
             lse_ref[rows, head : head + 1] = peak + jnp.log(total)
     part[...] = dot(attended_ref[...], exit_ref[...], ((1,), (0,))).astype(bf16).reshape(part.shape)
     reduce = Reduce(plan, 0, "seq", lambda i: part.at[i], bufs, half_rows).start()
-    low_y.relay()
-    high_x.relay()
     reduce.relay()
     middle = in_ref[...].astype(f32) + reduce.total()
     middle_ref[...] = middle
     mine[...] = (middle * unit_scale(middle) * gain_ref[...]).astype(bf16)
     gather = Gather(plan, 6, "seq", mine, lambda i: tokens_ref.at[core, i], half_rows).start()
-    local = pltpu.make_async_copy(mine, tokens_ref.at[core, me], copy_sem.at[0])
+    local = pltpu.make_async_copy(mine, tokens_ref.at[core, me], copy_sem)
     local.start()
     pairs = hand_over(send, 12, mine, tokens_ref, gather)
     for copy in pairs:
         copy.wait()
-    low_y.finish()
-    high_x.finish()
-    for transfer in (gather, reduce, low_x, high_y, low_y, high_x):
+    for transfer in (gather, reduce):
         transfer.drain()
     local.wait()
 
@@ -543,50 +500,43 @@
             jax.ShapeDtypeStruct((GROUP, HEADS_OWN), f32),
             jax.ShapeDtypeStruct((TOK_DEV, D), f32),
             jax.ShapeDtypeStruct((2, N_SEQ, TOK_DEV, D), bf16),
-            jax.ShapeDtypeStruct((4, 4, 144, 1024), bf16),
-        ],
-        in_specs=[VMEM] * 10 + [ANY],
-        out_specs=[VMEM] * 5 + [ANY] * 2,
+        ],
+        in_specs=[VMEM] * 10,
+        out_specs=[VMEM] * 5 + [ANY],
         scratch_shapes=[pltpu.VMEM((N_SEQ, TOK_DEV, D), bf16), pltpu.VMEM((TOK_DEV, D), bf16)]
         + reduce_scratch((TOK_DEV, D), (HALF, D))
-        + sems(40)
-        + [pltpu.SemaphoreType.DMA((2,))],
+        + sems(16)
+        + [pltpu.SemaphoreType.DMA],
         compiler_params=remote_params(3),
     )(*operands)
 
 
 def turn_kernel(
     rank_ref, up_ref, hidden_ref, gate_ref, cot_rows_ref, w_ref,
-    extra_up_ref, extra_hidden_ref, extra_w_ref, extra_grad_ref, middle_ref, cot_ref, my_gate_ref, router_ref, gain_ref,
+    line, middle_ref, cot_ref, my_gate_ref, router_ref, gain_ref,
     grad_ref, branch_ref, logit_ref, gain_grad_ref, out_sum_ref, extra_sum_ref,
-    back_s, out_s, other_back, from_core, part, other_out, out_core, mine, line, *rest
+    back_s, out_s, other_back, from_core, part, other_out, out_core, mine, *rest
 ):
-    bufs, (send_sem, recv_sem, copy_sem) = [rest[6 * i : 6 * i + 6] for i in range(5)], rest[30:]
+    bufs, (send_sem, recv_sem, copy_sem) = [rest[6 * i : 6 * i + 6] for i in range(3)], rest[18:]
     e = pl.program_id(0)
     me, core = lax.axis_index("seq"), lax.axis_index("core")
     send, plan = sender(send_sem, recv_sem), planner(send_sem, recv_sem)
-    low, high = pl.ds(0, 512), pl.ds(512, 512)
-    low_x = Reduce(
-        plan, 17, "x", lambda i: extra_grad_ref.at[i, :, :, low], bufs[1], half_rows
-    )
-    high_y = Reduce(
-        plan, 23, "y", lambda i: extra_grad_ref.at[:, i, :, high], bufs[2], half_rows
-    )
-    low_y = Reduce(plan, 29, "y", lambda i: line.at[0, i], bufs[3], half_lanes)
-    high_x = Reduce(plan, 35, "x", lambda i: line.at[1, i], bufs[4], half_lanes)
+    low_y = Reduce(plan, 17, "y", lambda i: line.at[0, i], bufs[1], half_lanes)
+    high_x = Reduce(plan, 23, "x", lambda i: line.at[1, i], bufs[2], half_lanes)
 
     @pl.when(e == 0)
     def _():
         greet(near("seq") + near("x") + near("y") + [sibling()])
-        low_x.start()
-        high_y.start()
+        low_y.start()
+        high_x.start()
 
     @pl.when(e == 2)
     def _():
-        low_x.relay()
-        high_y.relay()
-
-    def expert_rows(up_ref, hidden_ref, w_ref):
+        low_y.relay()
+        high_x.relay()
+
+    @pl.when(e < LOCAL_E)
+    def _():
         expand, left, right = weights_of(w_ref)
         at = pl.ds(pl.multiple_of(e * SLOTS, SLOTS), SLOTS)
         back_s[at, :D] = dot(up_ref[0], expand, ((1,), (1,))).astype(bf16)
@@ -601,14 +551,6 @@
         back_s[at, D:] = jnp.where(lane == column, gate_grad, 0.0).astype(bf16)
         out_s[at, :] = (gate_ref[0] * expert_out).astype(bf16)
 
-    @pl.when(e < MAIN_E)
-    def _():
-        expert_rows(up_ref, hidden_ref, w_ref)
-
-    @pl.when(e == MAIN_E)
-    def _():
-        expert_rows(extra_up_ref, extra_hidden_ref, extra_w_ref)
-
     @pl.when(e == LOCAL_E)
     def _():
         other = 1 - core
@@ -631,10 +573,6 @@
             send(other_back.at[block], from_core.at[block], 12 + i, "core", other)
             for i, block in enumerate(order)
         ]
-        line[0] = low_x.total().astype(bf16)
-        low_y.start()
-        line[1] = high_y.total().astype(bf16)
-        high_x.start()
         part[...] = dot(ours, back_s[...], ((1,), (0,))).astype(bf16).reshape(part.shape)
         reduce = Reduce(plan, 0, "seq", lambda i: part.at[i], bufs[0], half_rows)
         for i, block in enumerate(order):
@@ -649,8 +587,6 @@
         )
         out_swap = send(other_out, out_core, 16, "core", other)
         reduce.relay()
-        low_y.relay()
-        high_x.relay()
         out_sum_ref[...] = (
             dot(ours, out_s[...], ((1,), (0,))).astype(bf16).reshape(out_sum_ref.shape)
         )
@@ -674,7 +610,7 @@
         extra_sum_ref[:, :512] = low_y.total().astype(bf16)
         extra_sum_ref[:, 512:] = high_x.total().astype(bf16)
         gather.finish()
-        for transfer in (gather, reduce, low_x, high_y, low_y, high_x):
+        for transfer in (gather, reduce, low_y, high_x):
             transfer.drain()
         for copy in swaps + [out_swap]:
             copy.wait_send()
@@ -685,9 +621,8 @@
 
 
 def turn(*operands):
-    one = lambda e: (jnp.minimum(e, MAIN_E - 1), 0, 0)
-    each = lambda e: (jnp.minimum(e, LOCAL_E - 1), 0, 0)
-    wide = lambda e: (0, jnp.minimum(e, MAIN_E - 1), 0, 0)
+    one = lambda e: (jnp.minimum(e, LOCAL_E - 1), 0, 0)
+    wide = lambda e: (0, jnp.minimum(e, LOCAL_E - 1), 0, 0)
     cubes = lambda e: (0, 0, 0, 0)
     whole = lambda e: (0, 0)
     blocks = lambda e: (0, 0, 0)
@@ -703,13 +638,10 @@
             pl.BlockSpec((PAIR_TOK, LOCAL_E), whole),
             pl.BlockSpec((1, SLOTS, 2 * FF), one),
             pl.BlockSpec((1, SLOTS, FF), one),
-            pl.BlockSpec((1, SLOTS, 1), each),
-            pl.BlockSpec((1, SLOTS, D), each),
+            pl.BlockSpec((1, SLOTS, 1), one),
+            pl.BlockSpec((1, SLOTS, D), one),
             pl.BlockSpec((16, 1, 144, 1024), wide),
-            pl.BlockSpec((1, SLOTS, 2 * FF), blocks),
-            pl.BlockSpec((1, SLOTS, FF), blocks),
-            pl.BlockSpec((16, 1, 144, 1024), cubes, pipeline_mode=pl.Buffered(1)),
-            pl.BlockSpec((4, 4, 144, 1024), cubes, pipeline_mode=pl.Buffered(1)),
+            pl.BlockSpec((2, 4, 144, 512), cubes),
             row_block,
             row_block,
             lane_block,
@@ -741,12 +673,10 @@
             group_out,
             group_out,
             pltpu.VMEM((TOK_DEV, D), bf16),
-            pltpu.VMEM((2, 4, 144, 512), bf16),
         ]
         + reduce_scratch((TOK_DEV, BACK_WIDTH), (HALF, BACK_WIDTH))
-        + reduce_scratch((4, 144, 512), (2, 144, 512)) * 2
         + reduce_scratch((144, 512), (144, 256)) * 2
-        + sems(41)
+        + sems(29)
         + [pltpu.SemaphoreType.DMA],
         compiler_params=remote_params(4),
         cost_estimate=pl.CostEstimate(
@@ -949,7 +879,7 @@
     core = lax.axis_index("core")
     greet([sibling()])
     send = sender(send_sem, recv_sem)
-    most, last = pl.ds(core * LOCAL_E, MAIN_E), core * LOCAL_E + MAIN_E
+    most, single = pl.ds(core * LOCAL_E + 1, MAIN_E), core * LOCAL_E
 
     def pieces(owner):
         rows = pl.ds(pl.multiple_of(owner * 48, 16), 48)
@@ -960,9 +890,9 @@
             (sum_ref.at[:, rows], expand_ref.at[most]),
             (sum_ref.at[:, left], shrink_ref.at[most, :, start]),
             (sum_ref.at[:, low, ends], shrink_ref.at[most, :, end]),
-            (extra_ref.at[rows], expand_ref.at[last]),
-            (extra_ref.at[left], shrink_ref.at[last, :, start]),
-            (extra_ref.at[low, ends], shrink_ref.at[last, :, end]),
+            (extra_ref.at[rows], expand_ref.at[single]),
+            (extra_ref.at[left], shrink_ref.at[single, :, start]),
+            (extra_ref.at[low, ends], shrink_ref.at[single, :, end]),
         ]
 
     copies = [
@@ -1034,7 +964,20 @@
     right = jnp.concatenate([w_ref[:, 0, 128:144, :512], w_ref[:, 0, 128:144, 512:]], axis=1)
     return expand, left, right.reshape(FF, 512)
 
-def grads_kernel(rows_ref, cot_ref, gate_ref, w_ref, hidden_ref, up_ref, out_ref):
+def grads_kernel(
+    rows_ref, cot_ref, gate_ref, w_ref, hidden_ref, up_ref, out_ref, line_ref, own, *rest
+):
+    bufs, (send_sem, recv_sem) = [rest[6 * i : 6 * i + 6] for i in range(2)], rest[12:]
+    e = pl.program_id(0)
+    plan = planner(send_sem, recv_sem)
+    low, high = pl.ds(0, 512), pl.ds(512, 512)
+    low_x = Reduce(plan, 0, "x", lambda i: own.at[i, :, :, low], bufs[0], half_rows)
+    high_y = Reduce(plan, 6, "y", lambda i: own.at[:, i, :, high], bufs[1], half_rows)
+
+    @pl.when(e == 0)
+    def _():
+        greet(near("x") + near("y"))
+
     expand, left, right = weights_of(w_ref)
     grad_rows = (gate_ref[0] * cot_ref[0].astype(f32)).astype(bf16)
     rows = rows_ref[0]
@@ -1043,48 +986,98 @@
     sig = jax.nn.sigmoid(gate_pre)
     hidden = (gate_pre * sig * up_part).astype(bf16)
     hidden_ref[0] = hidden
+
+    @pl.when(e == 2)
+    def _():
+        low_x.relay()
+        high_y.relay()
+
     hidden_grad = dot(grad_rows[:, :1024], left, ((1,), (1,))) + dot(
         grad_rows[:, 1024:], right, ((1,), (1,))
     )
     up_ref[0, :, :FF] = (hidden_grad * up_part * sig * (1.0 + gate_pre * (1.0 - sig))).astype(bf16)
     up_ref[0, :, FF:] = (hidden_grad * gate_pre * sig).astype(bf16)
-    grad_left = dot(hidden, grad_rows[:, :1024], ((0,), (0,))).astype(bf16)
-    out_ref[:, 0, 96:128, :] = grad_left.reshape(16, 32, 1024)
-    grad_right = dot(hidden, grad_rows[:, 1024:], ((0,), (0,))).astype(bf16).reshape(16, 32, 512)
-    out_ref[:, 0, 128:144, :512] = grad_right[:, :16]
-    out_ref[:, 0, 128:144, 512:] = grad_right[:, 16:]
-    up_grad = up_ref[0]
-    for j in range(4):
-        part = dot(rows[:, 384 * j : 384 * (j + 1)], up_grad, ((0,), (0,))).astype(bf16)
-        out_ref[4 * j : 4 * (j + 1), 0, :96, :] = part.reshape(4, 96, 1024)
-
-def expert_grads(rows, cot_rows, row_gates, weights, first):
-    count = weights.shape[1]
-    at = lambda e: (e + first, 0, 0)
+
+    def write(shrink_at, end_at, expand_at):
+        grad_left = dot(hidden, grad_rows[:, :1024], ((0,), (0,))).astype(bf16)
+        grad_right = dot(hidden, grad_rows[:, 1024:], ((0,), (0,))).astype(bf16)
+        grad_right = grad_right.reshape(4, 4, 32, 512)
+        shrink_at(grad_left.reshape(4, 4, 32, 1024))
+        end_at(grad_right[:, :, :16], grad_right[:, :, 16:])
+        up_grad = up_ref[0]
+        for j in range(4):
+            part = dot(rows[:, 384 * j : 384 * (j + 1)], up_grad, ((0,), (0,))).astype(bf16)
+            expand_at(j, part.reshape(4, 96, 1024))
+
+    @pl.when(e == 0)
+    def _():
+        def shrink_at(value):
+            own[:, :, 96:128, :] = value
+
+        def end_at(first, second):
+            own[:, :, 128:144, :512] = first
+            own[:, :, 128:144, 512:] = second
+
+        def expand_at(j, value):
+            own[j, :, :96, :] = value
+
+        write(shrink_at, end_at, expand_at)
+        low_x.start()
+        high_y.start()
+
+    @pl.when(e > 0)
+    def _():
+        def shrink_at(value):
+            out_ref[:, :, 0, 96:128, :] = value
+
+        def end_at(first, second):
+            out_ref[:, :, 0, 128:144, :512] = first
+            out_ref[:, :, 0, 128:144, 512:] = second
+
+        def expand_at(j, value):
+            out_ref[j, :, 0, :96, :] = value
+
+        write(shrink_at, end_at, expand_at)
+
+    @pl.when(e == LOCAL_E - 1)
+    def _():
+        line_ref[0] = low_x.total().astype(bf16)
+        line_ref[1] = high_y.total().astype(bf16)
+        low_x.drain()
+        high_y.drain()
+
+
+def expert_grads(rows, cot_rows, row_gates, weights):
     one = lambda e: (e, 0, 0)
     wide = lambda e: (0, e, 0, 0)
+    out = lambda e: (0, 0, jnp.maximum(e - 1, 0), 0, 0)
     return pl.pallas_call(
         grads_kernel,
-        grid=(count,),
+        grid=(LOCAL_E,),
         in_specs=[
-            pl.BlockSpec((1, SLOTS, D), at),
-            pl.BlockSpec((1, SLOTS, D), at),
-            pl.BlockSpec((1, SLOTS, 1), at),
+            pl.BlockSpec((1, SLOTS, D), one),
+            pl.BlockSpec((1, SLOTS, D), one),
+            pl.BlockSpec((1, SLOTS, 1), one),
             pl.BlockSpec((16, 1, 144, 1024), wide),
         ],
         out_specs=[
             pl.BlockSpec((1, SLOTS, FF), one),
             pl.BlockSpec((1, SLOTS, 2 * FF), one),
-            pl.BlockSpec((16, 1, 144, 1024), wide),
+            pl.BlockSpec((4, 4, 1, 144, 1024), out),
+            pl.BlockSpec((2, 4, 144, 512), lambda e: (0, 0, 0, 0)),
         ],
         out_shape=[
-            jax.ShapeDtypeStruct((count, SLOTS, FF), bf16),
-            jax.ShapeDtypeStruct((count, SLOTS, 2 * FF), bf16),
-            jax.ShapeDtypeStruct((16, count, 144, 1024), bf16),
-        ],
-        compiler_params=pltpu.CompilerParams(vmem_limit_bytes=BIG),
+            jax.ShapeDtypeStruct((LOCAL_E, SLOTS, FF), bf16),
+            jax.ShapeDtypeStruct((LOCAL_E, SLOTS, 2 * FF), bf16),
+            jax.ShapeDtypeStruct((4, 4, MAIN_E, 144, 1024), bf16),
+            jax.ShapeDtypeStruct((2, 4, 144, 512), bf16),
+        ],
+        scratch_shapes=[pltpu.VMEM((4, 4, 144, 1024), bf16)]
+        + reduce_scratch((4, 144, 512), (2, 144, 512)) * 2
+        + sems(12),
+        compiler_params=remote_params(7),
         cost_estimate=pl.CostEstimate(
-            flops=12 * count * SLOTS * D * FF, bytes_accessed=count * (12 << 20), transcendentals=0
+            flops=12 * LOCAL_E * SLOTS * D * FF, bytes_accessed=60 << 20, transcendentals=0
         ),
     )(rows, cot_rows, row_gates, weights)
 
@@ -1149,7 +1142,7 @@
     core = lax.axis_index("core")
     first = (seq * 2 + core) * LOCAL_E
 
-    packed, extra = pack_experts(expand_weight, shrink_weight)
+    packed = pack_experts(expand_weight, shrink_weight)
     packed, rows_in, cots_in = lax.optimization_barrier((packed, activations[0], cotangent[0]))
     weights = lax.all_gather(packed, PLANE, axis=0, tiled=False)
 
@@ -1198,7 +1191,7 @@
     )
     angles = (cosine, sine, seq_ids[:, None], seq_ids[None, :])
 
-    normed, qkv, attended, lse, middle, tokens, extra_weights = middle_tokens(
+    normed, qkv, attended, lse, middle, tokens = middle_tokens(
         in_all,
         gains_full[0:1],
         entry_own,
@@ -1206,9 +1199,7 @@
         exit_own,
         activations[0],
         gains_full[1:2],
-        extra,
-    )
-    extra_weights = extra_weights.reshape(16, 1, 144, 1024)
+    )
     normed_two = lax.dynamic_slice(tokens, (core, seq, 0, 0), (1, 1, TOK_DEV, D))[0, 0]
     tokens = tokens.reshape(PAIR_TOK, D)
 
@@ -1218,10 +1209,8 @@
     gates = gate_expo / jnp.sum(gate_expo, axis=1, keepdims=True)
     own_gates = lax.dynamic_slice_in_dim(gates, first, LOCAL_E, 1)
     rows, cot_rows, row_gates = dispatch(rank.T, own_gates.T, tokens, cots.reshape(PAIR_TOK, D))
-    extra_hidden, extra_up, extra_grad = expert_grads(
-        rows, cot_rows, row_gates, extra_weights, MAIN_E
-    )
-    hidden, up_grad, expert_grad = expert_grads(rows, cot_rows, row_gates, weights, 0)
+    hidden, up_grad, expert_grad, line = expert_grads(rows, cot_rows, row_gates, weights)
+    expert_grad = expert_grad.reshape(16, MAIN_E, 144, 1024)
     expert_sum = lax.psum_scatter(expert_grad, PLANE, scatter_dimension=0, tiled=False)
     my_gates = lax.dynamic_slice_in_dim(gates, core * GROUP + seq * TOK_DEV, TOK_DEV, 0)
     my_gates = jnp.pad(my_gates, ((0, 0), (0, 128 - EXPERTS)))
@@ -1232,10 +1221,7 @@
         row_gates,
         cot_rows,
         weights,
-        extra_up,
-        extra_hidden,
-        extra_weights,
-        extra_grad.reshape(4, 4, 144, 1024),
+        line,
         middle,
         cotangent[0],
         my_gates,

time: 391 us -> 363 us (0.928)
  Pallas kernels: 317 us -> 272 us
  waiting for transfers between devices: 15.5 us -> 31.7 us
    pallas_call x1, Pallas kernels: 87.5 us -> 54.7 us  [turn(): pl.pallas_call(turn_kernel, grid=(LOCAL_E + 1,), in_specs=[pl.BlockSpec((...]
    pallas_call x1, Pallas kernels: 60.1 us -> 48.5 us  [middle_tokens(): pl.pallas_call(middle_kernel, out_shape=[jax.ShapeDtypeStruct((GROUP, D),...]
    all_gather x1, waiting for transfers between devices: 15.5 us -> 26.5 us  [on_device(): weights = lax.all_gather(packed, PLANE, axis=0, tiled=False)]
    unnamed x3, waiting for transfers between devices: 0.03 us -> 5.21 us
    pallas_call x3 -> x2, Pallas kernels: 34.2 us -> 38.5 us  [the longest x1 32.1 us: expert_grads(): pl.pallas_call(grads_kernel, grid=(LOCAL_E,), in_specs=[pl.BlockSpec((1,...]
  transfers between devices with their start and end apart: 3 -> 3, of which waited for: 1 -> 2; matrix products, arithmetic and copies ran while one was open for 8% -> 8% of each run, Pallas kernels for 74% -> 64%
where the time goes in v6:
time: 363 us; the launch traced here: 358 us
  Pallas kernels  272 us (75%)
  waiting for transfers between devices  31.7 us (9%)
  other arithmetic  18.7 us (5%)
  between operations  14.9 us (4%)
  local copies, waits for them, and re-layouts  13.8 us (4%)
  matrix products  6.48 us (2%)
    pallas_call x1, Pallas kernels, closing(): pl.pallas_call(closing_kernel, out_shape=[jax.ShapeDtypeStruct((TOK_DEV,...  62.8 us
    pallas_call x1, Pallas kernels, turn(): pl.pallas_call(turn_kernel, grid=(LOCAL_E + 1,), in_specs=[pl.BlockSpec((...  54.7 us
    pallas_call x1, Pallas kernels, start(): pl.pallas_call(start_kernel, out_shape=[jax.ShapeDtypeStruct((N_SEQ, TOK_...  49.6 us
    pallas_call x1, Pallas kernels, middle_tokens(): pl.pallas_call(middle_kernel, out_shape=[jax.ShapeDtypeStruct((GROUP, D),...  48.5 us
    pallas_call x1, Pallas kernels, expert_grads(): pl.pallas_call(grads_kernel, grid=(LOCAL_E,), in_specs=[pl.BlockSpec((1,...  32.1 us
    all_gather x1, waiting for transfers between devices, on_device(): weights = lax.all_gather(packed, PLANE, axis=0, tiled=False)  26.5 us
    pallas_call x1, Pallas kernels, dispatch(): pl.pallas_call(dispatch_kernel, grid=(LOCAL_E,), in_specs=[pl.BlockSpec((...  13.3 us
    sub x6, other arithmetic, adamw_step(): weight - rate * (mean_hat / (jnp.sqrt(square_hat) + adam_eps) + decay * w...  11.9 us
  transfers between devices with their start and end apart: 3, of which 2 were waited for; matrix products, arithmetic and copies ran while one was open for 8% of the time, Pallas kernels for 64%

profile of v6, /device:TPU:1, one launch (start us, length us, event | category | flops | bytes accessed | tf_op | source)
XLA Modules:
  0.0 358.1 jit_solution(4198306708594899858)
XLA Ops:
  7.3 6.4 %shard_map.374 = bf16[5,144,1024]{2,1,0:T(8,128)(2,1)} custom-call(f32[10,48,1024]{2,1,0:T(8,128)} %expand_ref.1, f32[10,16,1536]{2,1,0:T(8,128)} %shrink_ref.1), custom_call_target="tpu_custom_call" | custom-call | tf_op jit(solution)/shard_map/pallas_call | solution.py:294
  15.0 0.6 convert_element_type.46.hit_ref
  15.7 0.6 pad.18.exit_ref
  16.4 0.7 fusion.20.entry_ref
  17.1 49.6 %shard_map.375 = (bf16[4,128,1536]{2,1,0:T(8,128)(2,1)}, bf16[2,4,128,1536]{3,2,1,0:T(8,128)(2,1)}, bf16[4,128,128]{2,1,0:T(8,128)(2,1)}, bf16[1536,640]{1,0:T(8...) custom-call(bf16[128,1536]{1,0:T(8,128)(2,1)} %bitcast.82, bf16[128,1536]{1,0:T(8,128)(2,1)} %bitcast.97, ...), custom_call_target="tpu_custom_call" | custom-call | tf_op jit(solution)/shard_map/pallas_call | solution.py:400
  66.7 1.2 convolution_convert_fusion
  68.3 0.9 copy.160.seq_col_ref
  69.1 1.2 copy.153
  72.4 1.5 concatenate.22.sin_ref
  73.9 1.3 concatenate.21.cos_ref
  75.3 48.5 %shard_map.376 = (bf16[512,1536]{1,0:T(8,128)(2,1)}, bf16[512,640]{1,0:T(8,128)(2,1)}, bf16[512,384]{1,0:T(8,128)(2,1)}, f32[512,6]{1,0:T(8,128)}, f32[128,1536]...) custom-call(bf16[4,128,1536]{2,1,0:T(8,128)(2,1)} %get-tuple-element.56.all_ref, ...), custom_call_target="tpu_custom_call" | custom-call | tf_op jit(solution)/shard_map/pallas_call | solution.py:494
  124.2 1.4 reduce-window.11
  126.5 0.8 copy.164.rank_ref
  127.3 3.1 fusion.30
  131.4 0.8 copy.165.gate_ref
  132.2 13.3 %shard_map.377 = (bf16[5,256,1536]{2,1,0:T(8,128)(2,1)}, bf16[5,256,1536]{2,1,0:T(8,128)(2,1)}, f32[5,256,1]{2,1,0:T(8,128)}) custom-call(s32[5,1,1024]{2,1,0:T(1,128)} %copy.164.rank_ref, f32[5,1,1024]{2,1,0:T(1,128)} %copy.165.gate_ref, bf16[1024,1536]{1,0:T(8,128)(2,1)} %bitcast.108, bf16[1024,1536]{1,0:T(8,128)(2,1)} %bitcast.114), custom_call_target="tpu_custom_call" | custom-call | flops 8053063680 | bytes 16777216 | tf_op jit(solution)/shard_map/pallas_call | solution.py:936
  145.4 26.5 %all-gather.3.cloned.1.call-done = bf16[80,144,1024]{2,1,0:T(8,128)(2,1)} async-done(((bf16[5,144,1024]{2,1,0:T(8,128)(2,1)}), bf16[80,144,1024]{2,1,0:T(8,128)(2,1)}) %all-gather.3.cloned.1.call-update) | async-done | bytes 23592976 | tf_op jit(solution)/shard_map/all_gather | solution.py:1147
  171.9 32.1 %shard_map.378 = (bf16[5,256,512]{2,1,0:T(8,128)(2,1)}, bf16[5,256,1024]{2,1,0:T(8,128)(2,1)}, bf16[4,4,4,144,1024]{4,3,2,1,0:T(8,128)(2,1)}, bf16[2,4,144,512]{3,2,1,0:T(8,128)(2,1)}) custom-call(bf16[5,256,1536]{2,1,0:T(8,128)(2,1)} %get-tuple-element.65.rows_ref, bf16[5,256,1536]{2,1,0:T(8,128)(2,1)} %get-tuple-element.66.cot_ref.cot_rows_ref, ...), custom_call_target="tpu_custom_call" | custom-call | flops 12079595520 | bytes 62914560 | tf_op jit(solution)/shard_map/pallas_call | solution.py:1054
  204.1 0.6 pad.19.my_gate_ref
  204.7 54.7 %shard_map.379 = (f32[128,1536]{1,0:T(8,128)}, bf16[4,128,1536]{2,1,0:T(8,128)(2,1)}, bf16[128,128]{1,0:T(8,128)(2,1)}, f32[1,1536]{1,0:T(1,128)}, bf16[4,128,15...) custom-call(s32[1024,5]{1,0:T(8,128)} %copy-done.2, bf16[5,256,1024]{2,1,0:T(8,128)(2,1)} %get-tuple-element.69.up_ref, ...), custom_call_target="tpu_custom_call" | custom-call | flops 14092861440 | bytes 41943040 | tf_op jit(solution)/shard_map/pallas_call | solution.py:634
  259.4 2.2 fusion.8.router_grad_ref
  261.7 62.8 %shard_map.380 = (f32[128,1536]{1,0:T(8,128)}, f32[128,1536]{1,0:T(8,128)}, f32[4,16,768]{2,1,0:T(8,128)}, f32[16,1536]{1,0:T(8,128)}) custom-call(bf16[512,640]{1,0:T(8,128)(2,1)} %get-tuple-element.60.qkv_ref, f32[512,6]{1,0:T(8,128)} %get-tuple-element.61.lse_ref, f32[512,640]{1,0:T(8,128)} %concatenate.21.cos_ref, f32[512,640]{1,0:T(8,128)} %concatenate.22.sin_ref, ...), custom_call_target="tpu_custom_call" | custom-call | tf_op jit(solution)/shard_map/pallas_call | solution.py:848
  324.5 0.8 slice_reduce_fusion
  325.4 1.0 slice_bitcast_fusion
  326.5 0.8 slice_bitcast_fusion.1
  328.8 1.6 multiply_subtract_fusion.3
  330.4 1.0 convert_bitcast_fusion
  331.4 0.8 multiply_subtract_fusion.2
  332.2 5.2 %reduce-scatter.4.cloned.1.call-done = bf16[1,4,144,1024]{3,2,1,0:T(8,128)(2,1)} async-done(((bf16[16,4,144,1024]{3,2,1,0:T(8,128)(2,1)}), bf16[1,4,144,1024]{3,2,1,0:T(8,128)(2,1)}) %reduce-scatter.4.cloned.1.call-update) | async-done | bytes 1179664
  337.4 4.9 %shard_map.381 = (bf16[10,48,1024]{2,1,0:T(8,128)(2,1)}, bf16[10,16,1536]{2,1,0:T(8,128)(2,1)}) custom-call(bf16[4,144,1024]{2,1,0:T(8,128)(2,1)} %bitcast.94, bf16[144,1024]{1,0:T(8,128)(2,1)} %get-tuple-element.85.extra_ref), custom_call_target="tpu_custom_call" | custom-call | tf_op jit(solution)/shard_map/pallas_call | solution.py:910
  342.4 3.3 multiply_subtract_fusion.1
  346.1 4.9 %multiply_subtract_fusion = (f32[10,48,1024]{2,1,0:T(8,128)}, f32[10,48,1024]{2,1,0:T(8,128)}, f32[10,48,1024]{2,1,0:T(8,128)}) fusion(f32[10,48,1024]{2,1,0:T(8,128)S(1)} %copy-done, bf16[10,48,1024]{2,1,0:T(8,128)(2,1)} %get-tuple-element.86, f32[10,48,1024]{2,1,0:T(8,128)S(1)} %copy-done.3, f32[10,48,1024]{2,1,0:T(8,128)S(1)} %copy-done.4), kind=kLoop, calls=%fused_computation.4 | loop fusion | flops 7864320 | bytes 12779520 | tf_op jit(solution)/shard_map/sub | solution.py:1105
  (118 shorter events, 8.0 us)
Async XLA Ops:
  7.2 6.6 %copy-start.9 = (f32[12,2560]{1,0:T(8,128)S(1)}, f32[12,2560]{1,0:T(8,128)}, u32[]{:S(2)}) copy-start(f32[12,2560]{1,0:T(8,128)} %param.28) | copy-start | bytes 368644
  7.2 6.6 %copy-start.21 = (f32[2,12]{1,0:T(2,128)S(1)}, f32[2,12]{1,0:T(2,128)}, u32[]{:S(2)}) copy-start(f32[2,12]{1,0:T(2,128)} %param.43) | copy-start | bytes 292
  7.2 6.7 %copy-start.17 = (f32[12,40]{1,0:T(8,128)S(1)}, f32[12,40]{1,0:T(8,128)}, u32[]{:S(2)}) copy-start(f32[12,40]{1,0:T(8,128)} %param.34) | copy-start | bytes 5764
  7.2 164.7 %all-gather.3.cloned.1.call-start = ((), (), s32[]{:S(2)}) async-start(), calls=%async_computation.1 | async-start | bytes 25067520 | tf_op jit(solution)/shard_map/all_gather | solution.py:1147
  13.6 0.9 copy-start.11
  13.7 0.9 copy-start.20
  13.7 53.0 %copy-start.24 = (s32[1,512]{1,0:T(1,128)S(1)}, s32[1,512]{1,0:T(1,128)}, u32[]{:S(2)}) copy-start(s32[1,512]{1,0:T(1,128)} %param.26) | copy-start | bytes 6148
  13.7 54.3 %copy-start.25 = (s32[1,3]{1,0:T(1,128)S(1)}, s32[1,3]{1,0:T(1,128)}, u32[]{:S(2)}) copy-start(s32[1,3]{1,0:T(1,128)} %param.25) | copy-start | bytes 40
  13.7 323.7 %reduce-scatter.4.cloned.1.call-start = ((), (), s32[]{:S(2)}) async-start(), calls=%async_computation.2 | async-start | bytes 20054016
  67.9 56.0 %collective-permute-start = (bf16[512,128]{1,0:T(8,128)(2,1)S(1)}, bf16[512,128]{1,0:T(8,128)(2,1)S(1)}, u32[]{:S(2)}, u32[]{:S(2)}) collective-permute-start(bf16[512,128]{1,0:T(8,128)(2,1)S(1)} %convolution_convert_fusion), channel_id=1, source_target_pairs={{0,1},{1,0},{2,3},{3,2},{4,5},{5,4},{6,7},{7,6},{8,9},{9,8},{10,11... | collective-permute-start | bytes 393224 | tf_op jit(solution)/shard_map/ppermute | solution.py:1086
  68.3 3.8 %copy-start.16 = (s32[512]{0:T(512)}, s32[512]{0:T(512)S(1)}, u32[]{:S(2)}) copy-start(s32[512]{0:T(512)S(1)} %convert_reduce_fusion) | copy-start | bytes 6148
  123.9 3.5 copy-start.10
  126.5 3.9 %copy-start.2 = (s32[1024,5]{1,0:T(8,128)}, s32[1024,5]{1,0:T(8,128)S(1)}, u32[]{:S(2)}) copy-start(s32[1024,5]{1,0:T(8,128)S(1)} %bitcast_select_fusion.rank_ref) | copy-start | bytes 61444
  261.6 65.9 %copy-start.22 = (f32[2,12]{1,0:T(2,128)S(1)}, f32[2,12]{1,0:T(2,128)}, u32[]{:S(2)}) copy-start(f32[2,12]{1,0:T(2,128)} %param.45) | copy-start | bytes 292
  261.6 65.9 %copy-start.23 = (f32[2,12]{1,0:T(2,128)S(1)}, f32[2,12]{1,0:T(2,128)}, u32[]{:S(2)}) copy-start(f32[2,12]{1,0:T(2,128)} %param.44) | copy-start | bytes 292
  261.6 66.5 %copy-start.18 = (f32[12,40]{1,0:T(8,128)S(1)}, f32[12,40]{1,0:T(8,128)}, u32[]{:S(2)}) copy-start(f32[12,40]{1,0:T(8,128)} %param.36) | copy-start | bytes 5764
  261.6 66.5 %copy-start.19 = (f32[12,40]{1,0:T(8,128)S(1)}, f32[12,40]{1,0:T(8,128)}, u32[]{:S(2)}) copy-start(f32[12,40]{1,0:T(8,128)} %param.35) | copy-start | bytes 5764
  261.6 67.1 %copy-start.14 = (f32[12,1536]{1,0:T(8,128)S(1)}, f32[12,1536]{1,0:T(8,128)}, u32[]{:S(2)}) copy-start(f32[12,1536]{1,0:T(8,128)} %param.33) | copy-start | bytes 221188
  261.7 67.1 %copy-start.15 = (f32[12,1536]{1,0:T(8,128)S(1)}, f32[12,1536]{1,0:T(8,128)}, u32[]{:S(2)}) copy-start(f32[12,1536]{1,0:T(8,128)} %param.32) | copy-start | bytes 221188
  325.4 5.0 %copy-start.7 = (f32[128,1536]{1,0:T(8,128)S(1)}, f32[128,1536]{1,0:T(8,128)}, u32[]{:S(2)}) copy-start(f32[128,1536]{1,0:T(8,128)} %get-tuple-element.81) | copy-start | bytes 2359300
  325.4 5.0 %copy-start.8 = (f32[128,1536]{1,0:T(8,128)S(1)}, f32[128,1536]{1,0:T(8,128)}, u32[]{:S(2)}) copy-start(f32[128,1536]{1,0:T(8,128)} %get-tuple-element.80) | copy-start | bytes 2359300
  327.4 4.0 %copy-start.12 = (f32[12,2560]{1,0:T(8,128)S(1)}, f32[12,2560]{1,0:T(8,128)}, u32[]{:S(2)}) copy-start(f32[12,2560]{1,0:T(8,128)} %param.30) | copy-start | bytes 368644
  327.4 4.0 %copy-start.13 = (f32[12,2560]{1,0:T(8,128)S(1)}, f32[12,2560]{1,0:T(8,128)}, u32[]{:S(2)}) copy-start(f32[12,2560]{1,0:T(8,128)} %param.29) | copy-start | bytes 368644
  330.4 11.9 %copy-start.1 = (f32[10,16,1536]{2,1,0:T(8,128)S(1)}, f32[10,16,1536]{2,1,0:T(8,128)}, u32[]{:S(2)}) copy-start(f32[10,16,1536]{2,1,0:T(8,128)} %shrink_ref.1) | copy-start | bytes 2949124
  330.4 11.9 %copy-start.5 = (f32[10,16,1536]{2,1,0:T(8,128)S(1)}, f32[10,16,1536]{2,1,0:T(8,128)}, u32[]{:S(2)}) copy-start(f32[10,16,1536]{2,1,0:T(8,128)} %param.42) | copy-start | bytes 2949124
  330.4 11.9 %copy-start.6 = (f32[10,16,1536]{2,1,0:T(8,128)S(1)}, f32[10,16,1536]{2,1,0:T(8,128)}, u32[]{:S(2)}) copy-start(f32[10,16,1536]{2,1,0:T(8,128)} %param.41) | copy-start | bytes 2949124
  342.3 3.3 copy-start
  342.4 3.3 copy-start.3
  342.4 3.7 %copy-start.4 = (f32[10,48,1024]{2,1,0:T(8,128)S(1)}, f32[10,48,1024]{2,1,0:T(8,128)}, u32[]{:S(2)}) copy-start(f32[10,48,1024]{2,1,0:T(8,128)} %param.38) | copy-start | bytes 5898244
Sparse Core Ops, SparseCore 0:
  13.8 158.0 all-gather.2
  204.2 133.2 reduce-scatter.3
